TPU v7x, 32 devices: a whole 2x2x4 slice. The times are simulated.
32 devices in a mesh: groups: 2 (over y), ep: 4 (over z), tp: 2 (over x), sp: 2 (over core).
Axes of the slice: x: 2, y: 2, z: 4, core: 2. Of those that a mesh axis runs over, the one named last changes fastest.
Arguments:
- query: bfloat16 [512, 4096], P(('groups', 'ep', 'sp'), 'tp'), parts along dimension 0, may hold values from -80 to 80
- key_cache: bfloat16 [512, 256, 512], P(('groups', 'ep', 'sp')), parts along dimension 0, may hold values from -4.5 to 4.5
- value_cache: bfloat16 [512, 256, 512], P(('groups', 'ep', 'sp')), parts along dimension 0, may hold values from -6 to 6
- new_key: bfloat16 [512, 512], P(('groups', 'ep', 'sp')), parts along dimension 0, may hold values from -4.5 to 4.5
- new_value: bfloat16 [512, 512], P(('groups', 'ep', 'sp')), parts along dimension 0, may hold values from -6 to 6
- lengths: int32 [512], P(('groups', 'ep', 'sp')), parts along dimension 0, may hold values from 1 to 256, as said below
- out_weight: bfloat16 [4096, 2048], P('tp', 'sp'), may hold values from -0.09375 to 0.09375
- residual: bfloat16 [512, 2048], P(('groups', 'ep', 'sp')), parts along dimension 0, may hold values from -6 to 6
- norm_gain: float32 [2048], replicated, may hold values from 0.25 to 1.75
- expert_ids: int32 [512, 8], P(('groups', 'ep', 'sp')), parts along dimension 0, may hold values from 0 to 15, all different within a row; in each aligned block of 32 rows (0 to 31, 32 to 63, ...) at most 32 rows name the same one
- gate_weights: float32 [512, 8], P(('groups', 'ep', 'sp')), parts along dimension 0, may hold values from 0.05 to 1
- w_gate: bfloat16 [16, 2048, 1024], P(('ep', 'sp'), None, 'tp'), may hold values from -0.125 to 0.125
- w_up: bfloat16 [16, 2048, 1024], P(('ep', 'sp'), None, 'tp'), may hold values from -0.125 to 0.125
- w_down: bfloat16 [16, 1024, 2048], P(('ep', 'sp'), 'tp'), may hold values from -0.1875 to 0.1875
Outputs:
- layer_out: bfloat16 [512, 2048], P(('groups', 'ep', 'sp'), 'tp'), parts along dimension 0
There are 2 independent parts, one for each index of `groups`. A program takes and returns all parts, laid end to end along the dimension named above; an argument that names none is the same for every part. Nothing has to cross between parts.
Inputs may be any that keep to these rules, and one draw needn't show every extreme that they name: `expert_ids`: each row names 8 different experts; within each aligned block of 32 rows (the rows of one device), no expert is named by more than 32 rows, and in every draw some expert is named by exactly 32 rows of some block. `lengths`: one request in every draw has all 256 positions valid.
All inputs are finite; a program needn't handle non-finite values.
Results may differ from a plain program's by a relative error of at most 0.0056.
Values may be sent and summed in bfloat16 or wider, within the bound.
No kernel may reach another device: no remote copies, remote signals or barrier semaphores. Data moves between devices by JAX's collectives and lax.ppermute only.
A program may use at most 128 MiB of HBM per device.

v0:
```python
import jax
import jax.numpy as jnp
from jax import lax
from jax.sharding import PartitionSpec as P

HEADS = 32
KV_HEADS = 4
HD = 128
TOP = 8


masked_fill = -1e30
norm_epsilon = 1e-06


def merge_pair(first_state, second_state):
    peak = jnp.maximum(first_state[0], second_state[0])
    left_factor = jnp.exp(first_state[0] - peak)
    right_factor = jnp.exp(second_state[0] - peak)
    weight_sum = first_state[1] * left_factor + second_state[1] * right_factor
    blended = first_state[2] * left_factor[..., None] + second_state[2] * right_factor[..., None]
    return (peak, weight_sum, blended)


def expert_layer(received, w_gate, w_up, w_down, pattern):
    gate_act = jnp.einsum(pattern, received, w_gate, preferred_element_type=jnp.float32)
    up_act = jnp.einsum(pattern, received, w_up, preferred_element_type=jnp.float32)
    hidden = (jax.nn.silu(gate_act) * up_act).astype(jnp.bfloat16)
    down_terms = jnp.einsum("sjcf,jfd->sjcd", hidden, w_down, preferred_element_type=jnp.float32)
    summed = lax.psum_scatter(
        down_terms.astype(jnp.bfloat16), "tp", scatter_dimension=3, tiled=True
    )
    return lax.all_to_all(summed, ("ep", "sp"), split_axis=0, concat_axis=0, tiled=True)


def shards(
    query,
    key_cache,
    value_cache,
    new_key,
    new_value,
    lengths,
    out_weight,
    residual,
    norm_gain,
    expert_ids,
    gate_weights,
    w_gate,
    w_up,
    w_down,
):
    grouping = HEADS // KV_HEADS
    scaling = HD ** (-0.5)
    row_count = query.shape[0]
    local_heads = query.shape[1] // HD
    kv_count = max(1, local_heads // grouping)
    per_group = local_heads // kv_count
    tp_index = lax.axis_index("tp")
    kv_first = tp_index * local_heads // grouping
    cached = key_cache.shape[1]
    queries = query.reshape(row_count, kv_count, per_group, HD)
    key_rows = lax.dynamic_slice_in_dim(key_cache, kv_first * HD, kv_count * HD, 2).reshape(
        row_count, cached, kv_count, HD
    )
    value_rows = lax.dynamic_slice_in_dim(value_cache, kv_first * HD, kv_count * HD, 2).reshape(
        row_count, cached, kv_count, HD
    )
    position = jnp.arange(cached, dtype=jnp.int32)
    visible = position[None, :] < lengths[:, None]
    scores = (
        jnp.einsum("rkgd,rtkd->rkgt", queries, key_rows, preferred_element_type=jnp.float32)
        * scaling
    )
    scores = jnp.where(visible[:, None, None, :], scores, masked_fill)
    peak = jnp.max(scores, axis=-1)
    probabilities = jnp.where(visible[:, None, None, :], jnp.exp(scores - peak[..., None]), 0.0)
    weight_sum = jnp.sum(probabilities, axis=-1)
    blended = jnp.einsum(
        "rkgt,rtkd->rkgd",
        probabilities.astype(jnp.bfloat16),
        value_rows,
        preferred_element_type=jnp.float32,
    )
    softmax_state = (peak, weight_sum, blended)
    fresh_key = lax.dynamic_slice_in_dim(new_key, kv_first * HD, kv_count * HD, 1).reshape(
        row_count, kv_count, HD
    )
    fresh_value = lax.dynamic_slice_in_dim(new_value, kv_first * HD, kv_count * HD, 1).reshape(
        row_count, kv_count, HD
    )
    own_score = (
        jnp.einsum("rkgd,rkd->rkg", queries, fresh_key, preferred_element_type=jnp.float32)
        * scaling
    )
    own_state = (
        own_score,
        jnp.ones_like(own_score),
        jnp.broadcast_to(fresh_value.astype(jnp.float32)[:, :, None, :], blended.shape),
    )
    softmax_state = merge_pair(softmax_state, own_state)
    attended = (
        (softmax_state[2] / softmax_state[1][..., None])
        .reshape(row_count, local_heads * HD)
        .astype(jnp.bfloat16)
    )
    every_rows = lax.all_gather(attended, "sp", axis=0, tiled=True)
    half_terms = jnp.dot(every_rows, out_weight, preferred_element_type=jnp.float32)
    projected = lax.all_to_all(half_terms, "sp", split_axis=0, concat_axis=1, tiled=True)
    model_width = residual.shape[1]
    col_width = model_width // lax.axis_size("tp")
    totals = lax.psum(projected, "tp")
    stream = residual.astype(jnp.float32) + totals
    normed = (
        stream
        * lax.rsqrt(jnp.mean(stream * stream, axis=-1, keepdims=True) + norm_epsilon)
        * norm_gain
    ).astype(jnp.bfloat16)
    own_stream = lax.dynamic_slice_in_dim(stream, tp_index * col_width, col_width, 1)
    local_experts = w_gate.shape[0]
    targets = lax.axis_size("ep") * lax.axis_size("sp")
    experts_all = local_experts * targets
    slot_cap = max(2, row_count * TOP * 2 // experts_all)
    chosen = (expert_ids[:, :, None] == jnp.arange(experts_all, dtype=jnp.int32)).astype(jnp.int32)
    picked = jnp.sum(chosen, axis=1)
    before = jnp.cumsum(picked, axis=0) - picked
    slot_index = jnp.sum(chosen * before[:, None, :], axis=2)
    flat_index = expert_ids * slot_cap + slot_index
    places = (flat_index[:, :, None] == jnp.arange(experts_all * slot_cap, dtype=jnp.int32)).astype(
        jnp.float32
    )
    spread = jnp.sum(places, axis=1).astype(jnp.bfloat16)
    blend_weights = jnp.sum(places * gate_weights[:, :, None], axis=1)
    outgoing = jnp.einsum("rs,rd->sd", spread, normed, preferred_element_type=jnp.float32).astype(
        jnp.bfloat16
    )
    outgoing = outgoing.reshape(targets, local_experts, slot_cap, outgoing.shape[1])
    returned = expert_layer(
        lax.all_to_all(outgoing, ("ep", "sp"), split_axis=0, concat_axis=0, tiled=True),
        w_gate,
        w_up,
        w_down,
        "sjcd,jdf->sjcf",
    )
    mixture = jnp.dot(
        blend_weights,
        returned.reshape(experts_all * slot_cap, returned.shape[3]).astype(jnp.float32),
        precision=lax.Precision.HIGHEST,
    )
    return (own_stream + mixture).astype(jnp.bfloat16)


def solution(mesh):
    placed = (
        P(("groups", "ep", "sp"), "tp"),
        P(("groups", "ep", "sp"), None, None),
        P(("groups", "ep", "sp"), None, None),
        P(("groups", "ep", "sp"), None),
        P(("groups", "ep", "sp"), None),
        P(("groups", "ep", "sp")),
        P("tp", "sp"),
        P(("groups", "ep", "sp"), None),
        P(),
        P(("groups", "ep", "sp"), None),
        P(("groups", "ep", "sp"), None),
        P(("ep", "sp"), None, "tp"),
        P(("ep", "sp"), None, "tp"),
        P(("ep", "sp"), "tp", None),
    )
    return jax.shard_map(
        shards,
        mesh=mesh,
        in_specs=placed,
        out_specs=P(("groups", "ep", "sp"), "tp"),
        check_vma=False,
    )
```

profile of v0, /device:TPU:0, one launch (start us, length us, event | category | flops | bytes accessed | tf_op | source)
XLA Modules:
  0.0 204.2 jit_solution(3492942762304222493)
XLA Ops:
  6.5 0.0 all-reduce.2.cloned.1.call-start
  6.5 7.7 %constant_dynamic-slice_fusion.1 = (bf16[32,256,256]{2,1,0:T(8,128)(2,1)}, bf16[32,256,256]{2,1,0:T(8,128)(2,1)}) fusion(bf16[32,256,512]{2,1,0:T(8,128)(2,1)} %param.16, s32[]{:T(128)S(6)} %select_n.25, bf16[32,256,512]{2,1,0:T(8,128)(2,1)} %param.15), kind=kLoop, calls=%fused_computation.54 | loop fusion | bytes 16777220 | tf_op jit(solution)/shard_map/dynamic_slice | solution.py:65
  14.2 0.0 copy-start.8
  14.2 0.0 copy-start.1
  14.2 6.5 %copy.97 = bf16[32,256,256]{1,2,0:T(8,128)(2,1)} copy(bf16[32,256,256]{2,1,0:T(8,128)(2,1)} %get-tuple-element.17) | data formatting | bytes 8388608
  20.7 0.0 copy-done.8
  20.7 0.0 copy-start.5
  20.7 0.0 copy-start.6
  20.7 0.1 iota_compare_fusion.2
  20.8 0.0 copy-done.1
  20.8 2.9 %fusion.60 = (f32[32,2,8]{2,1,0:T(2,128)S(1)}, f32[32,2,8,256]{3,2,1,0:T(8,128)S(1)}) fusion(bf16[32,256,2,128]{1,3,2,0:T(8,128)(2,1)} %bitcast.77, bf16[32,2,8,128]{3,2,1,0:T(8,128)(2,1)S(1)} %bitcast.84, pred[32,256]{1,0:T(8,128)(4,1)S(1)} %iota_compare_fusion.2), kind=kOutput, calls=%fused_computation.59 | convolution fusion | flops 33947136 | bytes 4859904 | tf_op jit(solution)/shard_map/rkgd,rtkd->rkgt/dot_general | solution.py:71
  23.8 0.1 copy.76
  23.8 0.3 fusion.45
  24.1 0.1 copy.79
  24.2 0.0 copy-done.5
  24.2 0.0 copy-done.6
  24.3 0.2 fusion.61
  24.5 0.1 copy.93
  24.6 0.1 copy.77
  24.6 0.1 copy.78
  24.7 0.1 copy.80
  24.8 6.4 %copy.98 = bf16[32,256,256]{1,2,0:T(8,128)(2,1)} copy(bf16[32,256,256]{2,1,0:T(8,128)(2,1)} %get-tuple-element.16) | data formatting | bytes 8388608
  31.3 0.0 copy-start
  31.3 3.6 %fusion.38 = bf16[32,2,8,128]{3,2,1,0:T(8,128)(2,1)S(1)} fusion(bf16[32,256,2,128]{1,3,2,0:T(8,128)(2,1)} %bitcast.79, f32[32,2,8,256]{3,2,1,0:T(8,128)S(1)} %get-tuple-element.13, f32[32,2,8]{2,1,0:T(2,128)S(1)} %get-tuple-element.12, pred[32,256]{1,0:T(8,128)(4,1)S(1)} %iota_compare_fusion.2, f32[32,2,8]{2,1,0:T(2,128)S(1)} %copy.80, ...), kind=kOutput, calls=%fused_computation.21 | convolution fusion | flops 34275328 | bytes 4898816 | tf_op jit(solution)/shard_map/rkgt,rtkd->rkgd/dot_general | solution.py:78
  34.9 0.0 copy-start.3
  34.9 0.0 copy-start.7
  34.9 0.0 copy-start.2
  34.9 0.0 copy-start.4
  34.9 2.2 %all_gather.3 = bf16[64,2048]{1,0:T(8,128)(2,1)S(1)} all-gather(bf16[32,2048]{1,0:T(8,128)(2,1)S(1)} %bitcast.86), channel_id=1, replica_groups=mesh['groups'=2,'ep'=4,'tp'=2,'sp'=2] {'sp'}, dimensions={0}, use_global_device_ids=true | all-gather | bytes 393216 | tf_op jit(solution)/shard_map/all_gather | solution.py:106
  37.2 0.0 copy-done
  37.2 0.8 fusion.62
  38.0 3.9 %all_to_all.29 = f32[2,32,1024]{2,1,0:T(8,128)S(1)} all-to-all(f32[2,32,1024]{2,1,0:T(8,128)S(1)} %bitcast.81), channel_id=1, replica_groups=mesh['groups'=2,'ep'=4,'tp'=2,'sp'=2] {'sp'}, dimensions={0} | all-to-all | bytes 524288 | tf_op jit(solution)/shard_map/all_to_all | solution.py:108
  42.0 0.7 copy.99
  42.7 0.0 all-reduce.2.cloned.1.call-update
  42.7 0.0 reduce-scatter.2.cloned.1.call-start
  42.7 0.0 copy-done.3
  42.8 0.1 copy.82
  42.9 0.1 reduce_window_sum.11
  42.9 0.1 copy.84
  43.0 0.1 copy.85
  43.1 0.0 copy-done.7
  43.1 0.1 copy.86
  43.2 0.4 convert_reduce_fusion
  43.6 25.1 %all-reduce.2.cloned.1.call-done = f32[32,2048]{1,0:T(8,128)} async-done(((f32[32,2048]{1,0:T(8,128)}), f32[32,2048]{1,0:T(8,128)}) %all-reduce.2.cloned.1.call-update) | async-done | bytes 262160 | tf_op jit(solution)/shard_map/psum | solution.py:111
  68.7 0.0 copy-done.2
  68.7 0.0 copy-start.9
  68.7 1.2 multiply_reduce_fusion
  69.9 0.0 copy-done.4
  69.9 0.8 convolution_convert_fusion
  70.7 53.5 %all_to_all.30 = bf16[8,2,32,2048]{3,2,1,0:T(8,128)(2,1)S(1)} all-to-all(bf16[8,2,32,2048]{3,2,1,0:T(8,128)(2,1)S(1)} %bitcast.78), channel_id=1, replica_groups=mesh['groups'=2,'ep'=4,'tp'=2,'sp'=2] {'ep','sp'}, dimensions={0} | all-to-all | bytes 4194304 | tf_op jit(solution)/shard_map/all_to_all | solution.py:138
  124.2 0.0 copy-done.9
  124.2 1.2 fusion.14
  125.4 7.3 %fusion.9 = bf16[8,2,32,2048]{3,2,0,1:T(8,128)(2,1)} fusion(bf16[2,512,2048]{2,1,0:T(8,128)(2,1)} %param.27, bf16[2,2048,512]{2,1,0:T(8,128)(2,1)} %param.26, bf16[8,2,32,2048]{3,2,1,0:T(8,128)(2,1)S(1)} %all_to_all.30, f32[8,2,32,512]{3,2,0,1:T(8,128)S(1)} %fusion.14), kind=kOutput, calls=%fused_computation.8 | convolution fusion | flops 2150105088 | bytes 13631488 | tf_op jit(solution)/shard_map/sjcf,jfd->sjcd/dot_general | solution.py:29
  132.7 0.0 reduce-scatter.2.cloned.1.call-update
  132.7 29.9 %reduce-scatter.2.cloned.1.call-done = bf16[8,2,32,1024]{3,2,0,1:T(8,128)(2,1)} async-done(((bf16[8,2,32,2048]{3,2,0,1:T(8,128)(2,1)}), bf16[8,2,32,1024]{3,2,0,1:T(8,128)(2,1)}) %reduce-scatter.2.cloned.1.call-update) | async-done | bytes 1048592 | tf_op jit(solution)/shard_map/reduce_scatter | solution.py:30
  162.6 2.3 %copy.89 = bf16[8,2,32,1024]{3,2,1,0:T(8,128)(2,1)} copy(bf16[8,2,32,1024]{3,2,0,1:T(8,128)(2,1)} %reduce-scatter.2.cloned.1.call-done) | data formatting | bytes 2097152 | tf_op jit(solution)/shard_map/reduce_scatter | solution.py:30
  164.9 4.6 %all-to-all-start.2 = ((bf16[8,2,32,1024]{3,2,1,0:T(8,128)(2,1)}), bf16[8,2,32,1024]{3,2,1,0:T(8,128)(2,1)S(1)}, u32[]{:S(2)}, u32[]{:S(2)}) async-start(bf16[8,2,32,1024]{3,2,1,0:T(8,128)(2,1)} %copy.89), calls=%async_computation.3 | async-start | bytes 2097152 | tf_op jit(solution)/shard_map/all_to_all | solution.py:33
  169.5 26.6 %all-to-all-done.2 = bf16[8,2,32,1024]{3,2,1,0:T(8,128)(2,1)S(1)} async-done(((bf16[8,2,32,1024]{3,2,1,0:T(8,128)(2,1)}), bf16[8,2,32,1024]{3,2,1,0:T(8,128)(2,1)S(1)}, u32[]{:S(2)}, u32[]{:S(2)}) %all-to-all-start.2) | async-done | bytes 1048608 | tf_op jit(solution)/shard_map/all_to_all | solution.py:33
  196.1 1.2 fusion.39
  (11 shorter events, 0.2 us)
Async XLA Ops:
  6.5 62.1 %all-reduce.2.cloned.1.call-start = ((), (), s32[]{:S(2)}) async-start(), calls=%async_computation.4 | async-start | bytes 524288 | tf_op jit(solution)/shard_map/psum | solution.py:111
  14.2 6.5 %copy-start.8 = (s32[32]{0:T(128)S(1)}, s32[32]{0:T(128)}, u32[]{:S(2)}) copy-start(s32[32]{0:T(128)} %param.19) | copy-start | bytes 388
  14.2 6.6 %copy-start.1 = (bf16[32,2048]{1,0:T(8,128)(2,1)S(1)}, bf16[32,2048]{1,0:T(8,128)(2,1)}, u32[]{:S(2)}) copy-start(bf16[32,2048]{1,0:T(8,128)(2,1)} %param.14) | copy-start | bytes 393220
  20.7 3.5 %copy-start.5 = (bf16[32,512]{1,0:T(8,128)(2,1)S(1)}, bf16[32,512]{1,0:T(8,128)(2,1)}, u32[]{:S(2)}) copy-start(bf16[32,512]{1,0:T(8,128)(2,1)} %param.18) | copy-start | bytes 98308
  20.7 3.5 %copy-start.6 = (bf16[32,512]{1,0:T(8,128)(2,1)S(1)}, bf16[32,512]{1,0:T(8,128)(2,1)}, u32[]{:S(2)}) copy-start(bf16[32,512]{1,0:T(8,128)(2,1)} %param.17) | copy-start | bytes 98308
  31.3 5.9 %copy-start = (bf16[2048,1024]{1,0:T(8,128)(2,1)S(1)}, bf16[2048,1024]{1,0:T(8,128)(2,1)}, u32[]{:S(2)}) copy-start(bf16[2048,1024]{1,0:T(8,128)(2,1)} %param.20) | copy-start | bytes 12582916
  34.9 7.9 %copy-start.3 = (s32[32,8]{0,1:T(8,128)S(1)}, s32[32,8]{0,1:T(8,128)}, u32[]{:S(2)}) copy-start(s32[32,8]{0,1:T(8,128)} %param.23) | copy-start | bytes 3076
  34.9 8.2 %copy-start.7 = (f32[32,8]{0,1:T(8,128)S(1)}, f32[32,8]{0,1:T(8,128)}, u32[]{:S(2)}) copy-start(f32[32,8]{0,1:T(8,128)} %param.24) | copy-start | bytes 3076
  34.9 33.8 %copy-start.2 = (bf16[32,2048]{1,0:T(8,128)(2,1)S(1)}, bf16[32,2048]{1,0:T(8,128)(2,1)}, u32[]{:S(2)}) copy-start(bf16[32,2048]{1,0:T(8,128)(2,1)} %param.21) | copy-start | bytes 393220
  34.9 35.0 %copy-start.4 = (f32[2048]{0:T(1024)S(1)}, f32[2048]{0:T(1024)}, u32[]{:S(2)}) copy-start(f32[2048]{0:T(1024)} %param.22) | copy-start | bytes 24580
  42.7 119.9 %reduce-scatter.2.cloned.1.call-start = ((), (), s32[]{:S(2)}) async-start(), calls=%async_computation.5 | async-start | bytes 3145728 | tf_op jit(solution)/shard_map/reduce_scatter | solution.py:30
  68.7 55.5 %copy-start.9 = (bf16[2,2048,512]{2,1,0:T(8,128)(2,1)S(1)}, bf16[2,2048,512]{2,1,0:T(8,128)(2,1)}, u32[]{:S(2)}) copy-start(bf16[2,2048,512]{2,1,0:T(8,128)(2,1)} %param.25) | copy-start | bytes 12582916
  164.9 31.2 %all-to-all-start.2 = ((bf16[8,2,32,1024]{3,2,1,0:T(8,128)(2,1)}), bf16[8,2,32,1024]{3,2,1,0:T(8,128)(2,1)S(1)}, u32[]{:S(2)}, u32[]{:S(2)}) async-start(bf16[8,2,32,1024]{3,2,1,0:T(8,128)(2,1)} %copy.89), calls=%async_computation.3 | async-start | bytes 2097152 | tf_op jit(solution)/shard_map/all_to_all | solution.py:33
Sparse Core Ops, SparseCore 0:
  42.8 25.8 all-reduce.1
  132.8 29.7 reduce-scatter.1
where the time goes:
time: 205 us; the launch traced here: 204 us
  waiting for transfers between devices  81.6 us (40%)
  blocking collectives  59.6 us (29%)
  local copies, waits for them, and re-layouts  24.5 us (12%)
  matrix products  18 us (9%)
  between operations  13.6 us (7%)
  starting transfers between devices  4.65 us (2%)
  other arithmetic  2.16 us (1%)
    all_to_all x1, blocking collectives, shards(): lax.all_to_all(outgoing, ('ep', 'sp'), split_axis=0, concat_axis=0, tiled...  53.5 us
    reduce_scatter x1, waiting for transfers between devices, expert_layer(): lax.psum_scatter(down_terms.astype(jnp.bfloat16), 'tp', scatter_dimension...  29.9 us
    all_to_all x1, waiting for transfers between devices, expert_layer(): lax.all_to_all(summed, ('ep', 'sp'), split_axis=0, concat_axis=0, tiled=T...  26.6 us
    psum x1, waiting for transfers between devices, shards(): totals = lax.psum(projected, 'tp')  25.1 us
    unnamed x25, local copies, waits for them, and re-layouts  13.1 us
    dynamic_slice x1, local copies, waits for them, and re-layouts, shards(): lax.dynamic_slice_in_dim(value_cache, kv_first * HD, kv_count * HD, 2)  7.68 us
    dot_general x1, matrix products, expert_layer(): jnp.einsum('sjcf,jfd->sjcd', hidden, w_down, preferred_element_type=jnp.f...  7.25 us
    all_to_all x1, starting transfers between devices, expert_layer(): lax.all_to_all(summed, ('ep', 'sp'), split_axis=0, concat_axis=0, tiled=T...  4.61 us
  transfers between devices with their start and end apart: 3, of which 3 were waited for; matrix products, arithmetic and copies ran while one was open for 0% of the time, Pallas kernels for 0%

commit v1 on v0

v1 whole, which is shorter than its diff:
```python
import functools

import jax
import jax.numpy as jnp
from jax import lax
from jax.experimental import pallas as pl
from jax.experimental.pallas import tpu as pltpu
from jax.sharding import PartitionSpec as P

HEADS = 32
KV_HEADS = 4
HD = 128
TOP = 8
LANES = 128

masked_fill = -1e30
norm_epsilon = 1e-06
bf16 = jnp.bfloat16
f32 = jnp.float32


def attention_kernel(
    block_rows, kv_count, per_group, place_ref, lengths_ref, query_ref, key_ref, value_ref,
    new_key_ref, new_value_ref, out_ref, rows_ref
):
    step = pl.program_id(0)
    cached = key_ref.shape[1]
    heads = kv_count * per_group
    scaling = HD ** (-0.5)
    position = lax.broadcasted_iota(jnp.int32, (heads, cached), 1)
    scores, own = [], []
    for row in range(block_rows):
        queries = query_ref[row]
        score = lax.dot_general(
            queries, key_ref[row], (((1,), (1,)), ((), ())), preferred_element_type=f32
        )
        visible = position < lengths_ref[step * block_rows + row]
        scores.append(jnp.where(visible, score * scaling, masked_fill))
        fresh = new_key_ref[row].astype(f32)
        own.append(jnp.sum(queries.astype(f32) * fresh, axis=1, keepdims=True) * scaling)
    scores = jnp.concatenate(scores, axis=0)
    own = jnp.concatenate(own, axis=0)
    peak = jnp.maximum(jnp.max(scores, axis=1, keepdims=True), own)
    weights = jnp.exp(scores - peak)
    own_weight = jnp.exp(own - peak)
    total = jnp.sum(weights, axis=1, keepdims=True) + own_weight
    weights = weights.astype(bf16)
    inverse = 1.0 / total
    for row in range(block_rows):
        at = slice(row * heads, (row + 1) * heads)
        blended = jnp.dot(weights[at], value_ref[row], preferred_element_type=f32)
        fresh = new_value_ref[row].astype(f32)
        blended = (blended + own_weight[at] * fresh) * inverse[at]
        for kv in range(kv_count):
            rows_ref[step * block_rows + row, kv * per_group : (kv + 1) * per_group, :] = blended[
                kv * per_group : (kv + 1) * per_group, kv * HD : (kv + 1) * HD
            ]

    @pl.when(step == pl.num_programs(0) - 1)
    def _():
        for head in range(heads):
            out_ref[:, head * HD : (head + 1) * HD] = rows_ref[:, head, :].astype(bf16)


def attend(query, key_cache, value_cache, new_key, new_value, lengths, tp_index):
    rows, width = query.shape
    cached = key_cache.shape[1]
    heads = width // HD
    grouping = HEADS // KV_HEADS
    kv_count = max(1, heads // grouping)
    per_group = heads // kv_count
    kv_block = tp_index * heads // grouping // kv_count
    kv_width = kv_count * HD
    spread = query.reshape(rows, kv_count, per_group, 1, HD) * jnp.eye(kv_count, dtype=bf16)[
        None, :, None, :, None
    ]
    spread = spread.reshape(rows, heads, kv_width)
    fresh_key = lax.dynamic_slice_in_dim(new_key, kv_block * kv_width, kv_width, 1)
    fresh_value = lax.dynamic_slice_in_dim(new_value, kv_block * kv_width, kv_width, 1)
    block_rows = 4
    grid_spec = pltpu.PrefetchScalarGridSpec(
        num_scalar_prefetch=2,
        grid=(rows // block_rows,),
        in_specs=[
            pl.BlockSpec((block_rows, heads, kv_width), lambda i, place, lens: (i, 0, 0)),
            pl.BlockSpec((block_rows, cached, kv_width), lambda i, place, lens: (i, 0, place[0])),
            pl.BlockSpec((block_rows, cached, kv_width), lambda i, place, lens: (i, 0, place[0])),
            pl.BlockSpec((block_rows, 1, kv_width), lambda i, place, lens: (i, 0, 0)),
            pl.BlockSpec((block_rows, 1, kv_width), lambda i, place, lens: (i, 0, 0)),
        ],
        out_specs=pl.BlockSpec((rows, width), lambda i, place, lens: (0, 0)),
        scratch_shapes=[pltpu.VMEM((rows, heads, HD), f32)],
    )
    return pl.pallas_call(
        functools.partial(attention_kernel, block_rows, kv_count, per_group),
        grid_spec=grid_spec,
        out_shape=jax.ShapeDtypeStruct((rows, width), bf16),
        compiler_params=pltpu.CompilerParams(
            dimension_semantics=("arbitrary",), vmem_limit_bytes=16 * 2**20
        ),
        name="attention",
    )(
        kv_block.astype(jnp.int32).reshape(1),
        lengths,
        spread,
        key_cache,
        value_cache,
        fresh_key.reshape(rows, 1, kv_width),
        fresh_value.reshape(rows, 1, kv_width),
    )


def shift(array, axis, by):
    size = lax.axis_size(axis)
    return lax.ppermute(array, axis, [(i, (i + by) % size) for i in range(size)])


def shards(
    query,
    key_cache,
    value_cache,
    new_key,
    new_value,
    lengths,
    out_weight,
    residual,
    norm_gain,
    expert_ids,
    gate_weights,
    w_gate,
    w_up,
    w_down,
):
    rows = query.shape[0]
    width = residual.shape[1]
    n_ep, n_tp, n_sp = lax.axis_size("ep"), lax.axis_size("tp"), lax.axis_size("sp")
    ep_index, tp_index, sp_index = (lax.axis_index(name) for name in ("ep", "tp", "sp"))
    local_experts = w_gate.shape[0]
    experts = local_experts * n_ep * n_sp
    half = width // n_sp
    part = rows // n_tp
    out_width = width // n_tp

    chosen = expert_ids[:, :, None] == jnp.arange(experts, dtype=jnp.int32)
    coefficients = jnp.sum(jnp.where(chosen, gate_weights[:, :, None], 0.0), axis=1)
    high = lax.reduce_precision(coefficients, 8, 7)
    coefficients = jnp.concatenate(
        [high.astype(bf16), (coefficients - high).astype(bf16)], axis=1
    )
    coefficients = jnp.pad(coefficients, ((0, 0), (0, -2 * experts % LANES)))

    attended = attend(query, key_cache, value_cache, new_key, new_value, lengths, tp_index)

    residual_sent = lax.dynamic_slice_in_dim(residual, (1 - sp_index) * half, half, 1)
    packed = jnp.concatenate([attended, residual_sent, coefficients], axis=1)
    packed_other = shift(packed, "sp", 1)
    both = jnp.stack([attended, packed_other[:, : attended.shape[1]]])
    residual_both = jnp.stack(
        [
            lax.dynamic_slice_in_dim(residual, sp_index * half, half, 1),
            packed_other[:, attended.shape[1] : attended.shape[1] + half],
        ]
    )
    coefficients_both = jnp.stack([coefficients, packed_other[:, attended.shape[1] + half :]])
    terms = jnp.dot(
        both.reshape(2 * rows, -1), out_weight, preferred_element_type=f32
    ).reshape(2, n_tp, part, half)

    def block_of(array, index):
        return lax.dynamic_slice_in_dim(array, index % n_tp, 1, 1)[:, 0]

    stream = block_of(terms, tp_index) + block_of(
        residual_both.reshape(2, n_tp, part, half), tp_index
    ).astype(f32)
    for by in range(1, n_tp):
        stream = stream + shift(block_of(terms, tp_index + by).astype(bf16), "tp", by).astype(f32)
    own_coefficients = block_of(coefficients_both.reshape(2, n_tp, part, -1), tp_index)
    piece = jnp.concatenate([stream.astype(bf16), own_coefficients], axis=2)

    along_ep = jnp.stack([piece] + [shift(piece, "ep", by) for by in range(1, n_ep)])
    along_tp = jnp.stack(
        [along_ep] + [shift(along_ep, "tp", by) for by in range(1, n_tp)], axis=1
    )
    other = shift(along_tp[..., :half], "sp", 1)[:, :, ::-1]
    mine = along_tp[..., :half]
    streams = jnp.where(
        sp_index == 0,
        jnp.concatenate([mine, other], axis=4),
        jnp.concatenate([other, mine], axis=4),
    )
    streams = streams.reshape(-1, width)
    values = streams.astype(f32)
    normed = (
        values
        * lax.rsqrt(jnp.mean(values * values, axis=-1, keepdims=True) + norm_epsilon)
        * norm_gain
    ).astype(bf16)
    table = along_tp[..., half:].reshape(streams.shape[0], -1).astype(f32)
    first_expert = (ep_index * n_sp + sp_index) * local_experts
    mixture = 0.0
    for expert in range(local_experts):
        gate_act = jnp.dot(normed, w_gate[expert], preferred_element_type=f32)
        up_act = jnp.dot(normed, w_up[expert], preferred_element_type=f32)
        hidden = (jax.nn.silu(gate_act) * up_act).astype(bf16)
        down = jnp.dot(hidden, w_down[expert], preferred_element_type=f32)
        at = first_expert + expert
        scale = lax.dynamic_slice_in_dim(table, at, 1, 1) + lax.dynamic_slice_in_dim(
            table, at + experts, 1, 1
        )
        mixture = mixture + scale * down

    mixture = mixture.reshape(n_ep, n_tp, 2, part, width)
    mixture = mixture[:, :, 0] + shift(mixture[:, :, 1].astype(bf16), "sp", 1).astype(f32)

    def columns_of(array, index):
        return lax.dynamic_slice_in_dim(array, index % n_tp * out_width, out_width, array.ndim - 1)

    total = columns_of(mixture, tp_index)
    for by in range(1, n_tp):
        arrived = shift(columns_of(mixture, tp_index + by).astype(bf16), "tp", by)
        total = total + jnp.roll(arrived, by, axis=1).astype(f32)
    final = total[0]
    for by in range(1, n_ep):
        final = final + shift(total[by].astype(bf16), "ep", -by).astype(f32)
    own_stream = columns_of(streams.reshape(n_ep, n_tp, 2, part, width)[0, :, 0], tp_index)
    final = (final + own_stream.astype(f32)).astype(bf16)
    order = (tp_index - jnp.arange(n_tp)) % n_tp
    return jnp.take(final, order, axis=0).reshape(rows, out_width)


def solution(mesh):
    placed = (
        P(("groups", "ep", "sp"), "tp"),
        P(("groups", "ep", "sp"), None, None),
        P(("groups", "ep", "sp"), None, None),
        P(("groups", "ep", "sp"), None),
        P(("groups", "ep", "sp"), None),
        P(("groups", "ep", "sp")),
        P("tp", "sp"),
        P(("groups", "ep", "sp"), None),
        P(),
        P(("groups", "ep", "sp"), None),
        P(("groups", "ep", "sp"), None),
        P(("ep", "sp"), None, "tp"),
        P(("ep", "sp"), None, "tp"),
        P(("ep", "sp"), "tp", None),
    )
    return jax.shard_map(
        shards,
        mesh=mesh,
        in_specs=placed,
        out_specs=P(("groups", "ep", "sp"), "tp"),
        check_vma=False,
    )
```

time: 205 us -> 85.2 us (0.42)
  blocking collectives: 59.6 us -> 0 us
  waiting for transfers between devices: 81.6 us -> 27.9 us
  between operations: 13.6 us -> 0.31 us
  starting transfers between devices: 4.65 us -> 16.9 us
  local copies, waits for them, and re-layouts: 24.5 us -> 12.8 us
  Pallas kernels: 0 us -> 5.94 us
    all_to_all x2 -> x0, blocking collectives: 57.4 us -> none  [the longest x1 53.5 us: shards(): lax.all_to_all(outgoing, ('ep', 'sp'), split_axis=0, concat_axis=0, tiled...]
    reduce_scatter x1 -> x0, waiting for transfers between devices: 29.9 us -> none  [expert_layer(): lax.psum_scatter(down_terms.astype(jnp.bfloat16), 'tp', scatter_dimension...]
    ppermute x0 -> x12, waiting for transfers between devices: none -> 27.9 us  [shift(): lax.ppermute(array, axis, [(i, (i + by) % size) for i in range(size)])]
    all_to_all x1 -> x0, waiting for transfers between devices: 26.6 us -> none  [expert_layer(): lax.all_to_all(summed, ('ep', 'sp'), split_axis=0, concat_axis=0, tiled=T...]
    psum x1 -> x0, waiting for transfers between devices: 25.1 us -> none  [shards(): totals = lax.psum(projected, 'tp')]
    ppermute x0 -> x12, starting transfers between devices: none -> 16.9 us  [shift(): lax.ppermute(array, axis, [(i, (i + by) % size) for i in range(size)])]
    dynamic_slice x1, local copies, waits for them, and re-layouts: 7.68 us -> 0.89 us  [shards(): lax.dynamic_slice_in_dim(residual, sp_index * half, half, 1)]
    pallas_call x0 -> x1, Pallas kernels: none -> 5.94 us  [attend(): pl.pallas_call(functools.partial(attention_kernel, block_rows, kv_count,...]
  transfers between devices with their start and end apart: 3 -> 12, of which waited for: 3 -> 10; matrix products, arithmetic and copies ran while one was open for 0% -> 1% of each run, Pallas kernels for 0% -> 0%
where the time goes in v1:
time: 85.2 us; the launch traced here: 84.8 us
  waiting for transfers between devices  27.9 us (33%)
  starting transfers between devices  16.9 us (20%)
  matrix products  16.9 us (20%)
  local copies, waits for them, and re-layouts  12.8 us (15%)
  Pallas kernels  5.94 us (7%)
  other arithmetic  3.98 us (5%)
    ppermute x12, waiting for transfers between devices, shift(): lax.ppermute(array, axis, [(i, (i + by) % size) for i in range(size)])  27.9 us
    ppermute x12, starting transfers between devices, shift(): lax.ppermute(array, axis, [(i, (i + by) % size) for i in range(size)])  16.9 us
    dot_general x2, matrix products, shards(): down = jnp.dot(hidden, w_down[expert], preferred_element_type=f32)  10.6 us
    unnamed x11, local copies, waits for them, and re-layouts  8.66 us
    pallas_call x1, Pallas kernels, attend(): pl.pallas_call(functools.partial(attention_kernel, block_rows, kv_count,...  5.94 us
    dot_general x2, matrix products, shards(): gate_act = jnp.dot(normed, w_gate[expert], preferred_element_type=f32)  3.29 us
    dot_general x1, matrix products, shards(): jnp.dot(both.reshape(2 * rows, -1), out_weight, preferred_element_type=f32)  3.03 us
  transfers between devices with their start and end apart: 12, of which 10 were waited for; matrix products, arithmetic and copies ran while one was open for 1% of the time, Pallas kernels for 0%

profile of v1, /device:TPU:0, one launch (start us, length us, event | category | flops | bytes accessed | tf_op | source)
XLA Modules:
  0.0 84.8 jit_solution(12005069578300466089)
XLA Ops:
  0.0 0.7 select_reduce_fusion
  0.7 0.1 copy.44
  0.8 0.1 copy.43
  0.9 0.1 broadcast_bitcast_fusion
  1.0 0.9 %copy.57 = bf16[4,8,16,128]{3,2,1,0:T(8,128)(2,1)S(1)} copy(bf16[4,8,16,128]{3,1,2,0:T(8,128)(2,1)} %bitcast.138) | data formatting | bytes 262144
  1.9 0.7 dynamic-slice_bitcast_fusion
  2.7 0.1 fusion.73
  2.8 0.9 %constant_dynamic-slice_fusion = (bf16[32,1024]{1,0:T(8,128)(2,1)S(1)}, bf16[32,1024]{1,0:T(8,128)(2,1)S(1)}) fusion(bf16[32,2048]{1,0:T(8,128)(2,1)} %param.21, s32[]{:T(128)S(6)} %select_n.129, s32[]{:T(128)S(6)} %select_n.125), kind=kLoop, calls=%fused_computation.101 | loop fusion | bytes 262152 | tf_op jit(solution)/shard_map/dynamic_slice | solution.py:160
  3.7 0.0 copy-start
  3.7 3.4 %copy-done = bf16[32,256,512]{2,1,0:T(8,128)(2,1)S(1)} copy-done((bf16[32,256,512]{2,1,0:T(8,128)(2,1)S(1)}, bf16[32,256,512]{2,1,0:T(8,128)(2,1)}, u32[]{:S(2)}) %copy-start) | copy-done | bytes 8388632
  7.1 0.0 copy-start.1
  7.1 3.4 %copy-done.1 = bf16[32,256,512]{2,1,0:T(8,128)(2,1)S(1)} copy-done((bf16[32,256,512]{2,1,0:T(8,128)(2,1)S(1)}, bf16[32,256,512]{2,1,0:T(8,128)(2,1)}, u32[]{:S(2)}) %copy-start.1) | copy-done | bytes 8388632
  10.5 0.0 copy-start.2
  10.5 0.7 copy-done.2
  11.2 5.9 %attention.1 = bf16[32,2048]{1,0:T(8,128)(2,1)S(1)} custom-call(s32[1]{0:T(128)} %bitcast.place_ref, s32[32]{0:T(128)S(1)} %copy-done.2, bf16[32,16,256]{2,1,0:T(8,128)(2,1)S(1)} %bitcast_multiply_fusion.query_ref, bf16[32,256,512]{2,1,0:T(8,128)(2,1)S(1)} %copy-done, bf16[32,256,512]{2,1,0:T(8,128)(2,1)S(1)} %copy-done.1, ...), custom_call_target="tpu_custom_call" | custom-call | tf_op jit(solution)/shard_map/attention/pallas_call | solution.py:94
  17.1 0.5 collective-permute-start
  17.6 1.1 %collective-permute-done = bf16[32,3200]{1,0:T(8,128)(2,1)S(1)} collective-permute-done((bf16[32,3200]{1,0:T(8,128)(2,1)S(1)}, bf16[32,3200]{1,0:T(8,128)(2,1)S(1)}, u32[]{:S(2)}, u32[]{:S(2)}) %collective-permute-start) | collective-permute-done | bytes 204832 | tf_op jit(solution)/shard_map/ppermute | solution.py:115
  18.7 3.0 %fusion = f32[2,2,16,1024]{3,2,1,0:T(8,128)S(1)} fusion(bf16[2048,1024]{1,0:T(8,128)(2,1)} %param.20, bf16[1,2,16,2048]{3,2,1,0:T(8,128)(2,1)S(1)} %bitcast.135, bf16[1,2,16,2048]{3,2,1,0:T(8,128)(2,1)S(1)} %bitcast.118), kind=kOutput, calls=%fused_computation.1 | convolution fusion | flops 268566528 | bytes 4718592 | tf_op jit(solution)/shard_map/dot_general | solution.py:165
  21.8 2.9 %collective-permute-start.1 = (bf16[2,16,1024]{2,1,0:T(8,128)(2,1)S(1)}, bf16[2,16,1024]{2,1,0:T(8,128)(2,1)S(1)}, u32[]{:S(2)}, u32[]{:S(2)}) collective-permute-start(bf16[2,16,1024]{2,1,0:T(8,128)(2,1)S(1)} %fusion.63), channel_id=1, source_target_pairs={{0,2},{2,0},{1,3},{3,1},{4,6},{6,4},{5,7},{7,5},{8,10},{10,8},{9,1... | collective-permute-start | bytes 196616 | tf_op jit(solution)/shard_map/ppermute | solution.py:115
  24.7 2.4 %collective-permute-done.1 = bf16[2,16,1024]{2,1,0:T(8,128)(2,1)S(1)} collective-permute-done((bf16[2,16,1024]{2,1,0:T(8,128)(2,1)S(1)}, bf16[2,16,1024]{2,1,0:T(8,128)(2,1)S(1)}, u32[]{:S(2)}, u32[]{:S(2)}) %collective-permute-start.1) | collective-permute-done | bytes 65568 | tf_op jit(solution)/shard_map/ppermute | solution.py:115
  27.2 4.0 %collective-permute-start.4 = (bf16[2,16,1152]{2,1,0:T(8,128)(2,1)S(1)}, bf16[2,16,1152]{2,1,0:T(8,128)(2,1)S(1)}, u32[]{:S(2)}, u32[]{:S(2)}) collective-permute-start(bf16[2,16,1152]{2,1,0:T(8,128)(2,1)S(1)} %get-tuple-element.19), channel_id=1, source_target_pairs={{0,12},{4,0},{8,4},{12,8},{1,13},{5,1},{9,5},{13,9},{2,14},{6,2},{... | collective-permute-start | bytes 221192 | tf_op jit(solution)/shard_map/ppermute | solution.py:115
  31.2 0.0 collective-permute-start.3
  31.2 1.0 %collective-permute-start.2 = (bf16[2,16,1152]{2,1,0:T(8,128)(2,1)S(1)}, bf16[2,16,1152]{2,1,0:T(8,128)(2,1)S(1)}, u32[]{:S(2)}, u32[]{:S(2)}) collective-permute-start(bf16[2,16,1152]{2,1,0:T(8,128)(2,1)S(1)} %get-tuple-element.19), channel_id=1, source_target_pairs={{0,4},{4,8},{8,12},{12,0},{1,5},{5,9},{9,13},{13,1},{2,6},{6,10},{... | collective-permute-start | bytes 221192 | tf_op jit(solution)/shard_map/ppermute | solution.py:115
  32.2 1.3 %collective-permute-done.4 = bf16[2,16,1152]{2,1,0:T(8,128)(2,1)S(1)} collective-permute-done((bf16[2,16,1152]{2,1,0:T(8,128)(2,1)S(1)}, bf16[2,16,1152]{2,1,0:T(8,128)(2,1)S(1)}, u32[]{:S(2)}, u32[]{:S(2)}) %collective-permute-start.4) | collective-permute-done | bytes 73760 | tf_op jit(solution)/shard_map/ppermute | solution.py:115
  33.5 4.1 %collective-permute-done.3 = bf16[2,16,1152]{2,1,0:T(8,128)(2,1)S(1)} collective-permute-done((bf16[2,16,1152]{2,1,0:T(8,128)(2,1)S(1)}, bf16[2,16,1152]{2,1,0:T(8,128)(2,1)S(1)}, u32[]{:S(2)}, u32[]{:S(2)}) %collective-permute-start.3) | collective-permute-done | bytes 73760 | tf_op jit(solution)/shard_map/ppermute | solution.py:115
  37.5 0.0 collective-permute-done.2
  37.5 0.1 fusion.81
  37.6 1.6 %collective-permute-start.5 = (bf16[4,2,16,1152]{3,2,1,0:T(8,128)(2,1)S(1)}, bf16[4,2,16,1152]{3,2,1,0:T(8,128)(2,1)S(1)}, u32[]{:S(2)}, u32[]{:S(2)}) collective-permute-start(bf16[4,2,16,1152]{3,2,1,0:T(8,128)(2,1)S(1)} %get-tuple-element.10), channel_id=1, source_target_pairs={{0,2},{2,0},{1,3},{3,1},{4,6},{6,4},{5,7},{7,5},{8,10},{10,8},{9,1... | collective-permute-start | bytes 884744 | tf_op jit(solution)/shard_map/ppermute | solution.py:115
  39.2 6.2 %collective-permute-done.5 = bf16[4,2,16,1152]{3,2,1,0:T(8,128)(2,1)S(1)} collective-permute-done((bf16[4,2,16,1152]{3,2,1,0:T(8,128)(2,1)S(1)}, bf16[4,2,16,1152]{3,2,1,0:T(8,128)(2,1)S(1)}, u32[]{:S(2)}, u32[]{:S(2)}) %collective-permute-start.5) | collective-permute-done | bytes 294944 | tf_op jit(solution)/shard_map/ppermute | solution.py:115
  45.3 0.1 pad_maximum_fusion
  45.4 0.1 collective-permute-start.6
  45.5 0.0 copy-start.4
  45.6 0.3 add_reduce_fusion
  45.9 1.5 %collective-permute-done.6 = bf16[4,2,2,16,1024]{4,3,2,0,1:T(8,128)(2,1)S(1)} collective-permute-done((bf16[4,2,2,16,1024]{4,3,2,0,1:T(8,128)(2,1)S(1)}, bf16[4,2,2,16,1024]{4,3,2,0,1:T(8,128)(2,1)S(1)}, u32[]{:S(2)}, u32[]{:S(2)}) %collective-permute-start.6) | collective-permute-done | bytes 524320 | tf_op jit(solution)/shard_map/ppermute | solution.py:115
  47.5 0.4 fusion.3
  47.8 0.0 copy-done.4
  47.8 0.0 copy-start.3
  47.8 2.5 %fusion.14 = f32[256,512]{1,0:T(8,128)S(1)} fusion(bf16[2,2048,512]{2,1,0:T(8,128)(2,1)} %param.25, f32[2048]{0:T(1024)S(1)} %copy-done.4, f32[256]{0:T(256)S(1)} %add_rsqrt_fusion, bf16[256,1024]{1,0:T(8,128)(2,1)S(1)} %bitcast.121, bf16[256,1024]{1,0:T(8,128)(2,1)S(1)} %bitcast.126, pred[]{:T(512)S(6)} %eq.37), kind=kOutput, calls=%fused_computation.19 | convolution fusion | flops 543686656 | bytes 3679233 | tf_op jit(solution)/shard_map/dot_general | solution.py:202
  50.3 0.3 copy-done.3
  50.7 0.8 fusion.9
  51.5 5.0 %convolution_multiply_fusion.1 = f32[256,2048]{1,0:T(8,128)} fusion(bf16[2,512,2048]{2,1,0:T(8,128)(2,1)} %param.27, f32[256]{0:T(256)S(1)} %get-tuple-element.6, bf16[2,2048,512]{2,1,0:T(8,128)(2,1)} %param.26, f32[256,512]{1,0:T(8,128)S(1)} %fusion.14, f32[2048]{0:T(1024)S(1)} %copy-done.4, f32[256]{0:T(256)S(1)} %add_rsqrt_fusion, ...), kind=kOutput, calls=%fused_computation.5 | convolution fusion | flops 1081868288 | bytes 7874561 | tf_op jit(solution)/shard_map/dot_general | solution.py:205
  56.5 5.6 %fusion.2 = f32[256,2048]{1,0:T(8,128)} fusion(f32[256,2048]{1,0:T(8,128)} %convolution_multiply_fusion.1, bf16[2,512,2048]{2,1,0:T(8,128)(2,1)} %param.27, f32[256]{0:T(256)S(1)} %get-tuple-element.5, bf16[2,2048,512]{2,1,0:T(8,128)(2,1)} %param.26, f32[256,512]{1,0:T(8,128)S(1)} %fusion.9, f32[2048]{0:T(1024)S(1)} %copy-done.4, f32[256]{0:T(256)S(1)} %add_rsqrt_fusion, ...), kind=kOutput, calls=%fused_computation.4 | convolution fusion | flops 1082392576 | bytes 9971713 | tf_op jit(solution)/shard_map/dot_general | solution.py:205
  62.1 1.3 %fusion.39 = bf16[4,2,16,2048]{3,2,1,0:T(8,128)(2,1)S(1)} fusion(f32[4,2,2,16,2048]{4,3,2,1,0:T(8,128)} %bitcast.130), kind=kLoop, calls=%fused_computation.35 | loop fusion | bytes 1048576 | tf_op jit(solution)/shard_map/convert_element_type | solution.py:213
  63.4 0.2 collective-permute-start.7
  63.6 1.8 %collective-permute-done.7 = bf16[4,2,16,2048]{3,2,1,0:T(8,128)(2,1)S(1)} collective-permute-done((bf16[4,2,16,2048]{3,2,1,0:T(8,128)(2,1)S(1)}, bf16[4,2,16,2048]{3,2,1,0:T(8,128)(2,1)S(1)}, u32[]{:S(2)}, u32[]{:S(2)}) %collective-permute-start.7) | collective-permute-done | bytes 524320 | tf_op jit(solution)/shard_map/ppermute | solution.py:115
  65.4 1.3 %fusion.34 = f32[4,2,16,2048]{3,2,1,0:T(8,128)S(1)} fusion(bf16[4,2,16,2048]{3,2,1,0:T(8,128)(2,1)S(1)} %collective-permute-done.7, f32[4,2,2,16,2048]{4,3,2,1,0:T(8,128)} %bitcast.131), kind=kLoop, calls=%fused_computation.33 | loop fusion | flops 524288 | bytes 2621440 | tf_op jit(solution)/shard_map/add | solution.py:213
  66.8 1.6 %collective-permute-start.8 = (bf16[4,2,16,1024]{3,2,1,0:T(8,128)(2,1)S(1)}, bf16[4,2,16,1024]{3,2,1,0:T(8,128)(2,1)S(1)}, u32[]{:S(2)}, u32[]{:S(2)}) collective-permute-start(bf16[4,2,16,1024]{3,2,1,0:T(8,128)(2,1)S(1)} %dynamic-slice_convert_fusion), channel_id=1, source_target_pairs={{0,2},{2,0},{1,3},{3,1},{4,6},{6,4},{5,7},{7,5},{8,10},{10,8},{9,1... | collective-permute-start | bytes 786440 | tf_op jit(solution)/shard_map/ppermute | solution.py:115
  68.3 0.1 broadcast_in_dim.32
  68.4 0.1 broadcast_in_dim.33
  68.5 6.7 %collective-permute-done.8 = bf16[4,2,16,1024]{3,2,1,0:T(8,128)(2,1)S(1)} collective-permute-done((bf16[4,2,16,1024]{3,2,1,0:T(8,128)(2,1)S(1)}, bf16[4,2,16,1024]{3,2,1,0:T(8,128)(2,1)S(1)}, u32[]{:S(2)}, u32[]{:S(2)}) %collective-permute-start.8) | collective-permute-done | bytes 262176 | tf_op jit(solution)/shard_map/ppermute | solution.py:115
  75.2 0.1 fusion.88
  75.3 0.5 collective-permute-start.11
  75.8 1.7 %collective-permute-start.10 = (bf16[2,16,1024]{2,1,0:T(8,128)(2,1)S(1)}, bf16[2,16,1024]{2,1,0:T(8,128)(2,1)S(1)}, u32[]{:S(2)}, u32[]{:S(2)}) collective-permute-start(bf16[2,16,1024]{2,1,0:T(8,128)(2,1)S(1)} %get-tuple-element.13), channel_id=1, source_target_pairs={{0,8},{4,12},{8,0},{12,4},{1,9},{5,13},{9,1},{13,5},{2,10},{6,14},... | collective-permute-start | bytes 196616 | tf_op jit(solution)/shard_map/ppermute | solution.py:115
  77.5 2.8 %collective-permute-start.9 = (bf16[2,16,1024]{2,1,0:T(8,128)(2,1)S(1)}, bf16[2,16,1024]{2,1,0:T(8,128)(2,1)S(1)}, u32[]{:S(2)}, u32[]{:S(2)}) collective-permute-start(bf16[2,16,1024]{2,1,0:T(8,128)(2,1)S(1)} %get-tuple-element.11), channel_id=1, source_target_pairs={{0,12},{4,0},{8,4},{12,8},{1,13},{5,1},{9,5},{13,9},{2,14},{6,2},{... | collective-permute-start | bytes 196616 | tf_op jit(solution)/shard_map/ppermute | solution.py:115
  80.3 1.7 %collective-permute-done.11 = bf16[2,16,1024]{2,1,0:T(8,128)(2,1)S(1)} collective-permute-done((bf16[2,16,1024]{2,1,0:T(8,128)(2,1)S(1)}, bf16[2,16,1024]{2,1,0:T(8,128)(2,1)S(1)}, u32[]{:S(2)}, u32[]{:S(2)}) %collective-permute-start.11) | collective-permute-done | bytes 65568 | tf_op jit(solution)/shard_map/ppermute | solution.py:115
  82.0 1.4 %collective-permute-done.10 = bf16[2,16,1024]{2,1,0:T(8,128)(2,1)S(1)} collective-permute-done((bf16[2,16,1024]{2,1,0:T(8,128)(2,1)S(1)}, bf16[2,16,1024]{2,1,0:T(8,128)(2,1)S(1)}, u32[]{:S(2)}, u32[]{:S(2)}) %collective-permute-start.10) | collective-permute-done | bytes 65568 | tf_op jit(solution)/shard_map/ppermute | solution.py:115
  83.4 0.0 collective-permute-done.9
  83.4 0.1 fusion.59
  83.5 0.6 gather_fusion
  84.1 0.7 bitcast_select_fusion
  (26 shorter events, 0.4 us)
Async XLA Ops:
  3.7 3.4 %copy-start = (bf16[32,256,512]{2,1,0:T(8,128)(2,1)S(1)}, bf16[32,256,512]{2,1,0:T(8,128)(2,1)}, u32[]{:S(2)}) copy-start(bf16[32,256,512]{2,1,0:T(8,128)(2,1)} %key_ref.1) | copy-start | bytes 25165828
  7.1 3.4 %copy-start.1 = (bf16[32,256,512]{2,1,0:T(8,128)(2,1)S(1)}, bf16[32,256,512]{2,1,0:T(8,128)(2,1)}, u32[]{:S(2)}) copy-start(bf16[32,256,512]{2,1,0:T(8,128)(2,1)} %value_ref.1) | copy-start | bytes 25165828
  10.5 0.7 copy-start.2
  17.1 1.6 %collective-permute-start = (bf16[32,3200]{1,0:T(8,128)(2,1)S(1)}, bf16[32,3200]{1,0:T(8,128)(2,1)S(1)}, u32[]{:S(2)}, u32[]{:S(2)}) collective-permute-start(bf16[32,3200]{1,0:T(8,128)(2,1)S(1)} %pad_maximum_fusion.2), channel_id=1, source_target_pairs={{0,1},{1,0},{2,3},{3,2},{4,5},{5,4},{6,7},{7,6},{8,9},{9,8},{10,11... | collective-permute-start | bytes 614408 | tf_op jit(solution)/shard_map/ppermute | solution.py:115
  21.8 5.3 %collective-permute-start.1 = (bf16[2,16,1024]{2,1,0:T(8,128)(2,1)S(1)}, bf16[2,16,1024]{2,1,0:T(8,128)(2,1)S(1)}, u32[]{:S(2)}, u32[]{:S(2)}) collective-permute-start(bf16[2,16,1024]{2,1,0:T(8,128)(2,1)S(1)} %fusion.63), channel_id=1, source_target_pairs={{0,2},{2,0},{1,3},{3,1},{4,6},{6,4},{5,7},{7,5},{8,10},{10,8},{9,1... | collective-permute-start | bytes 196616 | tf_op jit(solution)/shard_map/ppermute | solution.py:115
  27.2 6.3 %collective-permute-start.4 = (bf16[2,16,1152]{2,1,0:T(8,128)(2,1)S(1)}, bf16[2,16,1152]{2,1,0:T(8,128)(2,1)S(1)}, u32[]{:S(2)}, u32[]{:S(2)}) collective-permute-start(bf16[2,16,1152]{2,1,0:T(8,128)(2,1)S(1)} %get-tuple-element.19), channel_id=1, source_target_pairs={{0,12},{4,0},{8,4},{12,8},{1,13},{5,1},{9,5},{13,9},{2,14},{6,2},{... | collective-permute-start | bytes 221192 | tf_op jit(solution)/shard_map/ppermute | solution.py:115
  31.2 6.3 %collective-permute-start.3 = (bf16[2,16,1152]{2,1,0:T(8,128)(2,1)S(1)}, bf16[2,16,1152]{2,1,0:T(8,128)(2,1)S(1)}, u32[]{:S(2)}, u32[]{:S(2)}) collective-permute-start(bf16[2,16,1152]{2,1,0:T(8,128)(2,1)S(1)} %get-tuple-element.19), channel_id=1, source_target_pairs={{0,8},{4,12},{8,0},{12,4},{1,9},{5,13},{9,1},{13,5},{2,10},{6,14},... | collective-permute-start | bytes 221192 | tf_op jit(solution)/shard_map/ppermute | solution.py:115
  31.2 6.3 %collective-permute-start.2 = (bf16[2,16,1152]{2,1,0:T(8,128)(2,1)S(1)}, bf16[2,16,1152]{2,1,0:T(8,128)(2,1)S(1)}, u32[]{:S(2)}, u32[]{:S(2)}) collective-permute-start(bf16[2,16,1152]{2,1,0:T(8,128)(2,1)S(1)} %get-tuple-element.19), channel_id=1, source_target_pairs={{0,4},{4,8},{8,12},{12,0},{1,5},{5,9},{9,13},{13,1},{2,6},{6,10},{... | collective-permute-start | bytes 221192 | tf_op jit(solution)/shard_map/ppermute | solution.py:115
  37.6 7.7 %collective-permute-start.5 = (bf16[4,2,16,1152]{3,2,1,0:T(8,128)(2,1)S(1)}, bf16[4,2,16,1152]{3,2,1,0:T(8,128)(2,1)S(1)}, u32[]{:S(2)}, u32[]{:S(2)}) collective-permute-start(bf16[4,2,16,1152]{3,2,1,0:T(8,128)(2,1)S(1)} %get-tuple-element.10), channel_id=1, source_target_pairs={{0,2},{2,0},{1,3},{3,1},{4,6},{6,4},{5,7},{7,5},{8,10},{10,8},{9,1... | collective-permute-start | bytes 884744 | tf_op jit(solution)/shard_map/ppermute | solution.py:115
  45.4 2.0 %collective-permute-start.6 = (bf16[4,2,2,16,1024]{4,3,2,0,1:T(8,128)(2,1)S(1)}, bf16[4,2,2,16,1024]{4,3,2,0,1:T(8,128)(2,1)S(1)}, u32[]{:S(2)}, u32[]{:S(2)}) collective-permute-start(bf16[4,2,2,16,1024]{4,3,2,0,1:T(8,128)(2,1)S(1)} %pad_maximum_fusion), channel_id=1, source_target_pairs={{0,1},{1,0},{2,3},{3,2},{4,5},{5,4},{6,7},{7,6},{8,9},{9,8},{10,11... | collective-permute-start | bytes 1572872 | tf_op jit(solution)/shard_map/ppermute | solution.py:115
  45.5 2.3 %copy-start.4 = (f32[2048]{0:T(1024)S(1)}, f32[2048]{0:T(1024)}, u32[]{:S(2)}) copy-start(f32[2048]{0:T(1024)} %param.22) | copy-start | bytes 24580
  47.8 2.8 %copy-start.3 = (bf16[2,2048,512]{2,1,0:T(8,128)(2,1)S(1)}, bf16[2,2048,512]{2,1,0:T(8,128)(2,1)}, u32[]{:S(2)}) copy-start(bf16[2,2048,512]{2,1,0:T(8,128)(2,1)} %param.25) | copy-start | bytes 12582916
  63.4 2.0 %collective-permute-start.7 = (bf16[4,2,16,2048]{3,2,1,0:T(8,128)(2,1)S(1)}, bf16[4,2,16,2048]{3,2,1,0:T(8,128)(2,1)S(1)}, u32[]{:S(2)}, u32[]{:S(2)}) collective-permute-start(bf16[4,2,16,2048]{3,2,1,0:T(8,128)(2,1)S(1)} %fusion.39), channel_id=1, source_target_pairs={{0,1},{1,0},{2,3},{3,2},{4,5},{5,4},{6,7},{7,6},{8,9},{9,8},{10,11... | collective-permute-start | bytes 1572872 | tf_op jit(solution)/shard_map/ppermute | solution.py:115
  66.8 8.4 %collective-permute-start.8 = (bf16[4,2,16,1024]{3,2,1,0:T(8,128)(2,1)S(1)}, bf16[4,2,16,1024]{3,2,1,0:T(8,128)(2,1)S(1)}, u32[]{:S(2)}, u32[]{:S(2)}) collective-permute-start(bf16[4,2,16,1024]{3,2,1,0:T(8,128)(2,1)S(1)} %dynamic-slice_convert_fusion), channel_id=1, source_target_pairs={{0,2},{2,0},{1,3},{3,1},{4,6},{6,4},{5,7},{7,5},{8,10},{10,8},{9,1... | collective-permute-start | bytes 786440 | tf_op jit(solution)/shard_map/ppermute | solution.py:115
  75.3 6.7 %collective-permute-start.11 = (bf16[2,16,1024]{2,1,0:T(8,128)(2,1)S(1)}, bf16[2,16,1024]{2,1,0:T(8,128)(2,1)S(1)}, u32[]{:S(2)}, u32[]{:S(2)}) collective-permute-start(bf16[2,16,1024]{2,1,0:T(8,128)(2,1)S(1)} %get-tuple-element.12), channel_id=1, source_target_pairs={{0,4},{4,8},{8,12},{12,0},{1,5},{5,9},{9,13},{13,1},{2,6},{6,10},{... | collective-permute-start | bytes 196616 | tf_op jit(solution)/shard_map/ppermute | solution.py:115
  75.8 7.6 %collective-permute-start.10 = (bf16[2,16,1024]{2,1,0:T(8,128)(2,1)S(1)}, bf16[2,16,1024]{2,1,0:T(8,128)(2,1)S(1)}, u32[]{:S(2)}, u32[]{:S(2)}) collective-permute-start(bf16[2,16,1024]{2,1,0:T(8,128)(2,1)S(1)} %get-tuple-element.13), channel_id=1, source_target_pairs={{0,8},{4,12},{8,0},{12,4},{1,9},{5,13},{9,1},{13,5},{2,10},{6,14},... | collective-permute-start | bytes 196616 | tf_op jit(solution)/shard_map/ppermute | solution.py:115
  77.5 5.9 %collective-permute-start.9 = (bf16[2,16,1024]{2,1,0:T(8,128)(2,1)S(1)}, bf16[2,16,1024]{2,1,0:T(8,128)(2,1)S(1)}, u32[]{:S(2)}, u32[]{:S(2)}) collective-permute-start(bf16[2,16,1024]{2,1,0:T(8,128)(2,1)S(1)} %get-tuple-element.11), channel_id=1, source_target_pairs={{0,12},{4,0},{8,4},{12,8},{1,13},{5,1},{9,5},{13,9},{2,14},{6,2},{... | collective-permute-start | bytes 196616 | tf_op jit(solution)/shard_map/ppermute | solution.py:115

commit v2 on v0

v2 whole, which is shorter than its diff:
```python
import functools

import jax
import jax.numpy as jnp
from jax import lax
from jax.experimental import pallas as pl
from jax.experimental.pallas import tpu as pltpu
from jax.sharding import PartitionSpec as P

HEADS = 32
KV_HEADS = 4
HD = 128
LANES = 128
MIB = 2**20

masked_fill = -1e30
norm_epsilon = 1e-06
bf16 = jnp.bfloat16
f32 = jnp.float32


def attention_kernel(
    kv_count, per_group, chunk, experts, kv_block_of, lengths_hbm, query_hbm, key_hbm, value_hbm,
    new_key_hbm, new_value_hbm, residual_hbm, ids_hbm, gates_hbm, weight_hbm,
    packed_ref, base_ref, weight_ref,
    query_ref, key_ref, value_ref, new_key_ref, new_value_ref, residual_ref, ids_ref, gates_ref,
    rows_ref, lengths_ref, small_sems, cache_sems, weight_sem,
):
    rows, cached, kv_width = key_ref.shape
    heads = kv_count * per_group
    half = base_ref.shape[1]
    chunks = rows // chunk
    kv_at = pl.multiple_of(kv_block_of(lax.axis_index("tp")) * kv_width, HD)
    sp_index = lax.axis_index("sp")
    kv_cols = pl.ds(kv_at, kv_width)
    small = [
        pltpu.make_async_copy(source, target, small_sems.at[i])
        for i, (source, target) in enumerate(
            [
                (query_hbm, query_ref),
                (new_key_hbm.at[:, kv_cols], new_key_ref),
                (new_value_hbm.at[:, kv_cols], new_value_ref),
                (lengths_hbm, lengths_ref),
                (residual_hbm, residual_ref),
                (ids_hbm, ids_ref),
                (gates_hbm, gates_ref),
            ]
        )
    ]
    for copy in small[:4]:
        copy.start()
    cache_copies = []
    for i in range(chunks):
        at = pl.ds(i * chunk, chunk)
        pair = [
            pltpu.make_async_copy(
                source.at[at, :, kv_cols], target.at[at], cache_sems.at[which, i]
            )
            for which, (source, target) in enumerate(
                [(key_hbm, key_ref), (value_hbm, value_ref)]
            )
        ]
        for copy in pair:
            copy.start()
        cache_copies.append(pair)
    for copy in small[4:]:
        copy.start()
    weight_copy = pltpu.make_async_copy(weight_hbm, weight_ref, weight_sem)
    weight_copy.start()
    for copy in small[:4]:
        copy.wait()

    scaling = HD ** (-0.5)
    position = lax.broadcasted_iota(jnp.int32, (heads, cached), 1)
    for head in range(heads):
        kv, group = head // per_group, head % per_group
        rows_ref[kv, pl.ds(group, rows, stride=per_group), :] = query_ref[
            :, head * HD : (head + 1) * HD
        ].astype(f32)
    blank = jnp.zeros((per_group, HD), f32)
    for i in range(chunks):
        cache_copies[i][0].wait()
        scores, own = [], []
        for row in range(i * chunk, (i + 1) * chunk):
            at = slice(row * per_group, (row + 1) * per_group)
            queries = jnp.concatenate(
                [
                    jnp.concatenate(
                        [rows_ref[kv, at, :] if kv == other else blank for other in range(kv_count)],
                        axis=1,
                    )
                    for kv in range(kv_count)
                ],
                axis=0,
            )
            score = lax.dot_general(
                queries.astype(bf16),
                key_ref[row],
                (((1,), (1,)), ((), ())),
                preferred_element_type=f32,
            )
            visible = position < lengths_ref[row]
            scores.append(jnp.where(visible, score * scaling, masked_fill))
            fresh = new_key_ref[row : row + 1, :].astype(f32)
            own.append(jnp.sum(queries * fresh, axis=1, keepdims=True) * scaling)
        scores = jnp.concatenate(scores, axis=0)
        own = jnp.concatenate(own, axis=0)
        peak = jnp.maximum(jnp.max(scores, axis=1, keepdims=True), own)
        weights = jnp.exp(scores - peak)
        own_weight = jnp.exp(own - peak)
        inverse = 1.0 / (jnp.sum(weights, axis=1, keepdims=True) + own_weight)
        weights = weights.astype(bf16)
        cache_copies[i][1].wait()
        for row in range(i * chunk, (i + 1) * chunk):
            at = slice((row - i * chunk) * heads, (row - i * chunk + 1) * heads)
            blended = jnp.dot(weights[at], value_ref[row], preferred_element_type=f32)
            fresh = new_value_ref[row : row + 1, :].astype(f32)
            blended = (blended + own_weight[at] * fresh) * inverse[at]
            for kv in range(kv_count):
                rows_ref[kv, row * per_group : (row + 1) * per_group, :] = blended[
                    kv * per_group : (kv + 1) * per_group, kv * HD : (kv + 1) * HD
                ]
    for copy in small[4:]:
        copy.wait()
    width = heads * HD
    for head in range(heads):
        kv, group = head // per_group, head % per_group
        packed_ref[:, head * HD : (head + 1) * HD] = rows_ref[
            kv, pl.ds(group, rows, stride=per_group), :
        ].astype(bf16)
    packed_ref[:, width : width + half] = residual_ref[
        :, pl.ds(pl.multiple_of((1 - sp_index) * half, LANES), half)
    ]
    base_ref[...] = residual_ref[:, pl.ds(pl.multiple_of(sp_index * half, LANES), half)]
    spare = packed_ref.shape[1] - width - half
    place = lax.broadcasted_iota(jnp.int32, (spare, rows), 0)
    expert = jnp.where(place < experts, place, place - experts)
    table = jnp.zeros((spare, rows), f32)
    for k in range(ids_ref.shape[0]):
        table = table + jnp.where(ids_ref[k : k + 1, :] == expert, gates_ref[k : k + 1, :], 0.0)
    high = table.astype(bf16).astype(f32)
    table = jnp.where(place < experts, high, table - high)
    packed_ref[:, width + half :] = table.T.astype(bf16)
    weight_copy.wait()


def in_hbm(array):
    return pltpu.with_memory_space_constraint(array, pltpu.HBM)


def in_vmem(array):
    return pltpu.with_memory_space_constraint(array, pltpu.VMEM)


ANYWHERE = pl.BlockSpec(memory_space=pl.ANY)
WHOLE = pl.BlockSpec(memory_space=pltpu.VMEM)


def attend(
    query, key_cache, value_cache, new_key, new_value, lengths, residual, expert_ids,
    gate_weights, out_weight, experts, n_sp
):
    rows, width = query.shape
    cached = key_cache.shape[1]
    heads = width // HD
    grouping = HEADS // KV_HEADS
    kv_count = max(1, heads // grouping)
    per_group = heads // kv_count
    kv_width = kv_count * HD

    def kv_block_of(tp_index):
        return tp_index * heads // grouping // kv_count

    half = residual.shape[1] // n_sp
    spare = -(-2 * experts // LANES) * LANES
    chunk = min(16, rows)
    arrays = [
        lengths, query, key_cache, value_cache, new_key, new_value, residual, expert_ids.T,
        gate_weights.T, out_weight
    ]
    return pl.pallas_call(
        functools.partial(attention_kernel, kv_count, per_group, chunk, experts, kv_block_of),
        in_specs=[ANYWHERE] * len(arrays),
        out_specs=[WHOLE] * 3,
        out_shape=[
            pltpu.VMEM((rows, width + half + spare), bf16),
            pltpu.VMEM((rows, half), bf16),
            pltpu.VMEM(out_weight.shape, bf16),
        ],
        scratch_shapes=[
            pltpu.VMEM((rows, width), bf16),
            pltpu.VMEM((rows, cached, kv_width), bf16),
            pltpu.VMEM((rows, cached, kv_width), bf16),
            pltpu.VMEM((rows, kv_width), bf16),
            pltpu.VMEM((rows, kv_width), bf16),
            pltpu.VMEM(residual.shape, bf16),
            pltpu.VMEM((expert_ids.shape[1], rows), jnp.int32),
            pltpu.VMEM((expert_ids.shape[1], rows), f32),
            pltpu.VMEM((kv_count, rows * per_group, HD), f32),
            pltpu.SMEM((rows,), jnp.int32),
            pltpu.SemaphoreType.DMA((7,)),
            pltpu.SemaphoreType.DMA((2, rows // chunk)),
            pltpu.SemaphoreType.DMA,
        ],
        compiler_params=pltpu.CompilerParams(vmem_limit_bytes=24 * MIB),
        name="attention",
    )(*map(in_hbm, arrays))


def project_kernel(width, packed_ref, other_ref, weight_ref, terms_ref, sent_ref):
    both = jnp.concatenate([packed_ref[:, :width], other_ref[:, :width]], axis=0)
    terms = jnp.dot(both, weight_ref[...], preferred_element_type=f32)
    terms_ref[...] = terms
    sent_ref[...] = terms.astype(bf16)


def project(packed, packed_other, weight):
    shape = (2 * packed.shape[0], weight.shape[1])
    return pl.pallas_call(
        functools.partial(project_kernel, weight.shape[0]),
        in_specs=[WHOLE] * 3,
        out_specs=[WHOLE] * 2,
        out_shape=[pltpu.VMEM(shape, f32), pltpu.VMEM(shape, bf16)],
        compiler_params=pltpu.CompilerParams(vmem_limit_bytes=8 * MIB),
        name="project",
    )(in_vmem(packed), in_vmem(packed_other), in_vmem(weight))


def load_kernel(*refs):
    *arrays, sems = refs
    count = len(arrays) // 2
    copies = [
        pltpu.make_async_copy(arrays[i], arrays[count + i], sems.at[i]) for i in range(count)
    ]
    for copy in copies:
        copy.start()
    for copy in copies:
        copy.wait()


def load(*arrays):
    return pl.pallas_call(
        load_kernel,
        in_specs=[ANYWHERE] * len(arrays),
        out_specs=[WHOLE] * len(arrays),
        out_shape=[pltpu.VMEM(array.shape, array.dtype) for array in arrays],
        scratch_shapes=[pltpu.SemaphoreType.DMA((len(arrays),))],
        compiler_params=pltpu.CompilerParams(vmem_limit_bytes=16 * MIB),
        cost_estimate=pl.CostEstimate(
            flops=0, bytes_accessed=2 * sum(array.nbytes for array in arrays), transcendentals=0
        ),
        name="load_weights",
    )(*map(in_hbm, arrays))


def experts_kernel(experts, first_of, places, *refs):
    count = len(places)
    mine, other = refs[:count], refs[count : 2 * count]
    gain_ref, gate_ref, up_ref, down_ref, keep_ref, send_ref, rows_ref, table_ref = refs[2 * count :]
    half = rows_ref.shape[1] // 2
    rows = rows_ref.shape[0]
    sp_index = lax.axis_index("sp")
    tp_index = lax.axis_index("tp")
    my_cols = pl.ds(pl.multiple_of(sp_index * half, LANES), half)
    other_cols = pl.ds(pl.multiple_of((1 - sp_index) * half, LANES), half)
    for a, b, (start, step, flip) in zip(mine, other, places):
        m = a.shape[0] // 2
        at = start if flip is None else pl.multiple_of(start + (tp_index ^ flip) * step, step)
        first, second = pl.ds(at, m), pl.ds(rows // 2 + at, m)
        rows_ref[first, my_cols] = a[:m, :half]
        rows_ref[second, my_cols] = a[m:, :half]
        rows_ref[first, other_cols] = b[m:, :half]
        rows_ref[second, other_cols] = b[:m, :half]
        table_ref[first, :] = a[:m, half:].astype(f32)
        table_ref[second, :] = a[m:, half:].astype(f32)
    values = rows_ref[...].astype(f32)
    inverse = lax.rsqrt(jnp.mean(values * values, axis=1, keepdims=True) + norm_epsilon)
    rows_ref[...] = (values * inverse * gain_ref[...]).astype(bf16)
    first_expert = first_of(lax.axis_index("ep"), sp_index)
    table = table_ref[...]
    lane = lax.broadcasted_iota(jnp.int32, table.shape, 1)
    total = None
    for e in range(gate_ref.shape[0]):
        wanted = (lane == first_expert + e) | (lane == first_expert + e + experts)
        scale = jnp.sum(jnp.where(wanted, table, 0.0), axis=1, keepdims=True)
        normed = rows_ref[...]
        gate = jnp.dot(normed, gate_ref[e], preferred_element_type=f32)
        up = jnp.dot(normed, up_ref[e], preferred_element_type=f32)
        hidden = (gate / (1.0 + jnp.exp(-gate)) * up * scale).astype(bf16)
        term = jnp.dot(hidden, down_ref[e], preferred_element_type=f32)
        total = term if total is None else total + term
    keep_ref[...] = total[: rows // 2]
    send_ref[...] = total[rows // 2 :].astype(bf16)


def run_experts(mine, other, places, gain, gate, up, down, experts, n_sp):
    rows = sum(array.shape[0] for array in mine)
    width = gain.shape[0]
    local = gate.shape[0]
    arrays = [*mine, *other, gain.reshape(1, width), gate, up, down]
    return pl.pallas_call(
        functools.partial(experts_kernel, experts, lambda e, s: (e * n_sp + s) * local, places),
        in_specs=[WHOLE] * len(arrays),
        out_specs=[WHOLE] * 2,
        out_shape=[pltpu.VMEM((rows // 2, width), f32), pltpu.VMEM((rows // 2, width), bf16)],
        scratch_shapes=[
            pltpu.VMEM((rows, width), bf16),
            pltpu.VMEM((rows, mine[0].shape[1] - width // 2), f32),
        ],
        compiler_params=pltpu.CompilerParams(vmem_limit_bytes=(24 if rows <= 256 else 48) * MIB),
        name="experts",
    )(*[array if array.shape[0] == 1 else in_vmem(array) for array in arrays])


def swap(array, axis, by=1):
    size = lax.axis_size(axis)
    return lax.ppermute(array, axis, [(i, i ^ by) for i in range(size)])


def shards(
    query,
    key_cache,
    value_cache,
    new_key,
    new_value,
    lengths,
    out_weight,
    residual,
    norm_gain,
    expert_ids,
    gate_weights,
    w_gate,
    w_up,
    w_down,
):
    rows = query.shape[0]
    width = residual.shape[1]
    n_ep, n_tp, n_sp = lax.axis_size("ep"), lax.axis_size("tp"), lax.axis_size("sp")
    tp_index, sp_index = lax.axis_index("tp"), lax.axis_index("sp")
    experts = w_gate.shape[0] * n_ep * n_sp
    half = width // n_sp
    part = rows // n_tp
    out_width = width // n_tp
    heads_width = query.shape[1]

    packed, base, weight = attend(
        query, key_cache, value_cache, new_key, new_value, lengths, residual, expert_ids,
        gate_weights, out_weight, experts, n_sp
    )
    packed_other = swap(packed, "sp")
    terms, sent = project(packed, packed_other, weight)
    totals = terms
    for by in range(1, n_tp):
        totals = totals + swap(sent, "tp", by).astype(f32)
    residual_both = jnp.concatenate([base, packed_other[:, heads_width : heads_width + half]], axis=0)
    table = jnp.concatenate([packed[:, heads_width + half :], packed_other[:, heads_width + half :]], axis=0)
    stream = (totals + residual_both.astype(f32)).astype(bf16)
    chip = jnp.concatenate([stream, table], axis=1)
    piece = lax.dynamic_slice_in_dim(
        chip.reshape(2, n_tp, part, -1), tp_index, 1, 1
    ).reshape(2 * part, -1)

    mine, places = [chip], [(0, rows, None)]
    for by in range(1, n_ep):
        arrived = swap(piece, "ep", by)
        for flip in range(n_tp):
            mine.append(swap(arrived, "tp", flip) if flip else arrived)
            places.append((by * rows, part, flip))
    w_gate, w_up, w_down, _ = lax.optimization_barrier((w_gate, w_up, w_down, piece))
    w_gate, w_up, w_down = load(w_gate, w_up, w_down)
    if part % 16:
        blocks = jnp.stack(mine[1:]).reshape(n_ep - 1, n_tp, 2, part, -1)
        bit = 1
        while bit < n_tp:
            flipped = blocks[:, jnp.array([j ^ bit for j in range(n_tp)])]
            blocks = jnp.where(tp_index & bit, flipped, blocks)
            bit *= 2
        blocks = blocks.transpose(2, 0, 1, 3, 4).reshape(2, (n_ep - 1) * rows, -1)
        mine = [jnp.concatenate([chip.reshape(2, rows, -1), blocks], axis=1).reshape(2 * n_ep * rows, -1)]
        places = [(0, rows, None)]
    other = [swap(array, "sp") for array in mine]
    keep, send = run_experts(
        mine, other, tuple(places), norm_gain, w_gate, w_up, w_down, experts, n_sp
    )
    mixture = (keep + swap(send, "sp").astype(f32)).reshape(n_ep, rows, width)

    def columns_of(array, index):
        return lax.dynamic_slice_in_dim(array, index * out_width, out_width, array.ndim - 1)

    total = columns_of(mixture, tp_index)
    for by in range(1, n_tp):
        total = total + swap(columns_of(mixture, tp_index ^ by).astype(bf16), "tp", by).astype(f32)
    final = total[0]
    for by in range(1, n_ep):
        final = final + swap(total[by].astype(bf16), "ep", by).astype(f32)

    start = tp_index * out_width - sp_index * half
    local = lax.dynamic_slice_in_dim(totals[:rows], jnp.clip(start, 0, half - out_width), out_width, 1)
    aside = jnp.clip(tp_index * out_width - sp_index * half, 0, half - out_width)
    arrived = swap(lax.dynamic_slice_in_dim(totals[rows:], aside, out_width, 1).astype(bf16), "sp")
    here = tp_index * out_width // half == sp_index
    projected = jnp.where(here, local, arrived.astype(f32))
    return (final + (projected + columns_of(residual, tp_index).astype(f32))).astype(bf16)


def solution(mesh):
    placed = (
        P(("groups", "ep", "sp"), "tp"),
        P(("groups", "ep", "sp"), None, None),
        P(("groups", "ep", "sp"), None, None),
        P(("groups", "ep", "sp"), None),
        P(("groups", "ep", "sp"), None),
        P(("groups", "ep", "sp")),
        P("tp", "sp"),
        P(("groups", "ep", "sp"), None),
        P(),
        P(("groups", "ep", "sp"), None),
        P(("groups", "ep", "sp"), None),
        P(("ep", "sp"), None, "tp"),
        P(("ep", "sp"), None, "tp"),
        P(("ep", "sp"), "tp", None),
    )
    return jax.shard_map(
        shards,
        mesh=mesh,
        in_specs=placed,
        out_specs=P(("groups", "ep", "sp"), "tp"),
        check_vma=False,
    )
```

time: 205 us -> 59.3 us (0.29)
  blocking collectives: 59.6 us -> 0 us
  waiting for transfers between devices: 81.6 us -> 22.5 us
  local copies, waits for them, and re-layouts: 24.5 us -> 0.1 us
  matrix products: 18 us -> 0 us
  starting transfers between devices: 4.65 us -> 21.1 us
  Pallas kernels: 0 us -> 14.4 us
  between operations: 13.6 us -> 0.18 us
    all_to_all x2 -> x0, blocking collectives: 57.4 us -> none  [the longest x1 53.5 us: shards(): lax.all_to_all(outgoing, ('ep', 'sp'), split_axis=0, concat_axis=0, tiled...]
    reduce_scatter x1 -> x0, waiting for transfers between devices: 29.9 us -> none  [expert_layer(): lax.psum_scatter(down_terms.astype(jnp.bfloat16), 'tp', scatter_dimension...]
    all_to_all x1 -> x0, waiting for transfers between devices: 26.6 us -> none  [expert_layer(): lax.all_to_all(summed, ('ep', 'sp'), split_axis=0, concat_axis=0, tiled=T...]
    psum x1 -> x0, waiting for transfers between devices: 25.1 us -> none  [shards(): totals = lax.psum(projected, 'tp')]
    ppermute x0 -> x21, waiting for transfers between devices: none -> 22.5 us  [swap(): return lax.ppermute(array, axis, [(i, i ^ by) for i in range(size)])]
    ppermute x0 -> x21, starting transfers between devices: none -> 21.1 us  [swap(): return lax.ppermute(array, axis, [(i, i ^ by) for i in range(size)])]
    dot_general x8 -> x0, matrix products: 18 us -> none  [the longest x1 7.25 us: expert_layer(): jnp.einsum('sjcf,jfd->sjcd', hidden, w_down, preferred_element_type=jnp.f...]
    pallas_call x0 -> x4, Pallas kernels: none -> 14.4 us  [the longest x1 4.91 us: attend(): pl.pallas_call(functools.partial(attention_kernel, kv_count, per_group, c...]
  transfers between devices with their start and end apart: 3 -> 21, of which waited for: 3 -> 11; matrix products, arithmetic and copies ran while one was open for 0% -> 0% of each run, Pallas kernels for 0% -> 8%
where the time goes in v2:
time: 59.3 us; the launch traced here: 59.2 us
  waiting for transfers between devices  22.5 us (38%)
  starting transfers between devices  21.1 us (36%)
  Pallas kernels  14.4 us (24%)
  other arithmetic  0.93 us (2%)
    ppermute x21, waiting for transfers between devices, swap(): return lax.ppermute(array, axis, [(i, i ^ by) for i in range(size)])  22.5 us
    ppermute x21, starting transfers between devices, swap(): return lax.ppermute(array, axis, [(i, i ^ by) for i in range(size)])  21.1 us
    pallas_call x1, Pallas kernels, attend(): pl.pallas_call(functools.partial(attention_kernel, kv_count, per_group, c...  4.91 us
    pallas_call x1, Pallas kernels, load(): pl.pallas_call(load_kernel, in_specs=[ANYWHERE] * len(arrays), out_specs=...  4.68 us
    pallas_call x1, Pallas kernels, run_experts(): pl.pallas_call(functools.partial(experts_kernel, experts, lambda e, s: (e...  3.93 us
  transfers between devices with their start and end apart: 21, of which 11 were waited for; matrix products, arithmetic and copies ran while one was open for 0% of the time, Pallas kernels for 8%

profile of v2, /device:TPU:0, one launch (start us, length us, event | category | flops | bytes accessed | tf_op | source)
XLA Modules:
  0.0 59.2 jit_solution(6422764139694209213)
XLA Ops:
  0.0 4.9 %attention.1 = (bf16[32,3200]{1,0:T(8,128)(2,1)S(1)}, bf16[32,1024]{1,0:T(8,128)(2,1)S(1)}, bf16[2048,1024]{1,0:T(8,128)(2,1)S(1)}) custom-call(s32[32]{0:T(128)} %lengths_hbm.1, bf16[32,2048]{1,0:T(8,128)(2,1)} %query_hbm.1, bf16[32,256,512]{2,1,0:T(8,128)(2,1)} %key_hbm.1, bf16[32,256,512]{2,1,0:T(8,128)(2,1)} %value_hbm.1, bf16[32,512]{1,0:T(8,128)(2,1)} %new_key_hbm.1, ...), custom_call_target="tpu_custom_call" | custom-call | tf_op jit(solution)/shard_map/attention/pallas_call | solution.py:181
  4.9 0.5 collective-permute-start
  5.4 1.1 %collective-permute-done.other_ref = bf16[32,3200]{1,0:T(8,128)(2,1)S(1)} collective-permute-done((bf16[32,3200]{1,0:T(8,128)(2,1)S(1)}, bf16[32,3200]{1,0:T(8,128)(2,1)S(1)}, u32[]{:S(2)}, u32[]{:S(2)}) %collective-permute-start) | collective-permute-done | bytes 204832 | tf_op jit(solution)/shard_map/ppermute | solution.py:317
  6.5 0.9 %project.1 = (f32[64,1024]{1,0:T(8,128)S(1)}, bf16[64,1024]{1,0:T(8,128)(2,1)S(1)}) custom-call(bf16[32,3200]{1,0:T(8,128)(2,1)S(1)} %get-tuple-element.18.packed_ref, bf16[32,3200]{1,0:T(8,128)(2,1)S(1)} %collective-permute-done.other_ref, bf16[2048,1024]{1,0:T(8,128)(2,1)S(1)} %get-tuple-element.19.weight_ref), custom_call_target="tpu_custom_call" | custom-call | tf_op jit(solution)/shard_map/project/pallas_call | solution.py:219
  7.4 2.9 %collective-permute-start.1 = (bf16[64,1024]{1,0:T(8,128)(2,1)S(1)}, bf16[64,1024]{1,0:T(8,128)(2,1)S(1)}, u32[]{:S(2)}, u32[]{:S(2)}) collective-permute-start(bf16[64,1024]{1,0:T(8,128)(2,1)S(1)} %get-tuple-element.21), channel_id=1, source_target_pairs={{0,2},{2,0},{1,3},{3,1},{4,6},{6,4},{5,7},{7,5},{8,10},{10,8},{9,1... | collective-permute-start | bytes 393224 | tf_op jit(solution)/shard_map/ppermute | solution.py:317
  10.3 3.8 %collective-permute-done.1 = bf16[64,1024]{1,0:T(8,128)(2,1)S(1)} collective-permute-done((bf16[64,1024]{1,0:T(8,128)(2,1)S(1)}, bf16[64,1024]{1,0:T(8,128)(2,1)S(1)}, u32[]{:S(2)}, u32[]{:S(2)}) %collective-permute-start.1) | collective-permute-done | bytes 131104 | tf_op jit(solution)/shard_map/ppermute | solution.py:317
  14.2 0.0 copy-start
  14.2 1.9 %collective-permute-start.2 = (bf16[32,1152]{1,0:T(8,128)(2,1)S(1)}, bf16[32,1152]{1,0:T(8,128)(2,1)S(1)}, u32[]{:S(2)}, u32[]{:S(2)}) collective-permute-start(bf16[32,1152]{1,0:T(8,128)(2,1)S(1)} %bitcast.28), channel_id=1, source_target_pairs={{0,4},{4,0},{8,12},{12,8},{1,5},{5,1},{9,13},{13,9},{2,6},{6,2},{1... | collective-permute-start | bytes 221192 | tf_op jit(solution)/shard_map/ppermute | solution.py:317
  16.1 2.6 %collective-permute-start.4 = (bf16[32,1152]{1,0:T(8,128)(2,1)S(1)}, bf16[32,1152]{1,0:T(8,128)(2,1)S(1)}, u32[]{:S(2)}, u32[]{:S(2)}) collective-permute-start(bf16[32,1152]{1,0:T(8,128)(2,1)S(1)} %bitcast.29), channel_id=1, source_target_pairs={{0,8},{4,12},{8,0},{12,4},{1,9},{5,13},{9,1},{13,5},{2,10},{6,14},... | collective-permute-start | bytes 221192 | tf_op jit(solution)/shard_map/ppermute | solution.py:317
  18.7 0.0 collective-permute-start.6
  18.7 0.0 collective-permute-done.2.refs_1_
  18.7 2.4 %collective-permute-start.3 = (bf16[32,1152]{1,0:T(8,128)(2,1)S(1)}, bf16[32,1152]{1,0:T(8,128)(2,1)S(1)}, u32[]{:S(2)}, u32[]{:S(2)}) collective-permute-start(bf16[32,1152]{1,0:T(8,128)(2,1)S(1)} %collective-permute-done.2.refs_1_), channel_id=1, source_target_pairs={{0,2},{2,0},{1,3},{3,1},{4,6},{6,4},{5,7},{7,5},{8,10},{10,8},{9,1... | collective-permute-start | bytes 221192 | tf_op jit(solution)/shard_map/ppermute | solution.py:317
  21.1 2.3 %collective-permute-done.4.refs_3_ = bf16[32,1152]{1,0:T(8,128)(2,1)S(1)} collective-permute-done((bf16[32,1152]{1,0:T(8,128)(2,1)S(1)}, bf16[32,1152]{1,0:T(8,128)(2,1)S(1)}, u32[]{:S(2)}, u32[]{:S(2)}) %collective-permute-start.4) | collective-permute-done | bytes 73760 | tf_op jit(solution)/shard_map/ppermute | solution.py:317
  23.4 1.5 %collective-permute-start.5 = (bf16[32,1152]{1,0:T(8,128)(2,1)S(1)}, bf16[32,1152]{1,0:T(8,128)(2,1)S(1)}, u32[]{:S(2)}, u32[]{:S(2)}) collective-permute-start(bf16[32,1152]{1,0:T(8,128)(2,1)S(1)} %collective-permute-done.4.refs_3_), channel_id=1, source_target_pairs={{0,2},{2,0},{1,3},{3,1},{4,6},{6,4},{5,7},{7,5},{8,10},{10,8},{9,1... | collective-permute-start | bytes 221192 | tf_op jit(solution)/shard_map/ppermute | solution.py:317
  24.9 0.1 collective-permute-done.6.refs_5_
  24.9 1.5 %collective-permute-start.7 = (bf16[32,1152]{1,0:T(8,128)(2,1)S(1)}, bf16[32,1152]{1,0:T(8,128)(2,1)S(1)}, u32[]{:S(2)}, u32[]{:S(2)}) collective-permute-start(bf16[32,1152]{1,0:T(8,128)(2,1)S(1)} %collective-permute-done.6.refs_5_), channel_id=1, source_target_pairs={{0,2},{2,0},{1,3},{3,1},{4,6},{6,4},{5,7},{7,5},{8,10},{10,8},{9,1... | collective-permute-start | bytes 221192 | tf_op jit(solution)/shard_map/ppermute | solution.py:317
  26.4 0.0 collective-permute-start.8
  26.4 0.5 collective-permute-start.9
  26.9 0.0 collective-permute-done.3.refs_2_
  26.9 0.0 collective-permute-start.11
  27.0 0.8 %collective-permute-done.5.refs_4_ = bf16[32,1152]{1,0:T(8,128)(2,1)S(1)} collective-permute-done((bf16[32,1152]{1,0:T(8,128)(2,1)S(1)}, bf16[32,1152]{1,0:T(8,128)(2,1)S(1)}, u32[]{:S(2)}, u32[]{:S(2)}) %collective-permute-start.5) | collective-permute-done | bytes 73760 | tf_op jit(solution)/shard_map/ppermute | solution.py:317
  27.7 0.0 collective-permute-start.13
  27.7 1.6 %collective-permute-done.7.refs_6_ = bf16[32,1152]{1,0:T(8,128)(2,1)S(1)} collective-permute-done((bf16[32,1152]{1,0:T(8,128)(2,1)S(1)}, bf16[32,1152]{1,0:T(8,128)(2,1)S(1)}, u32[]{:S(2)}, u32[]{:S(2)}) %collective-permute-start.7) | collective-permute-done | bytes 73760 | tf_op jit(solution)/shard_map/ppermute | solution.py:317
  29.3 0.0 collective-permute-start.10
  29.3 0.0 collective-permute-done.9.refs_8_
  29.3 0.5 collective-permute-start.12
  29.8 0.0 collective-permute-done.11.refs_10_
  29.8 0.1 collective-permute-start.14
  29.9 4.7 %load_weights.1 = (bf16[2,2048,512]{2,1,0:T(8,128)(2,1)S(1)}, bf16[2,2048,512]{2,1,0:T(8,128)(2,1)S(1)}, bf16[2,512,2048]{2,1,0:T(8,128)(2,1)S(1)}) custom-call(bf16[2,2048,512]{2,1,0:T(8,128)(2,1)} %refs_0_, bf16[2,2048,512]{2,1,0:T(8,128)(2,1)} %refs_1_, bf16[2,512,2048]{2,1,0:T(8,128)(2,1)} %refs_2_), custom_call_target="tpu_custom_call" | custom-call | bytes 25165824 | tf_op jit(solution)/shard_map/load_weights/pallas_call | solution.py:242
  34.6 0.0 collective-permute-done.13.refs_12_
  34.6 0.0 collective-permute-done.8.refs_7_
  34.6 0.0 collective-permute-done.10.refs_9_
  34.6 0.0 collective-permute-done.12.refs_11_
  34.6 0.0 collective-permute-done.14.refs_13_
  34.6 0.0 copy-done
  34.6 3.9 %experts.1 = (f32[128,2048]{1,0:T(8,128)S(1)}, bf16[128,2048]{1,0:T(8,128)(2,1)S(1)}) custom-call(bf16[64,1152]{1,0:T(8,128)(2,1)S(1)} %maximum_maximum_fusion.refs_0_, bf16[32,1152]{1,0:T(8,128)(2,1)S(1)} %collective-permute-done.2.refs_1_, bf16[32,1152]{1,0:T(8,128)(2,1)S(1)} %collective-permute-done.3.refs_2_, ...), custom_call_target="tpu_custom_call" | custom-call | tf_op jit(solution)/shard_map/experts/pallas_call | solution.py:301
  38.6 0.0 copy-start.1
  38.6 0.5 collective-permute-start.15
  39.1 1.5 %collective-permute-done.15 = bf16[128,2048]{1,0:T(8,128)(2,1)S(1)} collective-permute-done((bf16[128,2048]{1,0:T(8,128)(2,1)S(1)}, bf16[128,2048]{1,0:T(8,128)(2,1)S(1)}, u32[]{:S(2)}, u32[]{:S(2)}) %collective-permute-start.15) | collective-permute-done | bytes 524320 | tf_op jit(solution)/shard_map/ppermute | solution.py:317
  40.6 0.1 convert_add_fusion
  40.8 1.6 %collective-permute-start.16 = (bf16[4,32,1024]{2,1,0:T(8,128)(2,1)S(1)}, bf16[4,32,1024]{2,1,0:T(8,128)(2,1)S(1)}, u32[]{:S(2)}, u32[]{:S(2)}) collective-permute-start(bf16[4,32,1024]{2,1,0:T(8,128)(2,1)S(1)} %dynamic-slice_convert_fusion), channel_id=1, source_target_pairs={{0,2},{2,0},{1,3},{3,1},{4,6},{6,4},{5,7},{7,5},{8,10},{10,8},{9,1... | collective-permute-start | bytes 786440 | tf_op jit(solution)/shard_map/ppermute | solution.py:317
  42.4 0.1 collective-permute-start.20
  42.5 6.9 %collective-permute-done.16 = bf16[4,32,1024]{2,1,0:T(8,128)(2,1)S(1)} collective-permute-done((bf16[4,32,1024]{2,1,0:T(8,128)(2,1)S(1)}, bf16[4,32,1024]{2,1,0:T(8,128)(2,1)S(1)}, u32[]{:S(2)}, u32[]{:S(2)}) %collective-permute-start.16) | collective-permute-done | bytes 262176 | tf_op jit(solution)/shard_map/ppermute | solution.py:317
  49.4 0.1 fusion.6
  49.6 3.2 %collective-permute-start.19 = (bf16[32,1024]{1,0:T(8,128)(2,1)S(1)}, bf16[32,1024]{1,0:T(8,128)(2,1)S(1)}, u32[]{:S(2)}, u32[]{:S(2)}) collective-permute-start(bf16[32,1024]{1,0:T(8,128)(2,1)S(1)} %get-tuple-element.36), channel_id=1, source_target_pairs={{0,12},{4,8},{8,4},{12,0},{1,13},{5,9},{9,5},{13,1},{2,14},{6,10},... | collective-permute-start | bytes 196616 | tf_op jit(solution)/shard_map/ppermute | solution.py:317
  52.8 0.0 collective-permute-start.18
  52.8 1.2 %collective-permute-start.17 = (bf16[32,1024]{1,0:T(8,128)(2,1)S(1)}, bf16[32,1024]{1,0:T(8,128)(2,1)S(1)}, u32[]{:S(2)}, u32[]{:S(2)}) collective-permute-start(bf16[32,1024]{1,0:T(8,128)(2,1)S(1)} %get-tuple-element.35), channel_id=1, source_target_pairs={{0,4},{4,0},{8,12},{12,8},{1,5},{5,1},{9,13},{13,9},{2,6},{6,2},{1... | collective-permute-start | bytes 196616 | tf_op jit(solution)/shard_map/ppermute | solution.py:317
  54.0 0.0 collective-permute-done.20
  54.0 1.9 %collective-permute-done.19 = bf16[32,1024]{1,0:T(8,128)(2,1)S(1)} collective-permute-done((bf16[32,1024]{1,0:T(8,128)(2,1)S(1)}, bf16[32,1024]{1,0:T(8,128)(2,1)S(1)}, u32[]{:S(2)}, u32[]{:S(2)}) %collective-permute-start.19) | collective-permute-done | bytes 65568 | tf_op jit(solution)/shard_map/ppermute | solution.py:317
  55.9 2.1 %collective-permute-done.18 = bf16[32,1024]{1,0:T(8,128)(2,1)S(1)} collective-permute-done((bf16[32,1024]{1,0:T(8,128)(2,1)S(1)}, bf16[32,1024]{1,0:T(8,128)(2,1)S(1)}, u32[]{:S(2)}, u32[]{:S(2)}) %collective-permute-start.18) | collective-permute-done | bytes 65568 | tf_op jit(solution)/shard_map/ppermute | solution.py:317
  58.0 0.4 collective-permute-done.17
  58.5 0.0 copy-done.1
  58.5 0.7 %fusion.2 = bf16[32,1024]{1,0:T(8,128)(2,1)} fusion(f32[64,1024]{1,0:T(8,128)S(1)} %get-tuple-element.34, f32[4,32,1024]{2,1,0:T(8,128)S(1)} %get-tuple-element.32, bf16[32,1024]{1,0:T(8,128)(2,1)S(1)} %collective-permute-done.20, bf16[32,1024]{1,0:T(8,128)(2,1)S(1)} %collective-permute-done.19, bf16[32,1024]{1,0:T(8,128)(2,1)S(1)} %collective-permute-done.18, ...), kind=kLoop, calls=%fused_computation.10 | loop fusion | flops 393216 | bytes 655365 | tf_op jit(solution)/shard_map/convert_element_type | solution.py:403
  (9 shorter events, 0.1 us)
Async XLA Ops:
  4.9 1.6 %collective-permute-start = (bf16[32,3200]{1,0:T(8,128)(2,1)S(1)}, bf16[32,3200]{1,0:T(8,128)(2,1)S(1)}, u32[]{:S(2)}, u32[]{:S(2)}) collective-permute-start(bf16[32,3200]{1,0:T(8,128)(2,1)S(1)} %get-tuple-element.18.packed_ref), channel_id=1, source_target_pairs={{0,1},{1,0},{2,3},{3,2},{4,5},{5,4},{6,7},{7,6},{8,9},{9,8},{10,11... | collective-permute-start | bytes 614408 | tf_op jit(solution)/shard_map/ppermute | solution.py:317
  7.4 6.7 %collective-permute-start.1 = (bf16[64,1024]{1,0:T(8,128)(2,1)S(1)}, bf16[64,1024]{1,0:T(8,128)(2,1)S(1)}, u32[]{:S(2)}, u32[]{:S(2)}) collective-permute-start(bf16[64,1024]{1,0:T(8,128)(2,1)S(1)} %get-tuple-element.21), channel_id=1, source_target_pairs={{0,2},{2,0},{1,3},{3,1},{4,6},{6,4},{5,7},{7,5},{8,10},{10,8},{9,1... | collective-permute-start | bytes 393224 | tf_op jit(solution)/shard_map/ppermute | solution.py:317
  14.2 20.4 %copy-start = (f32[2048]{0:T(1024)S(1)}, f32[2048]{0:T(1024)}, u32[]{:S(2)}) copy-start(f32[2048]{0:T(1024)} %param.22) | copy-start | bytes 24580
  14.2 4.5 %collective-permute-start.2 = (bf16[32,1152]{1,0:T(8,128)(2,1)S(1)}, bf16[32,1152]{1,0:T(8,128)(2,1)S(1)}, u32[]{:S(2)}, u32[]{:S(2)}) collective-permute-start(bf16[32,1152]{1,0:T(8,128)(2,1)S(1)} %bitcast.28), channel_id=1, source_target_pairs={{0,4},{4,0},{8,12},{12,8},{1,5},{5,1},{9,13},{13,9},{2,6},{6,2},{1... | collective-permute-start | bytes 221192 | tf_op jit(solution)/shard_map/ppermute | solution.py:317
  16.1 7.3 %collective-permute-start.4 = (bf16[32,1152]{1,0:T(8,128)(2,1)S(1)}, bf16[32,1152]{1,0:T(8,128)(2,1)S(1)}, u32[]{:S(2)}, u32[]{:S(2)}) collective-permute-start(bf16[32,1152]{1,0:T(8,128)(2,1)S(1)} %bitcast.29), channel_id=1, source_target_pairs={{0,8},{4,12},{8,0},{12,4},{1,9},{5,13},{9,1},{13,5},{2,10},{6,14},... | collective-permute-start | bytes 221192 | tf_op jit(solution)/shard_map/ppermute | solution.py:317
  18.7 6.2 %collective-permute-start.6 = (bf16[32,1152]{1,0:T(8,128)(2,1)S(1)}, bf16[32,1152]{1,0:T(8,128)(2,1)S(1)}, u32[]{:S(2)}, u32[]{:S(2)}) collective-permute-start(bf16[32,1152]{1,0:T(8,128)(2,1)S(1)} %bitcast.30), channel_id=1, source_target_pairs={{0,12},{4,8},{8,4},{12,0},{1,13},{5,9},{9,5},{13,1},{2,14},{6,10},... | collective-permute-start | bytes 221192 | tf_op jit(solution)/shard_map/ppermute | solution.py:317
  18.7 8.2 %collective-permute-start.3 = (bf16[32,1152]{1,0:T(8,128)(2,1)S(1)}, bf16[32,1152]{1,0:T(8,128)(2,1)S(1)}, u32[]{:S(2)}, u32[]{:S(2)}) collective-permute-start(bf16[32,1152]{1,0:T(8,128)(2,1)S(1)} %collective-permute-done.2.refs_1_), channel_id=1, source_target_pairs={{0,2},{2,0},{1,3},{3,1},{4,6},{6,4},{5,7},{7,5},{8,10},{10,8},{9,1... | collective-permute-start | bytes 221192 | tf_op jit(solution)/shard_map/ppermute | solution.py:317
  23.4 4.4 %collective-permute-start.5 = (bf16[32,1152]{1,0:T(8,128)(2,1)S(1)}, bf16[32,1152]{1,0:T(8,128)(2,1)S(1)}, u32[]{:S(2)}, u32[]{:S(2)}) collective-permute-start(bf16[32,1152]{1,0:T(8,128)(2,1)S(1)} %collective-permute-done.4.refs_3_), channel_id=1, source_target_pairs={{0,2},{2,0},{1,3},{3,1},{4,6},{6,4},{5,7},{7,5},{8,10},{10,8},{9,1... | collective-permute-start | bytes 221192 | tf_op jit(solution)/shard_map/ppermute | solution.py:317
  24.9 4.4 %collective-permute-start.7 = (bf16[32,1152]{1,0:T(8,128)(2,1)S(1)}, bf16[32,1152]{1,0:T(8,128)(2,1)S(1)}, u32[]{:S(2)}, u32[]{:S(2)}) collective-permute-start(bf16[32,1152]{1,0:T(8,128)(2,1)S(1)} %collective-permute-done.6.refs_5_), channel_id=1, source_target_pairs={{0,2},{2,0},{1,3},{3,1},{4,6},{6,4},{5,7},{7,5},{8,10},{10,8},{9,1... | collective-permute-start | bytes 221192 | tf_op jit(solution)/shard_map/ppermute | solution.py:317
  26.4 8.2 %collective-permute-start.8 = (bf16[64,1152]{1,0:T(8,128)(2,1)S(1)}, bf16[64,1152]{1,0:T(8,128)(2,1)S(1)}, u32[]{:S(2)}, u32[]{:S(2)}) collective-permute-start(bf16[64,1152]{1,0:T(8,128)(2,1)S(1)} %maximum_maximum_fusion.refs_0_), channel_id=1, source_target_pairs={{0,1},{1,0},{2,3},{3,2},{4,5},{5,4},{6,7},{7,6},{8,9},{9,8},{10,11... | collective-permute-start | bytes 442376 | tf_op jit(solution)/shard_map/ppermute | solution.py:317
  26.4 2.9 %collective-permute-start.9 = (bf16[32,1152]{1,0:T(8,128)(2,1)S(1)}, bf16[32,1152]{1,0:T(8,128)(2,1)S(1)}, u32[]{:S(2)}, u32[]{:S(2)}) collective-permute-start(bf16[32,1152]{1,0:T(8,128)(2,1)S(1)} %collective-permute-done.2.refs_1_), channel_id=1, source_target_pairs={{0,1},{1,0},{2,3},{3,2},{4,5},{5,4},{6,7},{7,6},{8,9},{9,8},{10,11... | collective-permute-start | bytes 221192 | tf_op jit(solution)/shard_map/ppermute | solution.py:317
  26.9 2.9 %collective-permute-start.11 = (bf16[32,1152]{1,0:T(8,128)(2,1)S(1)}, bf16[32,1152]{1,0:T(8,128)(2,1)S(1)}, u32[]{:S(2)}, u32[]{:S(2)}) collective-permute-start(bf16[32,1152]{1,0:T(8,128)(2,1)S(1)} %collective-permute-done.4.refs_3_), channel_id=1, source_target_pairs={{0,1},{1,0},{2,3},{3,2},{4,5},{5,4},{6,7},{7,6},{8,9},{9,8},{10,11... | collective-permute-start | bytes 221192 | tf_op jit(solution)/shard_map/ppermute | solution.py:317
  27.7 6.9 %collective-permute-start.13 = (bf16[32,1152]{1,0:T(8,128)(2,1)S(1)}, bf16[32,1152]{1,0:T(8,128)(2,1)S(1)}, u32[]{:S(2)}, u32[]{:S(2)}) collective-permute-start(bf16[32,1152]{1,0:T(8,128)(2,1)S(1)} %collective-permute-done.6.refs_5_), channel_id=1, source_target_pairs={{0,1},{1,0},{2,3},{3,2},{4,5},{5,4},{6,7},{7,6},{8,9},{9,8},{10,11... | collective-permute-start | bytes 221192 | tf_op jit(solution)/shard_map/ppermute | solution.py:317
  29.3 5.3 %collective-permute-start.10 = (bf16[32,1152]{1,0:T(8,128)(2,1)S(1)}, bf16[32,1152]{1,0:T(8,128)(2,1)S(1)}, u32[]{:S(2)}, u32[]{:S(2)}) collective-permute-start(bf16[32,1152]{1,0:T(8,128)(2,1)S(1)} %collective-permute-done.3.refs_2_), channel_id=1, source_target_pairs={{0,1},{1,0},{2,3},{3,2},{4,5},{5,4},{6,7},{7,6},{8,9},{9,8},{10,11... | collective-permute-start | bytes 221192 | tf_op jit(solution)/shard_map/ppermute | solution.py:317
  29.3 5.3 %collective-permute-start.12 = (bf16[32,1152]{1,0:T(8,128)(2,1)S(1)}, bf16[32,1152]{1,0:T(8,128)(2,1)S(1)}, u32[]{:S(2)}, u32[]{:S(2)}) collective-permute-start(bf16[32,1152]{1,0:T(8,128)(2,1)S(1)} %collective-permute-done.5.refs_4_), channel_id=1, source_target_pairs={{0,1},{1,0},{2,3},{3,2},{4,5},{5,4},{6,7},{7,6},{8,9},{9,8},{10,11... | collective-permute-start | bytes 221192 | tf_op jit(solution)/shard_map/ppermute | solution.py:317
  29.8 4.8 %collective-permute-start.14 = (bf16[32,1152]{1,0:T(8,128)(2,1)S(1)}, bf16[32,1152]{1,0:T(8,128)(2,1)S(1)}, u32[]{:S(2)}, u32[]{:S(2)}) collective-permute-start(bf16[32,1152]{1,0:T(8,128)(2,1)S(1)} %collective-permute-done.7.refs_6_), channel_id=1, source_target_pairs={{0,1},{1,0},{2,3},{3,2},{4,5},{5,4},{6,7},{7,6},{8,9},{9,8},{10,11... | collective-permute-start | bytes 221192 | tf_op jit(solution)/shard_map/ppermute | solution.py:317
  38.6 19.9 %copy-start.1 = (bf16[32,2048]{1,0:T(8,128)(2,1)S(1)}, bf16[32,2048]{1,0:T(8,128)(2,1)}, u32[]{:S(2)}) copy-start(bf16[32,2048]{1,0:T(8,128)(2,1)} %residual_hbm.1) | copy-start | bytes 393220
  38.6 2.0 %collective-permute-start.15 = (bf16[128,2048]{1,0:T(8,128)(2,1)S(1)}, bf16[128,2048]{1,0:T(8,128)(2,1)S(1)}, u32[]{:S(2)}, u32[]{:S(2)}) collective-permute-start(bf16[128,2048]{1,0:T(8,128)(2,1)S(1)} %get-tuple-element.30), channel_id=1, source_target_pairs={{0,1},{1,0},{2,3},{3,2},{4,5},{5,4},{6,7},{7,6},{8,9},{9,8},{10,11... | collective-permute-start | bytes 1572872 | tf_op jit(solution)/shard_map/ppermute | solution.py:317
  40.8 8.7 %collective-permute-start.16 = (bf16[4,32,1024]{2,1,0:T(8,128)(2,1)S(1)}, bf16[4,32,1024]{2,1,0:T(8,128)(2,1)S(1)}, u32[]{:S(2)}, u32[]{:S(2)}) collective-permute-start(bf16[4,32,1024]{2,1,0:T(8,128)(2,1)S(1)} %dynamic-slice_convert_fusion), channel_id=1, source_target_pairs={{0,2},{2,0},{1,3},{3,1},{4,6},{6,4},{5,7},{7,5},{8,10},{10,8},{9,1... | collective-permute-start | bytes 786440 | tf_op jit(solution)/shard_map/ppermute | solution.py:317
  42.4 11.6 %collective-permute-start.20 = (bf16[32,1024]{1,0:T(8,128)(2,1)S(1)}, bf16[32,1024]{1,0:T(8,128)(2,1)S(1)}, u32[]{:S(2)}, u32[]{:S(2)}) collective-permute-start(bf16[32,1024]{1,0:T(8,128)(2,1)S(1)} %slice.68), channel_id=1, source_target_pairs={{0,1},{1,0},{2,3},{3,2},{4,5},{5,4},{6,7},{7,6},{8,9},{9,8},{10,11... | collective-permute-start | bytes 196616 | tf_op jit(solution)/shard_map/ppermute | solution.py:317
  49.6 6.3 %collective-permute-start.19 = (bf16[32,1024]{1,0:T(8,128)(2,1)S(1)}, bf16[32,1024]{1,0:T(8,128)(2,1)S(1)}, u32[]{:S(2)}, u32[]{:S(2)}) collective-permute-start(bf16[32,1024]{1,0:T(8,128)(2,1)S(1)} %get-tuple-element.36), channel_id=1, source_target_pairs={{0,12},{4,8},{8,4},{12,0},{1,13},{5,9},{9,5},{13,1},{2,14},{6,10},... | collective-permute-start | bytes 196616 | tf_op jit(solution)/shard_map/ppermute | solution.py:317
  52.8 5.2 %collective-permute-start.18 = (bf16[32,1024]{1,0:T(8,128)(2,1)S(1)}, bf16[32,1024]{1,0:T(8,128)(2,1)S(1)}, u32[]{:S(2)}, u32[]{:S(2)}) collective-permute-start(bf16[32,1024]{1,0:T(8,128)(2,1)S(1)} %get-tuple-element.37), channel_id=1, source_target_pairs={{0,8},{4,12},{8,0},{12,4},{1,9},{5,13},{9,1},{13,5},{2,10},{6,14},... | collective-permute-start | bytes 196616 | tf_op jit(solution)/shard_map/ppermute | solution.py:317
  52.8 5.7 %collective-permute-start.17 = (bf16[32,1024]{1,0:T(8,128)(2,1)S(1)}, bf16[32,1024]{1,0:T(8,128)(2,1)S(1)}, u32[]{:S(2)}, u32[]{:S(2)}) collective-permute-start(bf16[32,1024]{1,0:T(8,128)(2,1)S(1)} %get-tuple-element.35), channel_id=1, source_target_pairs={{0,4},{4,0},{8,12},{12,8},{1,5},{5,1},{9,13},{13,9},{2,6},{6,2},{1... | collective-permute-start | bytes 196616 | tf_op jit(solution)/shard_map/ppermute | solution.py:317

commit v3 on v2

--- a/solution.py
+++ b/solution.py
@@ -152,6 +152,7 @@
     return pltpu.with_memory_space_constraint(array, pltpu.VMEM)
 
 
+FREE = pl.CostEstimate(flops=0, bytes_accessed=0, transcendentals=0)
 ANYWHERE = pl.BlockSpec(memory_space=pl.ANY)
 WHOLE = pl.BlockSpec(memory_space=pltpu.VMEM)
 
@@ -203,27 +204,52 @@
             pltpu.SemaphoreType.DMA,
         ],
         compiler_params=pltpu.CompilerParams(vmem_limit_bytes=24 * MIB),
+        cost_estimate=FREE,
         name="attention",
     )(*map(in_hbm, arrays))
 
 
-def project_kernel(width, packed_ref, other_ref, weight_ref, terms_ref, sent_ref):
+def project_kernel(
+    packed_ref, other_ref, base_ref, weight_ref, send_first, send_last, keep_first, keep_last,
+    table_first, table_last, terms_ref
+):
+    rows, half = base_ref.shape
+    width = weight_ref.shape[0]
+    part = rows // 2
+    tp_index = lax.axis_index("tp")
     both = jnp.concatenate([packed_ref[:, :width], other_ref[:, :width]], axis=0)
-    terms = jnp.dot(both, weight_ref[...], preferred_element_type=f32)
-    terms_ref[...] = terms
-    sent_ref[...] = terms.astype(bf16)
-
-
-def project(packed, packed_other, weight):
-    shape = (2 * packed.shape[0], weight.shape[1])
-    return pl.pallas_call(
-        functools.partial(project_kernel, weight.shape[0]),
-        in_specs=[WHOLE] * 3,
-        out_specs=[WHOLE] * 2,
-        out_shape=[pltpu.VMEM(shape, f32), pltpu.VMEM(shape, bf16)],
+    terms_ref[...] = jnp.dot(both, weight_ref[...], preferred_element_type=f32)
+    for block, send_ref, keep_ref, table_ref in (
+        (tp_index, send_last, keep_first, table_first),
+        (1 - tp_index, send_first, keep_last, table_last),
+    ):
+        own = pl.ds(pl.multiple_of(block * part, part), part)
+        for i, residual in enumerate((base_ref[own, :], other_ref[own, width : width + half])):
+            to = slice(i * part, (i + 1) * part)
+            terms = terms_ref[pl.ds(pl.multiple_of(i * rows + block * part, part), part), :]
+            send_ref[to, :] = terms.astype(bf16)
+            keep_ref[to, :] = terms + residual.astype(f32)
+        table_ref[:part, :] = packed_ref[own, width + half :]
+        table_ref[part:, :] = other_ref[own, width + half :]
+
+
+def project(packed, packed_other, base, weight):
+    shape = base.shape
+    table = (shape[0], packed.shape[1] - weight.shape[0] - shape[1])
+    return pl.pallas_call(
+        project_kernel,
+        in_specs=[WHOLE] * 4,
+        out_specs=[WHOLE] * 6,
+        out_shape=[
+            *[pltpu.VMEM(shape, bf16)] * 2,
+            *[pltpu.VMEM(shape, f32)] * 2,
+            *[pltpu.VMEM(table, bf16)] * 2,
+        ],
+        scratch_shapes=[pltpu.VMEM((2 * shape[0], shape[1]), f32)],
         compiler_params=pltpu.CompilerParams(vmem_limit_bytes=8 * MIB),
+        cost_estimate=FREE,
         name="project",
-    )(in_vmem(packed), in_vmem(packed_other), in_vmem(weight))
+    )(*map(in_vmem, (packed, packed_other, base, weight)))
 
 
 def load_kernel(*refs):
@@ -247,35 +273,145 @@
         scratch_shapes=[pltpu.SemaphoreType.DMA((len(arrays),))],
         compiler_params=pltpu.CompilerParams(vmem_limit_bytes=16 * MIB),
         cost_estimate=pl.CostEstimate(
-            flops=0, bytes_accessed=2 * sum(array.nbytes for array in arrays), transcendentals=0
+            flops=0, bytes_accessed=0, transcendentals=0
         ),
         name="load_weights",
     )(*map(in_hbm, arrays))
 
 
-def experts_kernel(experts, first_of, places, *refs):
+def experts_kernel(experts, first_of, places, streams, loads, *refs):
     count = len(places)
     mine, other = refs[:count], refs[count : 2 * count]
-    gain_ref, gate_ref, up_ref, down_ref, keep_ref, send_ref, rows_ref, table_ref = refs[2 * count :]
+    gain_ref, gate_ref, up_ref, down_ref, keep_ref, send_ref, *refs = refs[2 * count :]
+    stream_ref = refs.pop(0) if streams else None
+    if loads:
+        down_hbm, down_ref, rows_ref, table_ref, sem = down_ref, *refs
+        down_copy = pltpu.make_async_copy(down_hbm, down_ref, sem)
+        down_copy.start()
+    else:
+        rows_ref, table_ref = refs
     half = rows_ref.shape[1] // 2
     rows = rows_ref.shape[0]
     sp_index = lax.axis_index("sp")
     tp_index = lax.axis_index("tp")
     my_cols = pl.ds(pl.multiple_of(sp_index * half, LANES), half)
     other_cols = pl.ds(pl.multiple_of((1 - sp_index) * half, LANES), half)
-    for a, b, (start, step, flip) in zip(mine, other, places):
-        m = a.shape[0] // 2
-        at = start if flip is None else pl.multiple_of(start + (tp_index ^ flip) * step, step)
-        first, second = pl.ds(at, m), pl.ds(rows // 2 + at, m)
-        rows_ref[first, my_cols] = a[:m, :half]
-        rows_ref[second, my_cols] = a[m:, :half]
-        rows_ref[first, other_cols] = b[m:, :half]
-        rows_ref[second, other_cols] = b[:m, :half]
-        table_ref[first, :] = a[:m, half:].astype(f32)
-        table_ref[second, :] = a[m:, half:].astype(f32)
+    for a, b, segments in zip(mine, other, places):
+        for source, m, start, flip in segments:
+            at = start if flip is None else pl.multiple_of(start + (tp_index ^ flip) * m, m)
+            own, others = pl.ds(at, m), pl.ds(rows // 2 + at, m)
+            upper, lower = slice(source, source + m), slice(source + m, source + 2 * m)
+            rows_ref[own, my_cols] = a[upper, :half]
+            rows_ref[others, my_cols] = a[lower, :half]
+            rows_ref[own, other_cols] = b[lower, :half]
+            rows_ref[others, other_cols] = b[upper, :half]
+            table_ref[own, :] = a[upper, half:].astype(f32)
+            table_ref[others, :] = a[lower, half:].astype(f32)
+    if streams:
+        count, width = stream_ref.shape
+        out_cols = pl.ds(pl.multiple_of(tp_index * width, LANES), width)
+        stream_ref[...] = rows_ref[:count, out_cols]
     values = rows_ref[...].astype(f32)
     inverse = lax.rsqrt(jnp.mean(values * values, axis=1, keepdims=True) + norm_epsilon)
     rows_ref[...] = (values * inverse * gain_ref[...]).astype(bf16)
+    first_expert = first_of(lax.axis_index("ep"), sp_index)
+    table = table_ref[...]
+    lane = lax.broadcasted_iota(jnp.int32, table.shape, 1)
+    hidden = []
+    for e in range(gate_ref.shape[0]):
+        wanted = (lane == first_expert + e) | (lane == first_expert + e + experts)
+        scale = jnp.sum(jnp.where(wanted, table, 0.0), axis=1, keepdims=True)
+        normed = rows_ref[...]
+        gate = jnp.dot(normed, gate_ref[e], preferred_element_type=f32)
+        up = jnp.dot(normed, up_ref[e], preferred_element_type=f32)
+        hidden.append((gate / (1.0 + jnp.exp(-gate)) * up * scale).astype(bf16))
+    if loads:
+        down_copy.wait()
+    total = None
+    for e, acts in enumerate(hidden):
+        term = jnp.dot(acts, down_ref[e], preferred_element_type=f32)
+        total = term if total is None else total + term
+    keep_ref[...] = total[: rows // 2]
+    send_ref[...] = total[rows // 2 :].astype(bf16)
+
+
+def run_experts(mine, other, places, gain, gate, up, down, experts, n_sp, stream_shape, loads):
+    rows = sum(array.shape[0] for array in mine)
+    width = gain.shape[0]
+    local = gate.shape[0]
+    arrays = [*mine, *other, gain.reshape(1, width), gate, up, down]
+    extra = [pltpu.VMEM(stream_shape, bf16)] if stream_shape else []
+    if loads:
+        extra.append(pltpu.VMEM(down.shape, bf16))
+    return pl.pallas_call(
+        functools.partial(
+            experts_kernel, experts, lambda e, s: (e * n_sp + s) * local, places, stream_shape is not None, loads
+        ),
+        in_specs=[WHOLE] * (len(arrays) - 1) + [ANYWHERE if loads else WHOLE],
+        out_specs=[WHOLE] * (2 + len(extra)),
+        out_shape=[
+            pltpu.VMEM((rows // 2, width), f32),
+            pltpu.VMEM((rows // 2, width), bf16),
+            *extra,
+        ],
+        scratch_shapes=[
+            pltpu.VMEM((rows, width), bf16),
+            pltpu.VMEM((rows, mine[0].shape[1] - width // 2), f32),
+        ]
+        + ([pltpu.SemaphoreType.DMA] if loads else []),
+        compiler_params=pltpu.CompilerParams(vmem_limit_bytes=(12 if rows <= 256 else 48) * MIB),
+        cost_estimate=pl.CostEstimate(
+            flops=0, bytes_accessed=0, transcendentals=0
+        ),
+        name="experts",
+    )(
+        *[array if array.shape[0] == 1 else in_vmem(array) for array in arrays[:-1]],
+        in_hbm(down) if loads else in_vmem(down),
+    )
+
+
+def place_rows(source_ref, target_ref, segments, first, columns, table_ref=None):
+    half, rows = columns.size, target_ref.shape[0]
+    for source, m, start, flip in segments:
+        at = pl.multiple_of(start + (lax.axis_index("tp") ^ flip) * m, m)
+        own, others = pl.ds(at, m), pl.ds(rows // 2 + at, m)
+        upper, lower = slice(source, source + m), slice(source + m, source + 2 * m)
+        for to, at in ((own, upper), (others, lower)) if first else ((own, lower), (others, upper)):
+            target_ref[to, columns] = source_ref[at, :half]
+            if table_ref is not None:
+                table_ref[to, :] = source_ref[at, half:].astype(f32)
+
+
+def start_kernel(segments, mine_ref, gain_ref, gate_ref, up_ref, partial_ref, rows_ref):
+    half, hidden = rows_ref.shape[1], gate_ref.shape[2]
+    place_rows(mine_ref, rows_ref, segments, True, pl.ds(0, half))
+    at = pl.ds(pl.multiple_of(lax.axis_index("sp") * half, LANES), half)
+    scaled = (rows_ref[...].astype(f32) * gain_ref[:, at]).astype(bf16)
+    for e in range(gate_ref.shape[0]):
+        for i, weight_ref in enumerate((gate_ref, up_ref)):
+            to = slice((2 * e + i) * hidden, (2 * e + i + 1) * hidden)
+            partial_ref[:, to] = jnp.dot(scaled, weight_ref[e, at, :], preferred_element_type=f32)
+
+
+def finish_kernel(
+    experts, first_of, segments, window, mine_ref, other_ref, partial_ref, gain_ref, gate_ref,
+    up_ref, down_ref, keep_ref, send_ref, *refs
+):
+    *stream_ref, rows_ref, table_ref = refs
+    rows, width = rows_ref.shape
+    half, hidden = width // 2, gate_ref.shape[2]
+    sp_index = lax.axis_index("sp")
+    my_cols = pl.ds(pl.multiple_of(sp_index * half, LANES), half)
+    other_cols = pl.ds(pl.multiple_of((1 - sp_index) * half, LANES), half)
+    place_rows(mine_ref, rows_ref, segments, True, my_cols, table_ref)
+    place_rows(other_ref, rows_ref, segments, False, other_cols)
+    for out_ref in stream_ref:
+        count, cut = out_ref.shape
+        at = pl.ds(pl.multiple_of(lax.axis_index("tp") * cut, LANES), cut)
+        out_ref[...] = rows_ref[:count, at]
+    values = rows_ref[...].astype(f32)
+    inverse = lax.rsqrt(jnp.mean(values * values, axis=1, keepdims=True) + norm_epsilon)
+    scaled = (rows_ref[:, other_cols].astype(f32) * gain_ref[:, other_cols]).astype(bf16)
     first_expert = first_of(lax.axis_index("ep"), sp_index)
     table = table_ref[...]
     lane = lax.broadcasted_iota(jnp.int32, table.shape, 1)
@@ -283,33 +419,109 @@
     for e in range(gate_ref.shape[0]):
         wanted = (lane == first_expert + e) | (lane == first_expert + e + experts)
         scale = jnp.sum(jnp.where(wanted, table, 0.0), axis=1, keepdims=True)
-        normed = rows_ref[...]
-        gate = jnp.dot(normed, gate_ref[e], preferred_element_type=f32)
-        up = jnp.dot(normed, up_ref[e], preferred_element_type=f32)
-        hidden = (gate / (1.0 + jnp.exp(-gate)) * up * scale).astype(bf16)
-        term = jnp.dot(hidden, down_ref[e], preferred_element_type=f32)
+        sums = []
+        for i, weight_ref in enumerate((gate_ref, up_ref)):
+            at = slice((2 * e + i) * hidden, (2 * e + i + 1) * hidden)
+            begun = jnp.concatenate(
+                [
+                    partial_ref[start + window : start + window + rows // 2, at]
+                    for start in (0, partial_ref.shape[0] // 2)
+                ],
+                axis=0,
+            )
+            rest = jnp.dot(scaled, weight_ref[e, other_cols, :], preferred_element_type=f32)
+            sums.append((begun + rest) * inverse)
+        gate, up = sums
+        acts = (gate / (1.0 + jnp.exp(-gate)) * up * scale).astype(bf16)
+        term = jnp.dot(acts, down_ref[e], preferred_element_type=f32)
         total = term if total is None else total + term
     keep_ref[...] = total[: rows // 2]
     send_ref[...] = total[rows // 2 :].astype(bf16)
 
 
-def run_experts(mine, other, places, gain, gate, up, down, experts, n_sp):
-    rows = sum(array.shape[0] for array in mine)
-    width = gain.shape[0]
-    local = gate.shape[0]
-    arrays = [*mine, *other, gain.reshape(1, width), gate, up, down]
-    return pl.pallas_call(
-        functools.partial(experts_kernel, experts, lambda e, s: (e * n_sp + s) * local, places),
-        in_specs=[WHOLE] * len(arrays),
+def start_experts(mine, segments, gain, gate, up):
+    rows = mine.shape[0]
+    return pl.pallas_call(
+        functools.partial(start_kernel, segments),
+        in_specs=[WHOLE] * 4,
+        out_specs=WHOLE,
+        out_shape=pltpu.VMEM((rows, 2 * gate.shape[0] * gate.shape[2]), f32),
+        scratch_shapes=[pltpu.VMEM((rows, gain.shape[1] // 2), bf16)],
+        compiler_params=pltpu.CompilerParams(vmem_limit_bytes=12 * MIB),
+        cost_estimate=FREE,
+        name="start_experts",
+    )(in_vmem(mine), gain, in_vmem(gate), in_vmem(up))
+
+
+def finish_experts(
+    mine, other, partial, segments, window, count, gain, gate, up, down, experts, n_sp, stream_shape
+):
+    width, local = gain.shape[1], gate.shape[0]
+    segments = tuple(
+        (source, m, start - window, flip)
+        for source, m, start, flip in segments
+        if window <= start < window + count
+    )
+    return pl.pallas_call(
+        functools.partial(
+            finish_kernel, experts, lambda e, s: (e * n_sp + s) * local, segments, window
+        ),
+        in_specs=[WHOLE] * 7,
+        out_specs=[WHOLE] * (3 if stream_shape else 2),
+        out_shape=[
+            pltpu.VMEM((count, width), f32),
+            pltpu.VMEM((count, width), bf16),
+            *([pltpu.VMEM(stream_shape, bf16)] if stream_shape else []),
+        ],
+        scratch_shapes=[
+            pltpu.VMEM((2 * count, width), bf16),
+            pltpu.VMEM((2 * count, mine.shape[1] - width // 2), f32),
+        ],
+        compiler_params=pltpu.CompilerParams(vmem_limit_bytes=12 * MIB),
+        cost_estimate=FREE,
+        name="finish_experts",
+    )(in_vmem(mine), in_vmem(other), in_vmem(partial), gain, *map(in_vmem, (gate, up, down)))
+
+
+def split_kernel(keep, back, keep_ref, send_ref):
+    tp_index = lax.axis_index("tp")
+    width = keep_ref.shape[1]
+    mine = pl.ds(pl.multiple_of(tp_index * width, LANES), width)
+    theirs = pl.ds(pl.multiple_of((1 - tp_index) * width, LANES), width)
+    keep_ref[...] = keep[:, mine] + back[:, mine].astype(f32)
+    send_ref[...] = (keep[:, theirs] + back[:, theirs].astype(f32)).astype(bf16)
+
+
+def split(keep, back):
+    shape = (keep.shape[0], keep.shape[1] // 2)
+    return pl.pallas_call(
+        split_kernel,
+        in_specs=[WHOLE] * 2,
         out_specs=[WHOLE] * 2,
-        out_shape=[pltpu.VMEM((rows // 2, width), f32), pltpu.VMEM((rows // 2, width), bf16)],
-        scratch_shapes=[
-            pltpu.VMEM((rows, width), bf16),
-            pltpu.VMEM((rows, mine[0].shape[1] - width // 2), f32),
-        ],
-        compiler_params=pltpu.CompilerParams(vmem_limit_bytes=(24 if rows <= 256 else 48) * MIB),
-        name="experts",
-    )(*[array if array.shape[0] == 1 else in_vmem(array) for array in arrays])
+        out_shape=[pltpu.VMEM(shape, f32), pltpu.VMEM(shape, bf16)],
+        compiler_params=pltpu.CompilerParams(vmem_limit_bytes=8 * MIB),
+        cost_estimate=FREE,
+        name="split",
+    )(in_vmem(keep), in_vmem(back))
+
+
+def part_kernel(keep, back, keep_ref, send_ref):
+    rows = keep_ref.shape[0]
+    keep_ref[...] = keep[:rows, :] + back[:rows, :].astype(f32)
+    send_ref[...] = (keep[rows:, :] + back[rows:, :].astype(f32)).astype(bf16)
+
+
+def part_near(keep, back):
+    shape = (keep.shape[0] // 2, keep.shape[1])
+    return pl.pallas_call(
+        part_kernel,
+        in_specs=[WHOLE] * 2,
+        out_specs=[WHOLE] * 2,
+        out_shape=[pltpu.VMEM(shape, f32), pltpu.VMEM(shape, bf16)],
+        compiler_params=pltpu.CompilerParams(vmem_limit_bytes=8 * MIB),
+        cost_estimate=FREE,
+        name="part_near",
+    )(in_vmem(keep), in_vmem(back))
 
 
 def swap(array, axis, by=1):
@@ -336,7 +548,7 @@
     rows = query.shape[0]
     width = residual.shape[1]
     n_ep, n_tp, n_sp = lax.axis_size("ep"), lax.axis_size("tp"), lax.axis_size("sp")
-    tp_index, sp_index = lax.axis_index("tp"), lax.axis_index("sp")
+    tp_index = lax.axis_index("tp")
     experts = w_gate.shape[0] * n_ep * n_sp
     half = width // n_sp
     part = rows // n_tp
@@ -348,59 +560,101 @@
         gate_weights, out_weight, experts, n_sp
     )
     packed_other = swap(packed, "sp")
-    terms, sent = project(packed, packed_other, weight)
-    totals = terms
+    stream_shape = (rows, out_width)
+    if (n_ep, n_tp) == (4, 2) and part % 16 == 0:
+        send_first, send_last, keep_first, keep_last, table_first, table_last = project(
+            packed, packed_other, base, weight
+        )
+        first, last = swap(send_first, "tp"), swap(send_last, "tp")
+        w_gate, _ = lax.optimization_barrier((w_gate, send_first))
+        (w_gate,) = load(w_gate)
+        first, w_gate = lax.optimization_barrier((first, w_gate))
+        piece = jnp.concatenate([(keep_first + first.astype(f32)).astype(bf16), table_first], axis=1)
+        second, third = swap(piece, "ep", 2), swap(piece, "ep", 3)
+        piece_far = jnp.concatenate([(keep_last + last.astype(f32)).astype(bf16), table_last], axis=1)
+        chip = jnp.concatenate([piece, piece_far], axis=0)
+        next_chip = swap(chip, "ep", 1)
+        w_up, _ = lax.optimization_barrier((w_up, chip))
+        (w_up,) = load(w_up)
+        second, third, w_up = lax.optimization_barrier((second, third, w_up))
+        parts = jnp.concatenate([second, third], axis=0)
+        far = swap(parts, "tp")
+        w_down, _ = lax.optimization_barrier((w_down, parts))
+        (w_down,) = load(w_down)
+        far, next_chip, w_down = lax.optimization_barrier((far, next_chip, w_down))
+        mine = jnp.concatenate([chip, next_chip, parts, far], axis=0)
+        other = swap(mine, "sp")
+        size = 2 * part
+        segments = tuple(
+            (i * size, part, k * rows, flip)
+            for i, (k, flip) in enumerate(
+                [(0, 0), (0, 1), (1, 0), (1, 1), (2, 0), (3, 0), (2, 1), (3, 1)]
+            )
+        )
+        gain = norm_gain.reshape(1, width)
+        partial = start_experts(mine, segments, gain, w_gate, w_up)
+        keep, send = finish_experts(
+            mine, other, partial, segments, 2 * rows, 2 * rows, gain, w_gate, w_up, w_down,
+            experts, n_sp, None
+        )
+        partial, send = lax.optimization_barrier((partial, send))
+        back = swap(send, "sp")
+        keep_near, send_near, own_stream = finish_experts(
+            mine, other, partial, segments, 0, 2 * rows, gain, w_gate, w_up, w_down,
+            experts, n_sp, stream_shape
+        )
+        keep, send = split(keep, back)
+        outer = keep + swap(send, "tp").astype(f32)
+        second = swap(outer[:rows].astype(bf16), "ep", 2)
+        third = swap(outer[rows:].astype(bf16), "ep", 3)
+        keep_near, nearest = part_near(keep_near, swap(send_near, "sp"))
+        keep_near, send_near = split(keep_near, swap(nearest, "ep", 1))
+        final = own_stream.astype(f32) + second.astype(f32) + third.astype(f32)
+        (final,) = lax.optimization_barrier((final,))
+        return (final + keep_near + swap(send_near, "tp").astype(f32)).astype(bf16)
+
+    def block_of(array, index):
+        blocks = array.reshape(2, n_tp, part, -1)
+        return lax.dynamic_slice_in_dim(blocks, index, 1, 1).reshape(2 * part, -1)
+
+    def columns_of(array, index):
+        return lax.dynamic_slice_in_dim(array, index * out_width, out_width, array.ndim - 1)
+
+    both = jnp.concatenate([packed, packed_other], axis=0)
+    terms = jnp.dot(both[:, :heads_width], weight, preferred_element_type=f32)
+    residual_both = jnp.concatenate([base, packed_other[:, heads_width : heads_width + half]], axis=0)
+    stream = block_of(terms, tp_index) + block_of(residual_both, tp_index).astype(f32)
     for by in range(1, n_tp):
-        totals = totals + swap(sent, "tp", by).astype(f32)
-    residual_both = jnp.concatenate([base, packed_other[:, heads_width : heads_width + half]], axis=0)
-    table = jnp.concatenate([packed[:, heads_width + half :], packed_other[:, heads_width + half :]], axis=0)
-    stream = (totals + residual_both.astype(f32)).astype(bf16)
-    chip = jnp.concatenate([stream, table], axis=1)
-    piece = lax.dynamic_slice_in_dim(
-        chip.reshape(2, n_tp, part, -1), tp_index, 1, 1
-    ).reshape(2 * part, -1)
-
-    mine, places = [chip], [(0, rows, None)]
-    for by in range(1, n_ep):
-        arrived = swap(piece, "ep", by)
+        stream = stream + swap(block_of(terms, tp_index ^ by).astype(bf16), "tp", by).astype(f32)
+    table = block_of(both[:, heads_width + half :], tp_index)
+    piece = jnp.concatenate([stream.astype(bf16), table], axis=1)
+    mine, places = [], []
+    for by in range(n_ep):
+        arrived = swap(piece, "ep", by) if by else piece
         for flip in range(n_tp):
             mine.append(swap(arrived, "tp", flip) if flip else arrived)
-            places.append((by * rows, part, flip))
-    w_gate, w_up, w_down, _ = lax.optimization_barrier((w_gate, w_up, w_down, piece))
-    w_gate, w_up, w_down = load(w_gate, w_up, w_down)
+            places.append(((0, part, by * rows, flip),))
     if part % 16:
-        blocks = jnp.stack(mine[1:]).reshape(n_ep - 1, n_tp, 2, part, -1)
+        gathered = jnp.stack(mine).reshape(n_ep, n_tp, 2, part, -1)
         bit = 1
         while bit < n_tp:
-            flipped = blocks[:, jnp.array([j ^ bit for j in range(n_tp)])]
-            blocks = jnp.where(tp_index & bit, flipped, blocks)
+            flipped = gathered[:, jnp.array([j ^ bit for j in range(n_tp)])]
+            gathered = jnp.where(tp_index & bit, flipped, gathered)
             bit *= 2
-        blocks = blocks.transpose(2, 0, 1, 3, 4).reshape(2, (n_ep - 1) * rows, -1)
-        mine = [jnp.concatenate([chip.reshape(2, rows, -1), blocks], axis=1).reshape(2 * n_ep * rows, -1)]
-        places = [(0, rows, None)]
+        mine = [gathered.transpose(2, 0, 1, 3, 4).reshape(2 * n_ep * rows, -1)]
+        places = [((0, n_ep * rows, 0, None),)]
     other = [swap(array, "sp") for array in mine]
-    keep, send = run_experts(
-        mine, other, tuple(places), norm_gain, w_gate, w_up, w_down, experts, n_sp
+    keep, send, own_stream = run_experts(
+        mine, other, tuple(places), norm_gain, w_gate, w_up, w_down, experts, n_sp, stream_shape, False
     )
     mixture = (keep + swap(send, "sp").astype(f32)).reshape(n_ep, rows, width)
-
-    def columns_of(array, index):
-        return lax.dynamic_slice_in_dim(array, index * out_width, out_width, array.ndim - 1)
-
-    total = columns_of(mixture, tp_index)
+    sums = columns_of(mixture, tp_index)
     for by in range(1, n_tp):
-        total = total + swap(columns_of(mixture, tp_index ^ by).astype(bf16), "tp", by).astype(f32)
-    final = total[0]
+        sums = sums + swap(columns_of(mixture, tp_index ^ by).astype(bf16), "tp", by).astype(f32)
+    final = sums[0]
     for by in range(1, n_ep):
-        final = final + swap(total[by].astype(bf16), "ep", by).astype(f32)
-
-    start = tp_index * out_width - sp_index * half
-    local = lax.dynamic_slice_in_dim(totals[:rows], jnp.clip(start, 0, half - out_width), out_width, 1)
-    aside = jnp.clip(tp_index * out_width - sp_index * half, 0, half - out_width)
-    arrived = swap(lax.dynamic_slice_in_dim(totals[rows:], aside, out_width, 1).astype(bf16), "sp")
-    here = tp_index * out_width // half == sp_index
-    projected = jnp.where(here, local, arrived.astype(f32))
-    return (final + (projected + columns_of(residual, tp_index).astype(f32))).astype(bf16)
+        final = final + swap(sums[by].astype(bf16), "ep", by).astype(f32)
+    return (final + own_stream.astype(f32)).astype(bf16)
 
 
 def solution(mesh):

time: 59.3 us -> 49.4 us (0.83)
  waiting for transfers between devices: 22.5 us -> 12.3 us
  Pallas kernels: 14.4 us -> 16.7 us
  starting transfers between devices: 21.1 us -> 19.1 us
    ppermute x21 -> x15, waiting for transfers between devices: 22.5 us -> 12.3 us  [swap(): return lax.ppermute(array, axis, [(i, i ^ by) for i in range(size)])]
    ppermute x21 -> x15, starting transfers between devices: 21.1 us -> 19.1 us  [swap(): return lax.ppermute(array, axis, [(i, i ^ by) for i in range(size)])]
    pallas_call x1 -> x3, Pallas kernels: 4.68 us -> 6.59 us  [load(): pl.pallas_call(load_kernel, in_specs=[ANYWHERE] * len(arrays), out_specs=...]
    pallas_call x2 -> x7, Pallas kernels: 4.78 us -> 5.2 us  [the longest x2 2.92 us: finish_experts(): pl.pallas_call(functools.partial(finish_kernel, experts, lambda e, s: (e...]
  transfers between devices with their start and end apart: 21 -> 15, of which waited for: 11 -> 8; matrix products, arithmetic and copies ran while one was open for 0% -> 0% of each run, Pallas kernels for 8% -> 19%
where the time goes in v3:
time: 49.4 us; the launch traced here: 49.2 us
  starting transfers between devices  19.1 us (39%)
  Pallas kernels  16.7 us (34%)
  waiting for transfers between devices  12.3 us (25%)
  other arithmetic  0.79 us (2%)
    ppermute x15, starting transfers between devices, swap(): return lax.ppermute(array, axis, [(i, i ^ by) for i in range(size)])  19.1 us
    ppermute x15, waiting for transfers between devices, swap(): return lax.ppermute(array, axis, [(i, i ^ by) for i in range(size)])  12.3 us
    pallas_call x3, Pallas kernels, load(): pl.pallas_call(load_kernel, in_specs=[ANYWHERE] * len(arrays), out_specs=...  6.59 us
    pallas_call x1, Pallas kernels, attend(): pl.pallas_call(functools.partial(attention_kernel, kv_count, per_group, c...  4.91 us
    pallas_call x2, Pallas kernels, finish_experts(): pl.pallas_call(functools.partial(finish_kernel, experts, lambda e, s: (e...  2.92 us
    pallas_call x1, Pallas kernels, start_experts(): pl.pallas_call(functools.partial(start_kernel, segments), in_specs=[WHOLE...  1.27 us
  transfers between devices with their start and end apart: 15, of which 8 were waited for; matrix products, arithmetic and copies ran while one was open for 0% of the time, Pallas kernels for 19%

profile of v3, /device:TPU:0, one launch (start us, length us, event | category | flops | bytes accessed | tf_op | source)
XLA Modules:
  0.0 49.2 jit_solution(1852023212591570822)
XLA Ops:
  0.0 4.9 %attention.1 = (bf16[32,3200]{1,0:T(8,128)(2,1)S(1)}, bf16[32,1024]{1,0:T(8,128)(2,1)S(1)}, bf16[2048,1024]{1,0:T(8,128)(2,1)S(1)}) custom-call(s32[32]{0:T(128)} %lengths_hbm.1, bf16[32,2048]{1,0:T(8,128)(2,1)} %query_hbm.1, bf16[32,256,512]{2,1,0:T(8,128)(2,1)} %key_hbm.1, bf16[32,256,512]{2,1,0:T(8,128)(2,1)} %value_hbm.1, bf16[32,512]{1,0:T(8,128)(2,1)} %new_key_hbm.1, ...), custom_call_target="tpu_custom_call" | custom-call | tf_op jit(solution)/shard_map/attention/pallas_call | solution.py:182
  4.9 0.5 %collective-permute-start = (bf16[32,3200]{1,0:T(8,128)(2,1)S(1)}, bf16[32,3200]{1,0:T(8,128)(2,1)S(1)}, u32[]{:S(2)}, u32[]{:S(2)}) collective-permute-start(bf16[32,3200]{1,0:T(8,128)(2,1)S(1)} %get-tuple-element.38.packed_ref), channel_id=1, source_target_pairs={{0,1},{1,0},{2,3},{3,2},{4,5},{5,4},{6,7},{7,6},{8,9},{9,8},{10,11... | collective-permute-start | bytes 614408 | tf_op jit(solution)/shard_map/ppermute | solution.py:529
  5.4 1.1 %collective-permute-done.other_ref = bf16[32,3200]{1,0:T(8,128)(2,1)S(1)} collective-permute-done((bf16[32,3200]{1,0:T(8,128)(2,1)S(1)}, bf16[32,3200]{1,0:T(8,128)(2,1)S(1)}, u32[]{:S(2)}, u32[]{:S(2)}) %collective-permute-start) | collective-permute-done | bytes 204832 | tf_op jit(solution)/shard_map/ppermute | solution.py:529
  6.5 0.9 %project.1 = (bf16[32,1024]{1,0:T(8,128)(2,1)S(1)}, bf16[32,1024]{1,0:T(8,128)(2,1)S(1)}, f32[32,1024]{1,0:T(8,128)S(1)}, f32[32,1024]{1,0:T(8,128)S(1)}, bf16[3...) custom-call(bf16[32,3200]{1,0:T(8,128)(2,1)S(1)} %get-tuple-element.38.packed_ref, ...), custom_call_target="tpu_custom_call" | custom-call | tf_op jit(solution)/shard_map/project/pallas_call | solution.py:239
  7.4 2.9 %collective-permute-start.1 = (bf16[32,1024]{1,0:T(8,128)(2,1)S(1)}, bf16[32,1024]{1,0:T(8,128)(2,1)S(1)}, u32[]{:S(2)}, u32[]{:S(2)}) collective-permute-start(bf16[32,1024]{1,0:T(8,128)(2,1)S(1)} %get-tuple-element.42), channel_id=1, source_target_pairs={{0,2},{2,0},{1,3},{3,1},{4,6},{6,4},{5,7},{7,5},{8,10},{10,8},{9,1... | collective-permute-start | bytes 196616 | tf_op jit(solution)/shard_map/ppermute | solution.py:529
  10.3 2.2 %load_weights.3.gate_ref = bf16[2,2048,512]{2,1,0:T(8,128)(2,1)S(1)} custom-call(bf16[2,2048,512]{2,1,0:T(8,128)(2,1)} %refs_0_), custom_call_target="tpu_custom_call" | custom-call | tf_op jit(solution)/shard_map/load_weights/pallas_call | solution.py:268
  12.6 0.1 collective-permute-start.2
  12.6 0.1 collective-permute-done.1
  12.8 3.1 %collective-permute-start.3 = (bf16[32,1152]{1,0:T(8,128)(2,1)S(1)}, bf16[32,1152]{1,0:T(8,128)(2,1)S(1)}, u32[]{:S(2)}, u32[]{:S(2)}) collective-permute-start(bf16[32,1152]{1,0:T(8,128)(2,1)S(1)} %get-tuple-element.73), channel_id=1, source_target_pairs={{0,8},{4,12},{8,0},{12,4},{1,9},{5,13},{9,1},{13,5},{2,10},{6,14},... | collective-permute-start | bytes 221192 | tf_op jit(solution)/shard_map/ppermute | solution.py:529
  15.9 1.3 %collective-permute-start.4 = (bf16[32,1152]{1,0:T(8,128)(2,1)S(1)}, bf16[32,1152]{1,0:T(8,128)(2,1)S(1)}, u32[]{:S(2)}, u32[]{:S(2)}) collective-permute-start(bf16[32,1152]{1,0:T(8,128)(2,1)S(1)} %get-tuple-element.73), channel_id=1, source_target_pairs={{0,12},{4,8},{8,4},{12,0},{1,13},{5,9},{9,5},{13,1},{2,14},{6,10},... | collective-permute-start | bytes 221192 | tf_op jit(solution)/shard_map/ppermute | solution.py:529
  17.2 0.0 collective-permute-done.2
  17.2 1.3 %collective-permute-start.6 = (bf16[64,1152]{1,0:T(8,128)(2,1)S(1)}, bf16[64,1152]{1,0:T(8,128)(2,1)S(1)}, u32[]{:S(2)}, u32[]{:S(2)}) collective-permute-start(bf16[64,1152]{1,0:T(8,128)(2,1)S(1)} %maximum_maximum_fusion), channel_id=1, source_target_pairs={{0,4},{4,0},{8,12},{12,8},{1,5},{5,1},{9,13},{13,9},{2,6},{6,2},{1... | collective-permute-start | bytes 442376 | tf_op jit(solution)/shard_map/ppermute | solution.py:529
  18.6 2.2 %load_weights.4.up_ref = bf16[2,2048,512]{2,1,0:T(8,128)(2,1)S(1)} custom-call(bf16[2,2048,512]{2,1,0:T(8,128)(2,1)} %refs_0_.1), custom_call_target="tpu_custom_call" | custom-call | tf_op jit(solution)/shard_map/load_weights/pallas_call | solution.py:268
  20.8 0.0 collective-permute-done.3
  20.8 2.1 %collective-permute-done.4 = bf16[32,1152]{1,0:T(8,128)(2,1)S(1)} collective-permute-done((bf16[32,1152]{1,0:T(8,128)(2,1)S(1)}, bf16[32,1152]{1,0:T(8,128)(2,1)S(1)}, u32[]{:S(2)}, u32[]{:S(2)}) %collective-permute-start.4) | collective-permute-done | bytes 73760 | tf_op jit(solution)/shard_map/ppermute | solution.py:529
  22.9 1.6 %collective-permute-start.5 = (bf16[64,1152]{1,0:T(8,128)(2,1)S(1)}, bf16[64,1152]{1,0:T(8,128)(2,1)S(1)}, u32[]{:S(2)}, u32[]{:S(2)}) collective-permute-start(bf16[64,1152]{1,0:T(8,128)(2,1)S(1)} %constant_dynamic-update-slice_fusion), channel_id=1, source_target_pairs={{0,2},{2,0},{1,3},{3,1},{4,6},{6,4},{5,7},{7,5},{8,10},{10,8},{9,1... | collective-permute-start | bytes 442376 | tf_op jit(solution)/shard_map/ppermute | solution.py:529
  24.4 0.0 copy-start
  24.4 2.2 %load_weights.5.down_ref = bf16[2,512,2048]{2,1,0:T(8,128)(2,1)S(1)} custom-call(bf16[2,512,2048]{2,1,0:T(8,128)(2,1)} %refs_0_.2), custom_call_target="tpu_custom_call" | custom-call | tf_op jit(solution)/shard_map/load_weights/pallas_call | solution.py:268
  26.7 0.0 collective-permute-done.6
  26.7 1.4 %collective-permute-done.5 = bf16[64,1152]{1,0:T(8,128)(2,1)S(1)} collective-permute-done((bf16[64,1152]{1,0:T(8,128)(2,1)S(1)}, bf16[64,1152]{1,0:T(8,128)(2,1)S(1)}, u32[]{:S(2)}, u32[]{:S(2)}) %collective-permute-start.5) | collective-permute-done | bytes 147488 | tf_op jit(solution)/shard_map/ppermute | solution.py:529
  28.2 0.1 collective-permute-start.7
  28.2 0.0 copy-done
  28.2 1.3 %start_experts.1.partial_ref = f32[256,2048]{1,0:T(8,128)S(1)} custom-call(bf16[256,1152]{1,0:T(8,128)(2,1)S(1)} %constant_dynamic-update-slice_fusion.2.mine_ref, f32[1,2048]{1,0:T(1,128)S(1)} %bitcast.3, bf16[2,2048,512]{2,1,0:T(8,128)(2,1)S(1)} %load_weights.3.gate_ref, bf16[2,2048,512]{2,1,0:T(8,128)(2,1)S(1)} %load_weights.4.up_ref), custom_call_target="tpu_custom_call" | custom-call | tf_op jit(solution)/shard_map/start_experts/pallas_call | solution.py:444
  29.5 0.7 %collective-permute-done.7.other_ref = bf16[256,1152]{1,0:T(8,128)(2,1)S(1)} collective-permute-done((bf16[256,1152]{1,0:T(8,128)(2,1)S(1)}, bf16[256,1152]{1,0:T(8,128)(2,1)S(1)}, u32[]{:S(2)}, u32[]{:S(2)}) %collective-permute-start.7) | collective-permute-done | bytes 589856 | tf_op jit(solution)/shard_map/ppermute | solution.py:529
  30.2 1.5 %finish_experts.2 = (f32[64,2048]{1,0:T(8,128)S(1)}, bf16[64,2048]{1,0:T(8,128)(2,1)S(1)}) custom-call(bf16[256,1152]{1,0:T(8,128)(2,1)S(1)} %constant_dynamic-update-slice_fusion.2.mine_ref, bf16[256,1152]{1,0:T(8,128)(2,1)S(1)} %collective-permute-done.7.other_ref, f32[256,2048]{1,0:T(8,128)S(1)} %start_experts.1.partial_ref, f32[1,2048]{1,0:T(1,128)S(1)} %bitcast.4, ...), custom_call_target="tpu_custom_call" | custom-call | tf_op jit(solution)/shard_map/finish_experts/pallas_call | solution.py:465
  31.7 0.2 collective-permute-start.8
  31.9 1.5 %finish_experts.3 = (f32[64,2048]{1,0:T(8,128)S(1)}, bf16[64,2048]{1,0:T(8,128)(2,1)S(1)}, bf16[32,1024]{1,0:T(8,128)(2,1)S(1)}) custom-call(bf16[256,1152]{1,0:T(8,128)(2,1)S(1)} %constant_dynamic-update-slice_fusion.2.mine_ref, bf16[256,1152]{1,0:T(8,128)(2,1)S(1)} %collective-permute-done.7.other_ref, f32[256,2048]{1,0:T(8,128)S(1)} %start_experts.1.partial_ref, ...), custom_call_target="tpu_custom_call" | custom-call | tf_op jit(solution)/shard_map/finish_experts/pallas_call | solution.py:465
  33.4 0.4 collective-permute-start.12
  33.8 0.0 collective-permute-done.8.back
  33.8 1.6 %collective-permute-start.9 = (bf16[64,1024]{1,0:T(8,128)(2,1)S(1)}, bf16[64,1024]{1,0:T(8,128)(2,1)S(1)}, u32[]{:S(2)}, u32[]{:S(2)}) collective-permute-start(bf16[64,1024]{1,0:T(8,128)(2,1)S(1)} %get-tuple-element.64), channel_id=1, source_target_pairs={{0,2},{2,0},{1,3},{3,1},{4,6},{6,4},{5,7},{7,5},{8,10},{10,8},{9,1... | collective-permute-start | bytes 393224 | tf_op jit(solution)/shard_map/ppermute | solution.py:529
  35.4 0.0 collective-permute-done.12.back
  35.5 1.0 %collective-permute-start.13 = (bf16[32,2048]{1,0:T(8,128)(2,1)S(1)}, bf16[32,2048]{1,0:T(8,128)(2,1)S(1)}, u32[]{:S(2)}, u32[]{:S(2)}) collective-permute-start(bf16[32,2048]{1,0:T(8,128)(2,1)S(1)} %get-tuple-element.68), channel_id=1, source_target_pairs={{0,4},{4,0},{8,12},{12,8},{1,5},{5,1},{9,13},{13,9},{2,6},{6,2},{1... | collective-permute-start | bytes 393224 | tf_op jit(solution)/shard_map/ppermute | solution.py:529
  36.5 3.0 %collective-permute-done.9 = bf16[64,1024]{1,0:T(8,128)(2,1)S(1)} collective-permute-done((bf16[64,1024]{1,0:T(8,128)(2,1)S(1)}, bf16[64,1024]{1,0:T(8,128)(2,1)S(1)}, u32[]{:S(2)}, u32[]{:S(2)}) %collective-permute-start.9) | collective-permute-done | bytes 131104 | tf_op jit(solution)/shard_map/ppermute | solution.py:529
  39.5 2.9 %collective-permute-start.10 = (bf16[32,1024]{1,0:T(8,128)(2,1)S(1)}, bf16[32,1024]{1,0:T(8,128)(2,1)S(1)}, u32[]{:S(2)}, u32[]{:S(2)}) collective-permute-start(bf16[32,1024]{1,0:T(8,128)(2,1)S(1)} %get-tuple-element.71), channel_id=1, source_target_pairs={{0,8},{4,12},{8,0},{12,4},{1,9},{5,13},{9,1},{13,5},{2,10},{6,14},... | collective-permute-start | bytes 196616 | tf_op jit(solution)/shard_map/ppermute | solution.py:529
  42.4 0.6 %collective-permute-start.11 = (bf16[32,1024]{1,0:T(8,128)(2,1)S(1)}, bf16[32,1024]{1,0:T(8,128)(2,1)S(1)}, u32[]{:S(2)}, u32[]{:S(2)}) collective-permute-start(bf16[32,1024]{1,0:T(8,128)(2,1)S(1)} %get-tuple-element.72), channel_id=1, source_target_pairs={{0,12},{4,8},{8,4},{12,0},{1,13},{5,9},{9,5},{13,1},{2,14},{6,10},... | collective-permute-start | bytes 196616 | tf_op jit(solution)/shard_map/ppermute | solution.py:529
  43.0 0.0 collective-permute-done.13.back
  43.0 1.5 %collective-permute-start.14 = (bf16[32,1024]{1,0:T(8,128)(2,1)S(1)}, bf16[32,1024]{1,0:T(8,128)(2,1)S(1)}, u32[]{:S(2)}, u32[]{:S(2)}) collective-permute-start(bf16[32,1024]{1,0:T(8,128)(2,1)S(1)} %get-tuple-element.70), channel_id=1, source_target_pairs={{0,2},{2,0},{1,3},{3,1},{4,6},{6,4},{5,7},{7,5},{8,10},{10,8},{9,1... | collective-permute-start | bytes 196616 | tf_op jit(solution)/shard_map/ppermute | solution.py:529
  44.5 2.3 %collective-permute-done.10 = bf16[32,1024]{1,0:T(8,128)(2,1)S(1)} collective-permute-done((bf16[32,1024]{1,0:T(8,128)(2,1)S(1)}, bf16[32,1024]{1,0:T(8,128)(2,1)S(1)}, u32[]{:S(2)}, u32[]{:S(2)}) %collective-permute-start.10) | collective-permute-done | bytes 65568 | tf_op jit(solution)/shard_map/ppermute | solution.py:529
  46.8 1.7 %collective-permute-done.11 = bf16[32,1024]{1,0:T(8,128)(2,1)S(1)} collective-permute-done((bf16[32,1024]{1,0:T(8,128)(2,1)S(1)}, bf16[32,1024]{1,0:T(8,128)(2,1)S(1)}, u32[]{:S(2)}, u32[]{:S(2)}) %collective-permute-start.11) | collective-permute-done | bytes 65568 | tf_op jit(solution)/shard_map/ppermute | solution.py:529
  48.5 0.0 collective-permute-done.14
  48.5 0.7 %add_convert_fusion.1 = bf16[32,1024]{1,0:T(8,128)(2,1)} fusion(bf16[32,1024]{1,0:T(8,128)(2,1)S(1)} %collective-permute-done.14, f32[32,1024]{1,0:T(8,128)S(1)} %convert_add_fusion, f32[32,1024]{1,0:T(8,128)S(1)} %get-tuple-element.69), kind=kLoop, calls=%fused_computation.2 | loop fusion | flops 131072 | bytes 393216 | tf_op jit(solution)/shard_map/convert_element_type | solution.py:614
  (17 shorter events, 0.3 us)
Async XLA Ops:
  4.9 1.6 %collective-permute-start = (bf16[32,3200]{1,0:T(8,128)(2,1)S(1)}, bf16[32,3200]{1,0:T(8,128)(2,1)S(1)}, u32[]{:S(2)}, u32[]{:S(2)}) collective-permute-start(bf16[32,3200]{1,0:T(8,128)(2,1)S(1)} %get-tuple-element.38.packed_ref), channel_id=1, source_target_pairs={{0,1},{1,0},{2,3},{3,2},{4,5},{5,4},{6,7},{7,6},{8,9},{9,8},{10,11... | collective-permute-start | bytes 614408 | tf_op jit(solution)/shard_map/ppermute | solution.py:529
  7.4 5.3 %collective-permute-start.1 = (bf16[32,1024]{1,0:T(8,128)(2,1)S(1)}, bf16[32,1024]{1,0:T(8,128)(2,1)S(1)}, u32[]{:S(2)}, u32[]{:S(2)}) collective-permute-start(bf16[32,1024]{1,0:T(8,128)(2,1)S(1)} %get-tuple-element.42), channel_id=1, source_target_pairs={{0,2},{2,0},{1,3},{3,1},{4,6},{6,4},{5,7},{7,5},{8,10},{10,8},{9,1... | collective-permute-start | bytes 196616 | tf_op jit(solution)/shard_map/ppermute | solution.py:529
  12.6 4.6 %collective-permute-start.2 = (bf16[32,1024]{1,0:T(8,128)(2,1)S(1)}, bf16[32,1024]{1,0:T(8,128)(2,1)S(1)}, u32[]{:S(2)}, u32[]{:S(2)}) collective-permute-start(bf16[32,1024]{1,0:T(8,128)(2,1)S(1)} %get-tuple-element.47), channel_id=1, source_target_pairs={{0,2},{2,0},{1,3},{3,1},{4,6},{6,4},{5,7},{7,5},{8,10},{10,8},{9,1... | collective-permute-start | bytes 196616 | tf_op jit(solution)/shard_map/ppermute | solution.py:529
  12.8 8.0 %collective-permute-start.3 = (bf16[32,1152]{1,0:T(8,128)(2,1)S(1)}, bf16[32,1152]{1,0:T(8,128)(2,1)S(1)}, u32[]{:S(2)}, u32[]{:S(2)}) collective-permute-start(bf16[32,1152]{1,0:T(8,128)(2,1)S(1)} %get-tuple-element.73), channel_id=1, source_target_pairs={{0,8},{4,12},{8,0},{12,4},{1,9},{5,13},{9,1},{13,5},{2,10},{6,14},... | collective-permute-start | bytes 221192 | tf_op jit(solution)/shard_map/ppermute | solution.py:529
  15.9 7.0 %collective-permute-start.4 = (bf16[32,1152]{1,0:T(8,128)(2,1)S(1)}, bf16[32,1152]{1,0:T(8,128)(2,1)S(1)}, u32[]{:S(2)}, u32[]{:S(2)}) collective-permute-start(bf16[32,1152]{1,0:T(8,128)(2,1)S(1)} %get-tuple-element.73), channel_id=1, source_target_pairs={{0,12},{4,8},{8,4},{12,0},{1,13},{5,9},{9,5},{13,1},{2,14},{6,10},... | collective-permute-start | bytes 221192 | tf_op jit(solution)/shard_map/ppermute | solution.py:529
  17.2 9.4 %collective-permute-start.6 = (bf16[64,1152]{1,0:T(8,128)(2,1)S(1)}, bf16[64,1152]{1,0:T(8,128)(2,1)S(1)}, u32[]{:S(2)}, u32[]{:S(2)}) collective-permute-start(bf16[64,1152]{1,0:T(8,128)(2,1)S(1)} %maximum_maximum_fusion), channel_id=1, source_target_pairs={{0,4},{4,0},{8,12},{12,8},{1,5},{5,1},{9,13},{13,9},{2,6},{6,2},{1... | collective-permute-start | bytes 442376 | tf_op jit(solution)/shard_map/ppermute | solution.py:529
  22.9 5.2 %collective-permute-start.5 = (bf16[64,1152]{1,0:T(8,128)(2,1)S(1)}, bf16[64,1152]{1,0:T(8,128)(2,1)S(1)}, u32[]{:S(2)}, u32[]{:S(2)}) collective-permute-start(bf16[64,1152]{1,0:T(8,128)(2,1)S(1)} %constant_dynamic-update-slice_fusion), channel_id=1, source_target_pairs={{0,2},{2,0},{1,3},{3,1},{4,6},{6,4},{5,7},{7,5},{8,10},{10,8},{9,1... | collective-permute-start | bytes 442376 | tf_op jit(solution)/shard_map/ppermute | solution.py:529
  24.4 3.8 %copy-start = (f32[2048]{0:T(1024)S(1)}, f32[2048]{0:T(1024)}, u32[]{:S(2)}) copy-start(f32[2048]{0:T(1024)} %param.22) | copy-start | bytes 24580
  28.2 2.1 %collective-permute-start.7 = (bf16[256,1152]{1,0:T(8,128)(2,1)S(1)}, bf16[256,1152]{1,0:T(8,128)(2,1)S(1)}, u32[]{:S(2)}, u32[]{:S(2)}) collective-permute-start(bf16[256,1152]{1,0:T(8,128)(2,1)S(1)} %constant_dynamic-update-slice_fusion.2.mine_ref), channel_id=1, source_target_pairs={{0,1},{1,0},{2,3},{3,2},{4,5},{5,4},{6,7},{7,6},{8,9},{9,8},{10,11... | collective-permute-start | bytes 1769480 | tf_op jit(solution)/shard_map/ppermute | solution.py:529
  31.7 2.1 %collective-permute-start.8 = (bf16[64,2048]{1,0:T(8,128)(2,1)S(1)}, bf16[64,2048]{1,0:T(8,128)(2,1)S(1)}, u32[]{:S(2)}, u32[]{:S(2)}) collective-permute-start(bf16[64,2048]{1,0:T(8,128)(2,1)S(1)} %get-tuple-element.62), channel_id=1, source_target_pairs={{0,1},{1,0},{2,3},{3,2},{4,5},{5,4},{6,7},{7,6},{8,9},{9,8},{10,11... | collective-permute-start | bytes 786440 | tf_op jit(solution)/shard_map/ppermute | solution.py:529
  33.4 2.1 %collective-permute-start.12 = (bf16[64,2048]{1,0:T(8,128)(2,1)S(1)}, bf16[64,2048]{1,0:T(8,128)(2,1)S(1)}, u32[]{:S(2)}, u32[]{:S(2)}) collective-permute-start(bf16[64,2048]{1,0:T(8,128)(2,1)S(1)} %get-tuple-element.66), channel_id=1, source_target_pairs={{0,1},{1,0},{2,3},{3,2},{4,5},{5,4},{6,7},{7,6},{8,9},{9,8},{10,11... | collective-permute-start | bytes 786440 | tf_op jit(solution)/shard_map/ppermute | solution.py:529
  33.8 5.6 %collective-permute-start.9 = (bf16[64,1024]{1,0:T(8,128)(2,1)S(1)}, bf16[64,1024]{1,0:T(8,128)(2,1)S(1)}, u32[]{:S(2)}, u32[]{:S(2)}) collective-permute-start(bf16[64,1024]{1,0:T(8,128)(2,1)S(1)} %get-tuple-element.64), channel_id=1, source_target_pairs={{0,2},{2,0},{1,3},{3,1},{4,6},{6,4},{5,7},{7,5},{8,10},{10,8},{9,1... | collective-permute-start | bytes 393224 | tf_op jit(solution)/shard_map/ppermute | solution.py:529
  35.5 7.6 %collective-permute-start.13 = (bf16[32,2048]{1,0:T(8,128)(2,1)S(1)}, bf16[32,2048]{1,0:T(8,128)(2,1)S(1)}, u32[]{:S(2)}, u32[]{:S(2)}) collective-permute-start(bf16[32,2048]{1,0:T(8,128)(2,1)S(1)} %get-tuple-element.68), channel_id=1, source_target_pairs={{0,4},{4,0},{8,12},{12,8},{1,5},{5,1},{9,13},{13,9},{2,6},{6,2},{1... | collective-permute-start | bytes 393224 | tf_op jit(solution)/shard_map/ppermute | solution.py:529
  39.5 7.3 %collective-permute-start.10 = (bf16[32,1024]{1,0:T(8,128)(2,1)S(1)}, bf16[32,1024]{1,0:T(8,128)(2,1)S(1)}, u32[]{:S(2)}, u32[]{:S(2)}) collective-permute-start(bf16[32,1024]{1,0:T(8,128)(2,1)S(1)} %get-tuple-element.71), channel_id=1, source_target_pairs={{0,8},{4,12},{8,0},{12,4},{1,9},{5,13},{9,1},{13,5},{2,10},{6,14},... | collective-permute-start | bytes 196616 | tf_op jit(solution)/shard_map/ppermute | solution.py:529
  42.4 6.1 %collective-permute-start.11 = (bf16[32,1024]{1,0:T(8,128)(2,1)S(1)}, bf16[32,1024]{1,0:T(8,128)(2,1)S(1)}, u32[]{:S(2)}, u32[]{:S(2)}) collective-permute-start(bf16[32,1024]{1,0:T(8,128)(2,1)S(1)} %get-tuple-element.72), channel_id=1, source_target_pairs={{0,12},{4,8},{8,4},{12,0},{1,13},{5,9},{9,5},{13,1},{2,14},{6,10},... | collective-permute-start | bytes 196616 | tf_op jit(solution)/shard_map/ppermute | solution.py:529
  43.0 5.5 %collective-permute-start.14 = (bf16[32,1024]{1,0:T(8,128)(2,1)S(1)}, bf16[32,1024]{1,0:T(8,128)(2,1)S(1)}, u32[]{:S(2)}, u32[]{:S(2)}) collective-permute-start(bf16[32,1024]{1,0:T(8,128)(2,1)S(1)} %get-tuple-element.70), channel_id=1, source_target_pairs={{0,2},{2,0},{1,3},{3,1},{4,6},{6,4},{5,7},{7,5},{8,10},{10,8},{9,1... | collective-permute-start | bytes 196616 | tf_op jit(solution)/shard_map/ppermute | solution.py:529

commit v4 on v3

--- a/solution.py
+++ b/solution.py
@@ -483,22 +483,25 @@
     )(in_vmem(mine), in_vmem(other), in_vmem(partial), gain, *map(in_vmem, (gate, up, down)))
 
 
-def split_kernel(keep, back, keep_ref, send_ref):
+def split_kernel(keep, back, *out_refs):
+    count = len(out_refs) // 2
     tp_index = lax.axis_index("tp")
-    width = keep_ref.shape[1]
+    rows, width = out_refs[0].shape
     mine = pl.ds(pl.multiple_of(tp_index * width, LANES), width)
     theirs = pl.ds(pl.multiple_of((1 - tp_index) * width, LANES), width)
-    keep_ref[...] = keep[:, mine] + back[:, mine].astype(f32)
-    send_ref[...] = (keep[:, theirs] + back[:, theirs].astype(f32)).astype(bf16)
-
-
-def split(keep, back):
-    shape = (keep.shape[0], keep.shape[1] // 2)
+    for i, (keep_ref, send_ref) in enumerate(zip(out_refs[:count], out_refs[count:])):
+        at = slice(i * rows, (i + 1) * rows)
+        keep_ref[...] = keep[at, mine] + back[at, mine].astype(f32)
+        send_ref[...] = (keep[at, theirs] + back[at, theirs].astype(f32)).astype(bf16)
+
+
+def split(pieces, keep, back):
+    shape = (keep.shape[0] // pieces, keep.shape[1] // 2)
     return pl.pallas_call(
         split_kernel,
         in_specs=[WHOLE] * 2,
-        out_specs=[WHOLE] * 2,
-        out_shape=[pltpu.VMEM(shape, f32), pltpu.VMEM(shape, bf16)],
+        out_specs=[WHOLE] * (2 * pieces),
+        out_shape=[pltpu.VMEM(shape, f32)] * pieces + [pltpu.VMEM(shape, bf16)] * pieces,
         compiler_params=pltpu.CompilerParams(vmem_limit_bytes=8 * MIB),
         cost_estimate=FREE,
         name="split",
@@ -576,13 +579,16 @@
         next_chip = swap(chip, "ep", 1)
         w_up, _ = lax.optimization_barrier((w_up, chip))
         (w_up,) = load(w_up)
-        second, third, w_up = lax.optimization_barrier((second, third, w_up))
-        parts = jnp.concatenate([second, third], axis=0)
-        far = swap(parts, "tp")
-        w_down, _ = lax.optimization_barrier((w_down, parts))
+        second, w_up = lax.optimization_barrier((second, w_up))
+        second_far, third_far = swap(second, "tp"), swap(third, "tp")
+        w_down, _, _ = lax.optimization_barrier((w_down, second, third))
         (w_down,) = load(w_down)
-        far, next_chip, w_down = lax.optimization_barrier((far, next_chip, w_down))
-        mine = jnp.concatenate([chip, next_chip, parts, far], axis=0)
+        second_far, third_far, next_chip, w_down = lax.optimization_barrier(
+            (second_far, third_far, next_chip, w_down)
+        )
+        mine = jnp.concatenate(
+            [chip, next_chip, second, third, second_far, third_far], axis=0
+        )
         other = swap(mine, "sp")
         size = 2 * part
         segments = tuple(
@@ -603,12 +609,12 @@
             mine, other, partial, segments, 0, 2 * rows, gain, w_gate, w_up, w_down,
             experts, n_sp, stream_shape
         )
-        keep, send = split(keep, back)
-        outer = keep + swap(send, "tp").astype(f32)
-        second = swap(outer[:rows].astype(bf16), "ep", 2)
-        third = swap(outer[rows:].astype(bf16), "ep", 3)
+        keep_second, keep_third, send_second, send_third = split(2, keep, back)
+        second = keep_second + swap(send_second, "tp").astype(f32)
+        third = keep_third + swap(send_third, "tp").astype(f32)
+        second, third = swap(second.astype(bf16), "ep", 2), swap(third.astype(bf16), "ep", 3)
         keep_near, nearest = part_near(keep_near, swap(send_near, "sp"))
-        keep_near, send_near = split(keep_near, swap(nearest, "ep", 1))
+        keep_near, send_near = split(1, keep_near, swap(nearest, "ep", 1))
         final = own_stream.astype(f32) + second.astype(f32) + third.astype(f32)
         (final,) = lax.optimization_barrier((final,))
         return (final + keep_near + swap(send_near, "tp").astype(f32)).astype(bf16)

time: 49.4 us -> 47.4 us (0.960)
  waiting for transfers between devices: 12.3 us -> 8.33 us
  starting transfers between devices: 19.1 us -> 21.1 us
    ppermute x15 -> x17, waiting for transfers between devices: 12.3 us -> 8.33 us  [swap(): return lax.ppermute(array, axis, [(i, i ^ by) for i in range(size)])]
    ppermute x15 -> x17, starting transfers between devices: 19.1 us -> 21.1 us  [swap(): return lax.ppermute(array, axis, [(i, i ^ by) for i in range(size)])]
  transfers between devices with their start and end apart: 15 -> 17, of which waited for: 8 -> 8; matrix products, arithmetic and copies ran while one was open for 0% -> 0% of each run, Pallas kernels for 19% -> 20%
where the time goes in v4:
time: 47.4 us; the launch traced here: 47.2 us
  starting transfers between devices  21.1 us (45%)
  Pallas kernels  16.7 us (35%)
  waiting for transfers between devices  8.33 us (18%)
  other arithmetic  0.79 us (2%)
    ppermute x17, starting transfers between devices, swap(): return lax.ppermute(array, axis, [(i, i ^ by) for i in range(size)])  21.1 us
    ppermute x17, waiting for transfers between devices, swap(): return lax.ppermute(array, axis, [(i, i ^ by) for i in range(size)])  8.33 us
    pallas_call x3, Pallas kernels, load(): pl.pallas_call(load_kernel, in_specs=[ANYWHERE] * len(arrays), out_specs=...  6.59 us
    pallas_call x1, Pallas kernels, attend(): pl.pallas_call(functools.partial(attention_kernel, kv_count, per_group, c...  4.91 us
    pallas_call x2, Pallas kernels, finish_experts(): pl.pallas_call(functools.partial(finish_kernel, experts, lambda e, s: (e...  2.92 us
    pallas_call x1, Pallas kernels, start_experts(): pl.pallas_call(functools.partial(start_kernel, segments), in_specs=[WHOLE...  1.26 us
  transfers between devices with their start and end apart: 17, of which 8 were waited for; matrix products, arithmetic and copies ran while one was open for 0% of the time, Pallas kernels for 20%

profile of v4, /device:TPU:0, one launch (start us, length us, event | category | flops | bytes accessed | tf_op | source)
XLA Modules:
  0.0 47.2 jit_solution(3888505016742644262)
XLA Ops:
  0.0 4.9 %attention.1 = (bf16[32,3200]{1,0:T(8,128)(2,1)S(1)}, bf16[32,1024]{1,0:T(8,128)(2,1)S(1)}, bf16[2048,1024]{1,0:T(8,128)(2,1)S(1)}) custom-call(s32[32]{0:T(128)} %lengths_hbm.1, bf16[32,2048]{1,0:T(8,128)(2,1)} %query_hbm.1, bf16[32,256,512]{2,1,0:T(8,128)(2,1)} %key_hbm.1, bf16[32,256,512]{2,1,0:T(8,128)(2,1)} %value_hbm.1, bf16[32,512]{1,0:T(8,128)(2,1)} %new_key_hbm.1, ...), custom_call_target="tpu_custom_call" | custom-call | tf_op jit(solution)/shard_map/attention/pallas_call | solution.py:182
  4.9 0.5 %collective-permute-start = (bf16[32,3200]{1,0:T(8,128)(2,1)S(1)}, bf16[32,3200]{1,0:T(8,128)(2,1)S(1)}, u32[]{:S(2)}, u32[]{:S(2)}) collective-permute-start(bf16[32,3200]{1,0:T(8,128)(2,1)S(1)} %get-tuple-element.40.packed_ref), channel_id=1, source_target_pairs={{0,1},{1,0},{2,3},{3,2},{4,5},{5,4},{6,7},{7,6},{8,9},{9,8},{10,11... | collective-permute-start | bytes 614408 | tf_op jit(solution)/shard_map/ppermute | solution.py:532
  5.4 1.1 %collective-permute-done.other_ref = bf16[32,3200]{1,0:T(8,128)(2,1)S(1)} collective-permute-done((bf16[32,3200]{1,0:T(8,128)(2,1)S(1)}, bf16[32,3200]{1,0:T(8,128)(2,1)S(1)}, u32[]{:S(2)}, u32[]{:S(2)}) %collective-permute-start) | collective-permute-done | bytes 204832 | tf_op jit(solution)/shard_map/ppermute | solution.py:532
  6.5 0.9 %project.1 = (bf16[32,1024]{1,0:T(8,128)(2,1)S(1)}, bf16[32,1024]{1,0:T(8,128)(2,1)S(1)}, f32[32,1024]{1,0:T(8,128)S(1)}, f32[32,1024]{1,0:T(8,128)S(1)}, bf16[3...) custom-call(bf16[32,3200]{1,0:T(8,128)(2,1)S(1)} %get-tuple-element.40.packed_ref, ...), custom_call_target="tpu_custom_call" | custom-call | tf_op jit(solution)/shard_map/project/pallas_call | solution.py:239
  7.4 2.9 %collective-permute-start.1 = (bf16[32,1024]{1,0:T(8,128)(2,1)S(1)}, bf16[32,1024]{1,0:T(8,128)(2,1)S(1)}, u32[]{:S(2)}, u32[]{:S(2)}) collective-permute-start(bf16[32,1024]{1,0:T(8,128)(2,1)S(1)} %get-tuple-element.44), channel_id=1, source_target_pairs={{0,2},{2,0},{1,3},{3,1},{4,6},{6,4},{5,7},{7,5},{8,10},{10,8},{9,1... | collective-permute-start | bytes 196616 | tf_op jit(solution)/shard_map/ppermute | solution.py:532
  10.3 2.2 %load_weights.3.gate_ref = bf16[2,2048,512]{2,1,0:T(8,128)(2,1)S(1)} custom-call(bf16[2,2048,512]{2,1,0:T(8,128)(2,1)} %refs_0_), custom_call_target="tpu_custom_call" | custom-call | tf_op jit(solution)/shard_map/load_weights/pallas_call | solution.py:268
  12.6 0.1 collective-permute-start.2
  12.6 0.1 collective-permute-done.1
  12.8 3.1 %collective-permute-start.3 = (bf16[32,1152]{1,0:T(8,128)(2,1)S(1)}, bf16[32,1152]{1,0:T(8,128)(2,1)S(1)}, u32[]{:S(2)}, u32[]{:S(2)}) collective-permute-start(bf16[32,1152]{1,0:T(8,128)(2,1)S(1)} %get-tuple-element.75), channel_id=1, source_target_pairs={{0,8},{4,12},{8,0},{12,4},{1,9},{5,13},{9,1},{13,5},{2,10},{6,14},... | collective-permute-start | bytes 221192 | tf_op jit(solution)/shard_map/ppermute | solution.py:532
  15.9 1.3 %collective-permute-start.5 = (bf16[32,1152]{1,0:T(8,128)(2,1)S(1)}, bf16[32,1152]{1,0:T(8,128)(2,1)S(1)}, u32[]{:S(2)}, u32[]{:S(2)}) collective-permute-start(bf16[32,1152]{1,0:T(8,128)(2,1)S(1)} %get-tuple-element.75), channel_id=1, source_target_pairs={{0,12},{4,8},{8,4},{12,0},{1,13},{5,9},{9,5},{13,1},{2,14},{6,10},... | collective-permute-start | bytes 221192 | tf_op jit(solution)/shard_map/ppermute | solution.py:532
  17.2 0.0 collective-permute-done.2
  17.2 1.3 %collective-permute-start.7 = (bf16[64,1152]{1,0:T(8,128)(2,1)S(1)}, bf16[64,1152]{1,0:T(8,128)(2,1)S(1)}, u32[]{:S(2)}, u32[]{:S(2)}) collective-permute-start(bf16[64,1152]{1,0:T(8,128)(2,1)S(1)} %maximum_maximum_fusion), channel_id=1, source_target_pairs={{0,4},{4,0},{8,12},{12,8},{1,5},{5,1},{9,13},{13,9},{2,6},{6,2},{1... | collective-permute-start | bytes 442376 | tf_op jit(solution)/shard_map/ppermute | solution.py:532
  18.6 2.2 %load_weights.4.up_ref = bf16[2,2048,512]{2,1,0:T(8,128)(2,1)S(1)} custom-call(bf16[2,2048,512]{2,1,0:T(8,128)(2,1)} %refs_0_.1), custom_call_target="tpu_custom_call" | custom-call | tf_op jit(solution)/shard_map/load_weights/pallas_call | solution.py:268
  20.8 0.0 collective-permute-done.3
  20.8 1.4 %collective-permute-start.4 = (bf16[32,1152]{1,0:T(8,128)(2,1)S(1)}, bf16[32,1152]{1,0:T(8,128)(2,1)S(1)}, u32[]{:S(2)}, u32[]{:S(2)}) collective-permute-start(bf16[32,1152]{1,0:T(8,128)(2,1)S(1)} %collective-permute-done.3), channel_id=1, source_target_pairs={{0,2},{2,0},{1,3},{3,1},{4,6},{6,4},{5,7},{7,5},{8,10},{10,8},{9,1... | collective-permute-start | bytes 221192 | tf_op jit(solution)/shard_map/ppermute | solution.py:532
  22.2 0.7 %collective-permute-done.5 = bf16[32,1152]{1,0:T(8,128)(2,1)S(1)} collective-permute-done((bf16[32,1152]{1,0:T(8,128)(2,1)S(1)}, bf16[32,1152]{1,0:T(8,128)(2,1)S(1)}, u32[]{:S(2)}, u32[]{:S(2)}) %collective-permute-start.5) | collective-permute-done | bytes 73760 | tf_op jit(solution)/shard_map/ppermute | solution.py:532
  22.8 1.5 %collective-permute-start.6 = (bf16[32,1152]{1,0:T(8,128)(2,1)S(1)}, bf16[32,1152]{1,0:T(8,128)(2,1)S(1)}, u32[]{:S(2)}, u32[]{:S(2)}) collective-permute-start(bf16[32,1152]{1,0:T(8,128)(2,1)S(1)} %collective-permute-done.5), channel_id=1, source_target_pairs={{0,2},{2,0},{1,3},{3,1},{4,6},{6,4},{5,7},{7,5},{8,10},{10,8},{9,1... | collective-permute-start | bytes 221192 | tf_op jit(solution)/shard_map/ppermute | solution.py:532
  24.3 0.0 copy-start
  24.4 2.2 %load_weights.5.down_ref = bf16[2,512,2048]{2,1,0:T(8,128)(2,1)S(1)} custom-call(bf16[2,512,2048]{2,1,0:T(8,128)(2,1)} %refs_0_.2), custom_call_target="tpu_custom_call" | custom-call | tf_op jit(solution)/shard_map/load_weights/pallas_call | solution.py:268
  26.6 0.0 collective-permute-done.4
  26.6 0.0 collective-permute-done.7
  26.6 0.6 %collective-permute-done.6 = bf16[32,1152]{1,0:T(8,128)(2,1)S(1)} collective-permute-done((bf16[32,1152]{1,0:T(8,128)(2,1)S(1)}, bf16[32,1152]{1,0:T(8,128)(2,1)S(1)}, u32[]{:S(2)}, u32[]{:S(2)}) %collective-permute-start.6) | collective-permute-done | bytes 73760 | tf_op jit(solution)/shard_map/ppermute | solution.py:532
  27.3 0.1 collective-permute-start.8
  27.4 0.0 copy-done
  27.4 1.3 %start_experts.1.partial_ref = f32[256,2048]{1,0:T(8,128)S(1)} custom-call(bf16[256,1152]{1,0:T(8,128)(2,1)S(1)} %constant_dynamic-update-slice_fusion.mine_ref, f32[1,2048]{1,0:T(1,128)S(1)} %bitcast.3, bf16[2,2048,512]{2,1,0:T(8,128)(2,1)S(1)} %load_weights.3.gate_ref, bf16[2,2048,512]{2,1,0:T(8,128)(2,1)S(1)} %load_weights.4.up_ref), custom_call_target="tpu_custom_call" | custom-call | tf_op jit(solution)/shard_map/start_experts/pallas_call | solution.py:444
  28.7 0.7 %collective-permute-done.8.other_ref = bf16[256,1152]{1,0:T(8,128)(2,1)S(1)} collective-permute-done((bf16[256,1152]{1,0:T(8,128)(2,1)S(1)}, bf16[256,1152]{1,0:T(8,128)(2,1)S(1)}, u32[]{:S(2)}, u32[]{:S(2)}) %collective-permute-start.8) | collective-permute-done | bytes 589856 | tf_op jit(solution)/shard_map/ppermute | solution.py:532
  29.4 1.5 %finish_experts.2 = (f32[64,2048]{1,0:T(8,128)S(1)}, bf16[64,2048]{1,0:T(8,128)(2,1)S(1)}) custom-call(bf16[256,1152]{1,0:T(8,128)(2,1)S(1)} %constant_dynamic-update-slice_fusion.mine_ref, bf16[256,1152]{1,0:T(8,128)(2,1)S(1)} %collective-permute-done.8.other_ref, f32[256,2048]{1,0:T(8,128)S(1)} %start_experts.1.partial_ref, f32[1,2048]{1,0:T(1,128)S(1)} %bitcast.4, ...), custom_call_target="tpu_custom_call" | custom-call | tf_op jit(solution)/shard_map/finish_experts/pallas_call | solution.py:465
  30.8 0.2 collective-permute-start.9
  31.0 1.5 %finish_experts.3 = (f32[64,2048]{1,0:T(8,128)S(1)}, bf16[64,2048]{1,0:T(8,128)(2,1)S(1)}, bf16[32,1024]{1,0:T(8,128)(2,1)S(1)}) custom-call(bf16[256,1152]{1,0:T(8,128)(2,1)S(1)} %constant_dynamic-update-slice_fusion.mine_ref, bf16[256,1152]{1,0:T(8,128)(2,1)S(1)} %collective-permute-done.8.other_ref, f32[256,2048]{1,0:T(8,128)S(1)} %start_experts.1.partial_ref, ...), custom_call_target="tpu_custom_call" | custom-call | tf_op jit(solution)/shard_map/finish_experts/pallas_call | solution.py:465
  32.5 0.4 collective-permute-start.14
  32.9 0.0 collective-permute-done.9.back
  33.0 1.6 %collective-permute-start.10 = (bf16[32,1024]{1,0:T(8,128)(2,1)S(1)}, bf16[32,1024]{1,0:T(8,128)(2,1)S(1)}, u32[]{:S(2)}, u32[]{:S(2)}) collective-permute-start(bf16[32,1024]{1,0:T(8,128)(2,1)S(1)} %get-tuple-element.66), channel_id=1, source_target_pairs={{0,2},{2,0},{1,3},{3,1},{4,6},{6,4},{5,7},{7,5},{8,10},{10,8},{9,1... | collective-permute-start | bytes 196616 | tf_op jit(solution)/shard_map/ppermute | solution.py:532
  34.5 0.5 %collective-permute-start.12 = (bf16[32,1024]{1,0:T(8,128)(2,1)S(1)}, bf16[32,1024]{1,0:T(8,128)(2,1)S(1)}, u32[]{:S(2)}, u32[]{:S(2)}) collective-permute-start(bf16[32,1024]{1,0:T(8,128)(2,1)S(1)} %get-tuple-element.68), channel_id=1, source_target_pairs={{0,2},{2,0},{1,3},{3,1},{4,6},{6,4},{5,7},{7,5},{8,10},{10,8},{9,1... | collective-permute-start | bytes 196616 | tf_op jit(solution)/shard_map/ppermute | solution.py:532
  35.1 0.0 collective-permute-done.14.back
  35.1 0.7 %collective-permute-start.15 = (bf16[32,2048]{1,0:T(8,128)(2,1)S(1)}, bf16[32,2048]{1,0:T(8,128)(2,1)S(1)}, u32[]{:S(2)}, u32[]{:S(2)}) collective-permute-start(bf16[32,2048]{1,0:T(8,128)(2,1)S(1)} %get-tuple-element.72), channel_id=1, source_target_pairs={{0,4},{4,0},{8,12},{12,8},{1,5},{5,1},{9,13},{13,9},{2,6},{6,2},{1... | collective-permute-start | bytes 393224 | tf_op jit(solution)/shard_map/ppermute | solution.py:532
  35.9 1.9 %collective-permute-done.10 = bf16[32,1024]{1,0:T(8,128)(2,1)S(1)} collective-permute-done((bf16[32,1024]{1,0:T(8,128)(2,1)S(1)}, bf16[32,1024]{1,0:T(8,128)(2,1)S(1)}, u32[]{:S(2)}, u32[]{:S(2)}) %collective-permute-start.10) | collective-permute-done | bytes 65568 | tf_op jit(solution)/shard_map/ppermute | solution.py:532
  37.8 2.5 %collective-permute-start.11 = (bf16[32,1024]{1,0:T(8,128)(2,1)S(1)}, bf16[32,1024]{1,0:T(8,128)(2,1)S(1)}, u32[]{:S(2)}, u32[]{:S(2)}) collective-permute-start(bf16[32,1024]{1,0:T(8,128)(2,1)S(1)} %add_convert_fusion.2), channel_id=1, source_target_pairs={{0,8},{4,12},{8,0},{12,4},{1,9},{5,13},{9,1},{13,5},{2,10},{6,14},... | collective-permute-start | bytes 196616 | tf_op jit(solution)/shard_map/ppermute | solution.py:532
  40.3 0.0 collective-permute-done.12
  40.3 1.9 %collective-permute-start.13 = (bf16[32,1024]{1,0:T(8,128)(2,1)S(1)}, bf16[32,1024]{1,0:T(8,128)(2,1)S(1)}, u32[]{:S(2)}, u32[]{:S(2)}) collective-permute-start(bf16[32,1024]{1,0:T(8,128)(2,1)S(1)} %add_convert_fusion.1), channel_id=1, source_target_pairs={{0,12},{4,8},{8,4},{12,0},{1,13},{5,9},{9,5},{13,1},{2,14},{6,10},... | collective-permute-start | bytes 196616 | tf_op jit(solution)/shard_map/ppermute | solution.py:532
  42.2 0.0 collective-permute-done.15.back
  42.3 1.0 %collective-permute-start.16 = (bf16[32,1024]{1,0:T(8,128)(2,1)S(1)}, bf16[32,1024]{1,0:T(8,128)(2,1)S(1)}, u32[]{:S(2)}, u32[]{:S(2)}) collective-permute-start(bf16[32,1024]{1,0:T(8,128)(2,1)S(1)} %get-tuple-element.74), channel_id=1, source_target_pairs={{0,2},{2,0},{1,3},{3,1},{4,6},{6,4},{5,7},{7,5},{8,10},{10,8},{9,1... | collective-permute-start | bytes 196616 | tf_op jit(solution)/shard_map/ppermute | solution.py:532
  43.3 1.7 %collective-permute-done.11 = bf16[32,1024]{1,0:T(8,128)(2,1)S(1)} collective-permute-done((bf16[32,1024]{1,0:T(8,128)(2,1)S(1)}, bf16[32,1024]{1,0:T(8,128)(2,1)S(1)}, u32[]{:S(2)}, u32[]{:S(2)}) %collective-permute-start.11) | collective-permute-done | bytes 65568 | tf_op jit(solution)/shard_map/ppermute | solution.py:532
  45.0 1.5 %collective-permute-done.13 = bf16[32,1024]{1,0:T(8,128)(2,1)S(1)} collective-permute-done((bf16[32,1024]{1,0:T(8,128)(2,1)S(1)}, bf16[32,1024]{1,0:T(8,128)(2,1)S(1)}, u32[]{:S(2)}, u32[]{:S(2)}) %collective-permute-start.13) | collective-permute-done | bytes 65568 | tf_op jit(solution)/shard_map/ppermute | solution.py:532
  46.5 0.0 collective-permute-done.16
  46.6 0.6 %add_convert_fusion = bf16[32,1024]{1,0:T(8,128)(2,1)} fusion(bf16[32,1024]{1,0:T(8,128)(2,1)S(1)} %collective-permute-done.16, f32[32,1024]{1,0:T(8,128)S(1)} %convert_add_fusion, f32[32,1024]{1,0:T(8,128)S(1)} %get-tuple-element.73), kind=kLoop, calls=%fused_computation.1 | loop fusion | flops 131072 | bytes 393216 | tf_op jit(solution)/shard_map/convert_element_type | solution.py:620
  (16 shorter events, 0.3 us)
Async XLA Ops:
  4.9 1.6 %collective-permute-start = (bf16[32,3200]{1,0:T(8,128)(2,1)S(1)}, bf16[32,3200]{1,0:T(8,128)(2,1)S(1)}, u32[]{:S(2)}, u32[]{:S(2)}) collective-permute-start(bf16[32,3200]{1,0:T(8,128)(2,1)S(1)} %get-tuple-element.40.packed_ref), channel_id=1, source_target_pairs={{0,1},{1,0},{2,3},{3,2},{4,5},{5,4},{6,7},{7,6},{8,9},{9,8},{10,11... | collective-permute-start | bytes 614408 | tf_op jit(solution)/shard_map/ppermute | solution.py:532
  7.4 5.3 %collective-permute-start.1 = (bf16[32,1024]{1,0:T(8,128)(2,1)S(1)}, bf16[32,1024]{1,0:T(8,128)(2,1)S(1)}, u32[]{:S(2)}, u32[]{:S(2)}) collective-permute-start(bf16[32,1024]{1,0:T(8,128)(2,1)S(1)} %get-tuple-element.44), channel_id=1, source_target_pairs={{0,2},{2,0},{1,3},{3,1},{4,6},{6,4},{5,7},{7,5},{8,10},{10,8},{9,1... | collective-permute-start | bytes 196616 | tf_op jit(solution)/shard_map/ppermute | solution.py:532
  12.6 4.6 %collective-permute-start.2 = (bf16[32,1024]{1,0:T(8,128)(2,1)S(1)}, bf16[32,1024]{1,0:T(8,128)(2,1)S(1)}, u32[]{:S(2)}, u32[]{:S(2)}) collective-permute-start(bf16[32,1024]{1,0:T(8,128)(2,1)S(1)} %get-tuple-element.49), channel_id=1, source_target_pairs={{0,2},{2,0},{1,3},{3,1},{4,6},{6,4},{5,7},{7,5},{8,10},{10,8},{9,1... | collective-permute-start | bytes 196616 | tf_op jit(solution)/shard_map/ppermute | solution.py:532
  12.8 8.0 %collective-permute-start.3 = (bf16[32,1152]{1,0:T(8,128)(2,1)S(1)}, bf16[32,1152]{1,0:T(8,128)(2,1)S(1)}, u32[]{:S(2)}, u32[]{:S(2)}) collective-permute-start(bf16[32,1152]{1,0:T(8,128)(2,1)S(1)} %get-tuple-element.75), channel_id=1, source_target_pairs={{0,8},{4,12},{8,0},{12,4},{1,9},{5,13},{9,1},{13,5},{2,10},{6,14},... | collective-permute-start | bytes 221192 | tf_op jit(solution)/shard_map/ppermute | solution.py:532
  15.9 7.0 %collective-permute-start.5 = (bf16[32,1152]{1,0:T(8,128)(2,1)S(1)}, bf16[32,1152]{1,0:T(8,128)(2,1)S(1)}, u32[]{:S(2)}, u32[]{:S(2)}) collective-permute-start(bf16[32,1152]{1,0:T(8,128)(2,1)S(1)} %get-tuple-element.75), channel_id=1, source_target_pairs={{0,12},{4,8},{8,4},{12,0},{1,13},{5,9},{9,5},{13,1},{2,14},{6,10},... | collective-permute-start | bytes 221192 | tf_op jit(solution)/shard_map/ppermute | solution.py:532
  17.2 9.3 %collective-permute-start.7 = (bf16[64,1152]{1,0:T(8,128)(2,1)S(1)}, bf16[64,1152]{1,0:T(8,128)(2,1)S(1)}, u32[]{:S(2)}, u32[]{:S(2)}) collective-permute-start(bf16[64,1152]{1,0:T(8,128)(2,1)S(1)} %maximum_maximum_fusion), channel_id=1, source_target_pairs={{0,4},{4,0},{8,12},{12,8},{1,5},{5,1},{9,13},{13,9},{2,6},{6,2},{1... | collective-permute-start | bytes 442376 | tf_op jit(solution)/shard_map/ppermute | solution.py:532
  20.8 5.8 %collective-permute-start.4 = (bf16[32,1152]{1,0:T(8,128)(2,1)S(1)}, bf16[32,1152]{1,0:T(8,128)(2,1)S(1)}, u32[]{:S(2)}, u32[]{:S(2)}) collective-permute-start(bf16[32,1152]{1,0:T(8,128)(2,1)S(1)} %collective-permute-done.3), channel_id=1, source_target_pairs={{0,2},{2,0},{1,3},{3,1},{4,6},{6,4},{5,7},{7,5},{8,10},{10,8},{9,1... | collective-permute-start | bytes 221192 | tf_op jit(solution)/shard_map/ppermute | solution.py:532
  22.8 4.4 %collective-permute-start.6 = (bf16[32,1152]{1,0:T(8,128)(2,1)S(1)}, bf16[32,1152]{1,0:T(8,128)(2,1)S(1)}, u32[]{:S(2)}, u32[]{:S(2)}) collective-permute-start(bf16[32,1152]{1,0:T(8,128)(2,1)S(1)} %collective-permute-done.5), channel_id=1, source_target_pairs={{0,2},{2,0},{1,3},{3,1},{4,6},{6,4},{5,7},{7,5},{8,10},{10,8},{9,1... | collective-permute-start | bytes 221192 | tf_op jit(solution)/shard_map/ppermute | solution.py:532
  24.3 3.0 %copy-start = (f32[2048]{0:T(1024)S(1)}, f32[2048]{0:T(1024)}, u32[]{:S(2)}) copy-start(f32[2048]{0:T(1024)} %param.22) | copy-start | bytes 24580
  27.3 2.1 %collective-permute-start.8 = (bf16[256,1152]{1,0:T(8,128)(2,1)S(1)}, bf16[256,1152]{1,0:T(8,128)(2,1)S(1)}, u32[]{:S(2)}, u32[]{:S(2)}) collective-permute-start(bf16[256,1152]{1,0:T(8,128)(2,1)S(1)} %constant_dynamic-update-slice_fusion.mine_ref), channel_id=1, source_target_pairs={{0,1},{1,0},{2,3},{3,2},{4,5},{5,4},{6,7},{7,6},{8,9},{9,8},{10,11... | collective-permute-start | bytes 1769480 | tf_op jit(solution)/shard_map/ppermute | solution.py:532
  30.8 2.1 %collective-permute-start.9 = (bf16[64,2048]{1,0:T(8,128)(2,1)S(1)}, bf16[64,2048]{1,0:T(8,128)(2,1)S(1)}, u32[]{:S(2)}, u32[]{:S(2)}) collective-permute-start(bf16[64,2048]{1,0:T(8,128)(2,1)S(1)} %get-tuple-element.64), channel_id=1, source_target_pairs={{0,1},{1,0},{2,3},{3,2},{4,5},{5,4},{6,7},{7,6},{8,9},{9,8},{10,11... | collective-permute-start | bytes 786440 | tf_op jit(solution)/shard_map/ppermute | solution.py:532
  32.5 2.6 %collective-permute-start.14 = (bf16[64,2048]{1,0:T(8,128)(2,1)S(1)}, bf16[64,2048]{1,0:T(8,128)(2,1)S(1)}, u32[]{:S(2)}, u32[]{:S(2)}) collective-permute-start(bf16[64,2048]{1,0:T(8,128)(2,1)S(1)} %get-tuple-element.70), channel_id=1, source_target_pairs={{0,1},{1,0},{2,3},{3,2},{4,5},{5,4},{6,7},{7,6},{8,9},{9,8},{10,11... | collective-permute-start | bytes 786440 | tf_op jit(solution)/shard_map/ppermute | solution.py:532
  33.0 4.7 %collective-permute-start.10 = (bf16[32,1024]{1,0:T(8,128)(2,1)S(1)}, bf16[32,1024]{1,0:T(8,128)(2,1)S(1)}, u32[]{:S(2)}, u32[]{:S(2)}) collective-permute-start(bf16[32,1024]{1,0:T(8,128)(2,1)S(1)} %get-tuple-element.66), channel_id=1, source_target_pairs={{0,2},{2,0},{1,3},{3,1},{4,6},{6,4},{5,7},{7,5},{8,10},{10,8},{9,1... | collective-permute-start | bytes 196616 | tf_op jit(solution)/shard_map/ppermute | solution.py:532
  34.5 5.7 %collective-permute-start.12 = (bf16[32,1024]{1,0:T(8,128)(2,1)S(1)}, bf16[32,1024]{1,0:T(8,128)(2,1)S(1)}, u32[]{:S(2)}, u32[]{:S(2)}) collective-permute-start(bf16[32,1024]{1,0:T(8,128)(2,1)S(1)} %get-tuple-element.68), channel_id=1, source_target_pairs={{0,2},{2,0},{1,3},{3,1},{4,6},{6,4},{5,7},{7,5},{8,10},{10,8},{9,1... | collective-permute-start | bytes 196616 | tf_op jit(solution)/shard_map/ppermute | solution.py:532
  35.1 7.1 %collective-permute-start.15 = (bf16[32,2048]{1,0:T(8,128)(2,1)S(1)}, bf16[32,2048]{1,0:T(8,128)(2,1)S(1)}, u32[]{:S(2)}, u32[]{:S(2)}) collective-permute-start(bf16[32,2048]{1,0:T(8,128)(2,1)S(1)} %get-tuple-element.72), channel_id=1, source_target_pairs={{0,4},{4,0},{8,12},{12,8},{1,5},{5,1},{9,13},{13,9},{2,6},{6,2},{1... | collective-permute-start | bytes 393224 | tf_op jit(solution)/shard_map/ppermute | solution.py:532
  37.8 7.3 %collective-permute-start.11 = (bf16[32,1024]{1,0:T(8,128)(2,1)S(1)}, bf16[32,1024]{1,0:T(8,128)(2,1)S(1)}, u32[]{:S(2)}, u32[]{:S(2)}) collective-permute-start(bf16[32,1024]{1,0:T(8,128)(2,1)S(1)} %add_convert_fusion.2), channel_id=1, source_target_pairs={{0,8},{4,12},{8,0},{12,4},{1,9},{5,13},{9,1},{13,5},{2,10},{6,14},... | collective-permute-start | bytes 196616 | tf_op jit(solution)/shard_map/ppermute | solution.py:532
  40.3 6.2 %collective-permute-start.13 = (bf16[32,1024]{1,0:T(8,128)(2,1)S(1)}, bf16[32,1024]{1,0:T(8,128)(2,1)S(1)}, u32[]{:S(2)}, u32[]{:S(2)}) collective-permute-start(bf16[32,1024]{1,0:T(8,128)(2,1)S(1)} %add_convert_fusion.1), channel_id=1, source_target_pairs={{0,12},{4,8},{8,4},{12,0},{1,13},{5,9},{9,5},{13,1},{2,14},{6,10},... | collective-permute-start | bytes 196616 | tf_op jit(solution)/shard_map/ppermute | solution.py:532
  42.3 4.3 %collective-permute-start.16 = (bf16[32,1024]{1,0:T(8,128)(2,1)S(1)}, bf16[32,1024]{1,0:T(8,128)(2,1)S(1)}, u32[]{:S(2)}, u32[]{:S(2)}) collective-permute-start(bf16[32,1024]{1,0:T(8,128)(2,1)S(1)} %get-tuple-element.74), channel_id=1, source_target_pairs={{0,2},{2,0},{1,3},{3,1},{4,6},{6,4},{5,7},{7,5},{8,10},{10,8},{9,1... | collective-permute-start | bytes 196616 | tf_op jit(solution)/shard_map/ppermute | solution.py:532

commit v5 on v4

--- a/solution.py
+++ b/solution.py
@@ -370,9 +370,10 @@
     )
 
 
-def place_rows(source_ref, target_ref, segments, first, columns, table_ref=None):
+def place_rows(source_refs, target_ref, segments, first, columns, table_ref=None):
     half, rows = columns.size, target_ref.shape[0]
-    for source, m, start, flip in segments:
+    pieces = [(ref, *piece) for ref, group in zip(source_refs, segments) for piece in group]
+    for source_ref, source, m, start, flip in pieces:
         at = pl.multiple_of(start + (lax.axis_index("tp") ^ flip) * m, m)
         own, others = pl.ds(at, m), pl.ds(rows // 2 + at, m)
         upper, lower = slice(source, source + m), slice(source + m, source + 2 * m)
@@ -382,9 +383,10 @@
                 table_ref[to, :] = source_ref[at, half:].astype(f32)
 
 
-def start_kernel(segments, mine_ref, gain_ref, gate_ref, up_ref, partial_ref, rows_ref):
+def start_kernel(segments, *refs):
+    *mine, gain_ref, gate_ref, up_ref, partial_ref, rows_ref = refs
     half, hidden = rows_ref.shape[1], gate_ref.shape[2]
-    place_rows(mine_ref, rows_ref, segments, True, pl.ds(0, half))
+    place_rows(mine, rows_ref, segments, True, pl.ds(0, half))
     at = pl.ds(pl.multiple_of(lax.axis_index("sp") * half, LANES), half)
     scaled = (rows_ref[...].astype(f32) * gain_ref[:, at]).astype(bf16)
     for e in range(gate_ref.shape[0]):
@@ -394,17 +396,19 @@
 
 
 def finish_kernel(
-    experts, first_of, segments, window, mine_ref, other_ref, partial_ref, gain_ref, gate_ref,
-    up_ref, down_ref, keep_ref, send_ref, *refs
+    experts, first_of, segments, window, *refs
 ):
+    count = len(segments)
+    mine, other = refs[:count], refs[count : 2 * count]
+    partial_ref, gain_ref, gate_ref, up_ref, down_ref, keep_ref, send_ref, *refs = refs[2 * count :]
     *stream_ref, rows_ref, table_ref = refs
     rows, width = rows_ref.shape
     half, hidden = width // 2, gate_ref.shape[2]
     sp_index = lax.axis_index("sp")
     my_cols = pl.ds(pl.multiple_of(sp_index * half, LANES), half)
     other_cols = pl.ds(pl.multiple_of((1 - sp_index) * half, LANES), half)
-    place_rows(mine_ref, rows_ref, segments, True, my_cols, table_ref)
-    place_rows(other_ref, rows_ref, segments, False, other_cols)
+    place_rows(mine, rows_ref, segments, True, my_cols, table_ref)
+    place_rows(other, rows_ref, segments, False, other_cols)
     for out_ref in stream_ref:
         count, cut = out_ref.shape
         at = pl.ds(pl.multiple_of(lax.axis_index("tp") * cut, LANES), cut)
@@ -440,17 +444,17 @@
 
 
 def start_experts(mine, segments, gain, gate, up):
-    rows = mine.shape[0]
+    rows = sum(array.shape[0] for array in mine)
     return pl.pallas_call(
         functools.partial(start_kernel, segments),
-        in_specs=[WHOLE] * 4,
+        in_specs=[WHOLE] * (len(mine) + 3),
         out_specs=WHOLE,
         out_shape=pltpu.VMEM((rows, 2 * gate.shape[0] * gate.shape[2]), f32),
         scratch_shapes=[pltpu.VMEM((rows, gain.shape[1] // 2), bf16)],
         compiler_params=pltpu.CompilerParams(vmem_limit_bytes=12 * MIB),
         cost_estimate=FREE,
         name="start_experts",
-    )(in_vmem(mine), gain, in_vmem(gate), in_vmem(up))
+    )(*map(in_vmem, mine), gain, in_vmem(gate), in_vmem(up))
 
 
 def finish_experts(
@@ -458,15 +462,18 @@
 ):
     width, local = gain.shape[1], gate.shape[0]
     segments = tuple(
-        (source, m, start - window, flip)
-        for source, m, start, flip in segments
-        if window <= start < window + count
+        tuple(
+            (source, m, start - window, flip)
+            for source, m, start, flip in group
+            if window <= start < window + count
+        )
+        for group in segments
     )
     return pl.pallas_call(
         functools.partial(
             finish_kernel, experts, lambda e, s: (e * n_sp + s) * local, segments, window
         ),
-        in_specs=[WHOLE] * 7,
+        in_specs=[WHOLE] * (2 * len(mine) + 5),
         out_specs=[WHOLE] * (3 if stream_shape else 2),
         out_shape=[
             pltpu.VMEM((count, width), f32),
@@ -475,12 +482,12 @@
         ],
         scratch_shapes=[
             pltpu.VMEM((2 * count, width), bf16),
-            pltpu.VMEM((2 * count, mine.shape[1] - width // 2), f32),
+            pltpu.VMEM((2 * count, mine[0].shape[1] - width // 2), f32),
         ],
         compiler_params=pltpu.CompilerParams(vmem_limit_bytes=12 * MIB),
         cost_estimate=FREE,
         name="finish_experts",
-    )(in_vmem(mine), in_vmem(other), in_vmem(partial), gain, *map(in_vmem, (gate, up, down)))
+    )(*map(in_vmem, (*mine, *other, partial)), gain, *map(in_vmem, (gate, up, down)))
 
 
 def split_kernel(keep, back, *out_refs):
@@ -583,18 +590,18 @@
         second_far, third_far = swap(second, "tp"), swap(third, "tp")
         w_down, _, _ = lax.optimization_barrier((w_down, second, third))
         (w_down,) = load(w_down)
-        second_far, third_far, next_chip, w_down = lax.optimization_barrier(
-            (second_far, third_far, next_chip, w_down)
-        )
-        mine = jnp.concatenate(
-            [chip, next_chip, second, third, second_far, third_far], axis=0
-        )
-        other = swap(mine, "sp")
+        next_chip, w_down = lax.optimization_barrier((next_chip, w_down))
+        second_far, third_far, w_down = lax.optimization_barrier((second_far, third_far, w_down))
+        near = jnp.concatenate([chip, next_chip, second, third], axis=0)
+        far = jnp.concatenate([second_far, third_far], axis=0)
+        mine = (near, far)
+        other = (swap(near, "sp"), swap(far, "sp"))
         size = 2 * part
         segments = tuple(
-            (i * size, part, k * rows, flip)
-            for i, (k, flip) in enumerate(
-                [(0, 0), (0, 1), (1, 0), (1, 1), (2, 0), (3, 0), (2, 1), (3, 1)]
+            tuple((i * size, part, k * rows, flip) for i, (k, flip) in enumerate(blocks))
+            for blocks in (
+                [(0, 0), (0, 1), (1, 0), (1, 1), (2, 0), (3, 0)],
+                [(2, 1), (3, 1)],
             )
         )
         gain = norm_gain.reshape(1, width)

time: 47.4 us -> 47.4 us (level)
  starting transfers between devices: 21.1 us -> 21.7 us
  waiting for transfers between devices: 8.33 us -> 7.74 us
    ppermute x17 -> x18, waiting for transfers between devices: 8.33 us -> 7.74 us  [swap(): return lax.ppermute(array, axis, [(i, i ^ by) for i in range(size)])]
    ppermute x17 -> x18, starting transfers between devices: 21.1 us -> 21.7 us  [swap(): return lax.ppermute(array, axis, [(i, i ^ by) for i in range(size)])]
  transfers between devices with their start and end apart: 17 -> 18, of which waited for: 8 -> 8; matrix products, arithmetic and copies ran while one was open for 0% -> 0% of each run, Pallas kernels for 20% -> 20%
where the time goes in v5:
time: 47.4 us; the launch traced here: 47.2 us
  starting transfers between devices  21.7 us (46%)
  Pallas kernels  16.7 us (35%)
  waiting for transfers between devices  7.74 us (16%)
  other arithmetic  0.79 us (2%)
    ppermute x18, starting transfers between devices, swap(): return lax.ppermute(array, axis, [(i, i ^ by) for i in range(size)])  21.7 us
    ppermute x18, waiting for transfers between devices, swap(): return lax.ppermute(array, axis, [(i, i ^ by) for i in range(size)])  7.74 us
    pallas_call x3, Pallas kernels, load(): pl.pallas_call(load_kernel, in_specs=[ANYWHERE] * len(arrays), out_specs=...  6.59 us
    pallas_call x1, Pallas kernels, attend(): pl.pallas_call(functools.partial(attention_kernel, kv_count, per_group, c...  4.91 us
    pallas_call x2, Pallas kernels, finish_experts(): pl.pallas_call(functools.partial(finish_kernel, experts, lambda e, s: (e...  2.91 us
    pallas_call x1, Pallas kernels, start_experts(): pl.pallas_call(functools.partial(start_kernel, segments), in_specs=[WHOLE...  1.26 us
  transfers between devices with their start and end apart: 18, of which 8 were waited for; matrix products, arithmetic and copies ran while one was open for 0% of the time, Pallas kernels for 20%

profile of v5, /device:TPU:0, one launch (start us, length us, event | category | flops | bytes accessed | tf_op | source)
XLA Modules:
  0.0 47.2 jit_solution(9767847511606901410)
XLA Ops:
  0.0 4.9 %attention.1 = (bf16[32,3200]{1,0:T(8,128)(2,1)S(1)}, bf16[32,1024]{1,0:T(8,128)(2,1)S(1)}, bf16[2048,1024]{1,0:T(8,128)(2,1)S(1)}) custom-call(s32[32]{0:T(128)} %lengths_hbm.1, bf16[32,2048]{1,0:T(8,128)(2,1)} %query_hbm.1, bf16[32,256,512]{2,1,0:T(8,128)(2,1)} %key_hbm.1, bf16[32,256,512]{2,1,0:T(8,128)(2,1)} %value_hbm.1, bf16[32,512]{1,0:T(8,128)(2,1)} %new_key_hbm.1, ...), custom_call_target="tpu_custom_call" | custom-call | tf_op jit(solution)/shard_map/attention/pallas_call | solution.py:182
  4.9 0.5 %collective-permute-start = (bf16[32,3200]{1,0:T(8,128)(2,1)S(1)}, bf16[32,3200]{1,0:T(8,128)(2,1)S(1)}, u32[]{:S(2)}, u32[]{:S(2)}) collective-permute-start(bf16[32,3200]{1,0:T(8,128)(2,1)S(1)} %get-tuple-element.41.packed_ref), channel_id=1, source_target_pairs={{0,1},{1,0},{2,3},{3,2},{4,5},{5,4},{6,7},{7,6},{8,9},{9,8},{10,11... | collective-permute-start | bytes 614408 | tf_op jit(solution)/shard_map/ppermute | solution.py:539
  5.4 1.1 %collective-permute-done.other_ref = bf16[32,3200]{1,0:T(8,128)(2,1)S(1)} collective-permute-done((bf16[32,3200]{1,0:T(8,128)(2,1)S(1)}, bf16[32,3200]{1,0:T(8,128)(2,1)S(1)}, u32[]{:S(2)}, u32[]{:S(2)}) %collective-permute-start) | collective-permute-done | bytes 204832 | tf_op jit(solution)/shard_map/ppermute | solution.py:539
  6.5 0.9 %project.1 = (bf16[32,1024]{1,0:T(8,128)(2,1)S(1)}, bf16[32,1024]{1,0:T(8,128)(2,1)S(1)}, f32[32,1024]{1,0:T(8,128)S(1)}, f32[32,1024]{1,0:T(8,128)S(1)}, bf16[3...) custom-call(bf16[32,3200]{1,0:T(8,128)(2,1)S(1)} %get-tuple-element.41.packed_ref, ...), custom_call_target="tpu_custom_call" | custom-call | tf_op jit(solution)/shard_map/project/pallas_call | solution.py:239
  7.4 2.9 %collective-permute-start.1 = (bf16[32,1024]{1,0:T(8,128)(2,1)S(1)}, bf16[32,1024]{1,0:T(8,128)(2,1)S(1)}, u32[]{:S(2)}, u32[]{:S(2)}) collective-permute-start(bf16[32,1024]{1,0:T(8,128)(2,1)S(1)} %get-tuple-element.45), channel_id=1, source_target_pairs={{0,2},{2,0},{1,3},{3,1},{4,6},{6,4},{5,7},{7,5},{8,10},{10,8},{9,1... | collective-permute-start | bytes 196616 | tf_op jit(solution)/shard_map/ppermute | solution.py:539
  10.3 2.2 %load_weights.3.refs_3_.refs_6_ = bf16[2,2048,512]{2,1,0:T(8,128)(2,1)S(1)} custom-call(bf16[2,2048,512]{2,1,0:T(8,128)(2,1)} %refs_0_), custom_call_target="tpu_custom_call" | custom-call | tf_op jit(solution)/shard_map/load_weights/pallas_call | solution.py:268
  12.6 0.1 collective-permute-start.2
  12.6 0.1 collective-permute-done.1
  12.8 3.1 %collective-permute-start.4 = (bf16[32,1152]{1,0:T(8,128)(2,1)S(1)}, bf16[32,1152]{1,0:T(8,128)(2,1)S(1)}, u32[]{:S(2)}, u32[]{:S(2)}) collective-permute-start(bf16[32,1152]{1,0:T(8,128)(2,1)S(1)} %get-tuple-element.77), channel_id=1, source_target_pairs={{0,8},{4,12},{8,0},{12,4},{1,9},{5,13},{9,1},{13,5},{2,10},{6,14},... | collective-permute-start | bytes 221192 | tf_op jit(solution)/shard_map/ppermute | solution.py:539
  15.9 1.3 %collective-permute-start.5 = (bf16[32,1152]{1,0:T(8,128)(2,1)S(1)}, bf16[32,1152]{1,0:T(8,128)(2,1)S(1)}, u32[]{:S(2)}, u32[]{:S(2)}) collective-permute-start(bf16[32,1152]{1,0:T(8,128)(2,1)S(1)} %get-tuple-element.77), channel_id=1, source_target_pairs={{0,12},{4,8},{8,4},{12,0},{1,13},{5,9},{9,5},{13,1},{2,14},{6,10},... | collective-permute-start | bytes 221192 | tf_op jit(solution)/shard_map/ppermute | solution.py:539
  17.2 0.0 collective-permute-done.2
  17.2 1.3 %collective-permute-start.3 = (bf16[64,1152]{1,0:T(8,128)(2,1)S(1)}, bf16[64,1152]{1,0:T(8,128)(2,1)S(1)}, u32[]{:S(2)}, u32[]{:S(2)}) collective-permute-start(bf16[64,1152]{1,0:T(8,128)(2,1)S(1)} %maximum_maximum_fusion), channel_id=1, source_target_pairs={{0,4},{4,0},{8,12},{12,8},{1,5},{5,1},{9,13},{13,9},{2,6},{6,2},{1... | collective-permute-start | bytes 442376 | tf_op jit(solution)/shard_map/ppermute | solution.py:539
  18.6 2.2 %load_weights.4.refs_4_.refs_7_ = bf16[2,2048,512]{2,1,0:T(8,128)(2,1)S(1)} custom-call(bf16[2,2048,512]{2,1,0:T(8,128)(2,1)} %refs_0_.1), custom_call_target="tpu_custom_call" | custom-call | tf_op jit(solution)/shard_map/load_weights/pallas_call | solution.py:268
  20.8 0.0 collective-permute-done.4
  20.8 1.4 %collective-permute-start.6 = (bf16[32,1152]{1,0:T(8,128)(2,1)S(1)}, bf16[32,1152]{1,0:T(8,128)(2,1)S(1)}, u32[]{:S(2)}, u32[]{:S(2)}) collective-permute-start(bf16[32,1152]{1,0:T(8,128)(2,1)S(1)} %collective-permute-done.4), channel_id=1, source_target_pairs={{0,2},{2,0},{1,3},{3,1},{4,6},{6,4},{5,7},{7,5},{8,10},{10,8},{9,1... | collective-permute-start | bytes 221192 | tf_op jit(solution)/shard_map/ppermute | solution.py:539
  22.2 0.7 %collective-permute-done.5 = bf16[32,1152]{1,0:T(8,128)(2,1)S(1)} collective-permute-done((bf16[32,1152]{1,0:T(8,128)(2,1)S(1)}, bf16[32,1152]{1,0:T(8,128)(2,1)S(1)}, u32[]{:S(2)}, u32[]{:S(2)}) %collective-permute-start.5) | collective-permute-done | bytes 73760 | tf_op jit(solution)/shard_map/ppermute | solution.py:539
  22.8 1.5 %collective-permute-start.7 = (bf16[32,1152]{1,0:T(8,128)(2,1)S(1)}, bf16[32,1152]{1,0:T(8,128)(2,1)S(1)}, u32[]{:S(2)}, u32[]{:S(2)}) collective-permute-start(bf16[32,1152]{1,0:T(8,128)(2,1)S(1)} %collective-permute-done.5), channel_id=1, source_target_pairs={{0,2},{2,0},{1,3},{3,1},{4,6},{6,4},{5,7},{7,5},{8,10},{10,8},{9,1... | collective-permute-start | bytes 221192 | tf_op jit(solution)/shard_map/ppermute | solution.py:539
  24.3 0.0 copy-start
  24.4 2.2 %load_weights.5.refs_8_ = bf16[2,512,2048]{2,1,0:T(8,128)(2,1)S(1)} custom-call(bf16[2,512,2048]{2,1,0:T(8,128)(2,1)} %refs_0_.2), custom_call_target="tpu_custom_call" | custom-call | tf_op jit(solution)/shard_map/load_weights/pallas_call | solution.py:268
  26.6 0.0 collective-permute-done.3
  26.6 0.0 collective-permute-done.6
  26.6 0.6 %collective-permute-done.7 = bf16[32,1152]{1,0:T(8,128)(2,1)S(1)} collective-permute-done((bf16[32,1152]{1,0:T(8,128)(2,1)S(1)}, bf16[32,1152]{1,0:T(8,128)(2,1)S(1)}, u32[]{:S(2)}, u32[]{:S(2)}) %collective-permute-start.7) | collective-permute-done | bytes 73760 | tf_op jit(solution)/shard_map/ppermute | solution.py:539
  27.3 0.1 collective-permute-start.8
  27.4 0.5 %collective-permute-start.9 = (bf16[64,1152]{1,0:T(8,128)(2,1)S(1)}, bf16[64,1152]{1,0:T(8,128)(2,1)S(1)}, u32[]{:S(2)}, u32[]{:S(2)}) collective-permute-start(bf16[64,1152]{1,0:T(8,128)(2,1)S(1)} %constant_dynamic-update-slice_fusion.4.refs_1_), channel_id=1, source_target_pairs={{0,1},{1,0},{2,3},{3,2},{4,5},{5,4},{6,7},{7,6},{8,9},{9,8},{10,11... | collective-permute-start | bytes 442376 | tf_op jit(solution)/shard_map/ppermute | solution.py:539
  27.9 0.0 copy-done
  27.9 1.3 %start_experts.1.refs_4_ = f32[256,2048]{1,0:T(8,128)S(1)} custom-call(bf16[192,1152]{1,0:T(8,128)(2,1)S(1)} %constant_dynamic-update-slice_fusion.refs_0_, bf16[64,1152]{1,0:T(8,128)(2,1)S(1)} %constant_dynamic-update-slice_fusion.4.refs_1_, f32[1,2048]{1,0:T(1,128)S(1)} %bitcast.3, bf16[2,2048,512]{2,1,0:T(8,128)(2,1)S(1)} %load_weights.3.refs_3_.refs_6_, ...), custom_call_target="tpu_custom_call" | custom-call | tf_op jit(solution)/shard_map/start_experts/pallas_call | solution.py:448
  29.2 0.1 collective-permute-done.9.refs_3_
  29.3 0.0 collective-permute-done.8.refs_2_
  29.3 1.5 %finish_experts.2 = (f32[64,2048]{1,0:T(8,128)S(1)}, bf16[64,2048]{1,0:T(8,128)(2,1)S(1)}) custom-call(bf16[192,1152]{1,0:T(8,128)(2,1)S(1)} %constant_dynamic-update-slice_fusion.refs_0_, bf16[64,1152]{1,0:T(8,128)(2,1)S(1)} %constant_dynamic-update-slice_fusion.4.refs_1_, bf16[192,1152]{1,0:T(8,128)(2,1)S(1)} %collective-permute-done.8.refs_2_, ...), custom_call_target="tpu_custom_call" | custom-call | tf_op jit(solution)/shard_map/finish_experts/pallas_call | solution.py:472
  30.8 0.2 collective-permute-start.10
  31.0 1.5 %finish_experts.3 = (f32[64,2048]{1,0:T(8,128)S(1)}, bf16[64,2048]{1,0:T(8,128)(2,1)S(1)}, bf16[32,1024]{1,0:T(8,128)(2,1)S(1)}) custom-call(bf16[192,1152]{1,0:T(8,128)(2,1)S(1)} %constant_dynamic-update-slice_fusion.refs_0_, bf16[64,1152]{1,0:T(8,128)(2,1)S(1)} %constant_dynamic-update-slice_fusion.4.refs_1_, ...), custom_call_target="tpu_custom_call" | custom-call | tf_op jit(solution)/shard_map/finish_experts/pallas_call | solution.py:472
  32.5 0.4 collective-permute-start.15
  32.9 0.0 collective-permute-done.10.back
  32.9 1.6 %collective-permute-start.11 = (bf16[32,1024]{1,0:T(8,128)(2,1)S(1)}, bf16[32,1024]{1,0:T(8,128)(2,1)S(1)}, u32[]{:S(2)}, u32[]{:S(2)}) collective-permute-start(bf16[32,1024]{1,0:T(8,128)(2,1)S(1)} %get-tuple-element.68), channel_id=1, source_target_pairs={{0,2},{2,0},{1,3},{3,1},{4,6},{6,4},{5,7},{7,5},{8,10},{10,8},{9,1... | collective-permute-start | bytes 196616 | tf_op jit(solution)/shard_map/ppermute | solution.py:539
  34.5 0.5 %collective-permute-start.13 = (bf16[32,1024]{1,0:T(8,128)(2,1)S(1)}, bf16[32,1024]{1,0:T(8,128)(2,1)S(1)}, u32[]{:S(2)}, u32[]{:S(2)}) collective-permute-start(bf16[32,1024]{1,0:T(8,128)(2,1)S(1)} %get-tuple-element.70), channel_id=1, source_target_pairs={{0,2},{2,0},{1,3},{3,1},{4,6},{6,4},{5,7},{7,5},{8,10},{10,8},{9,1... | collective-permute-start | bytes 196616 | tf_op jit(solution)/shard_map/ppermute | solution.py:539
  35.0 0.0 collective-permute-done.15.back
  35.1 0.8 %collective-permute-start.16 = (bf16[32,2048]{1,0:T(8,128)(2,1)S(1)}, bf16[32,2048]{1,0:T(8,128)(2,1)S(1)}, u32[]{:S(2)}, u32[]{:S(2)}) collective-permute-start(bf16[32,2048]{1,0:T(8,128)(2,1)S(1)} %get-tuple-element.74), channel_id=1, source_target_pairs={{0,4},{4,0},{8,12},{12,8},{1,5},{5,1},{9,13},{13,9},{2,6},{6,2},{1... | collective-permute-start | bytes 393224 | tf_op jit(solution)/shard_map/ppermute | solution.py:539
  35.8 1.8 %collective-permute-done.11 = bf16[32,1024]{1,0:T(8,128)(2,1)S(1)} collective-permute-done((bf16[32,1024]{1,0:T(8,128)(2,1)S(1)}, bf16[32,1024]{1,0:T(8,128)(2,1)S(1)}, u32[]{:S(2)}, u32[]{:S(2)}) %collective-permute-start.11) | collective-permute-done | bytes 65568 | tf_op jit(solution)/shard_map/ppermute | solution.py:539
  37.7 2.5 %collective-permute-start.12 = (bf16[32,1024]{1,0:T(8,128)(2,1)S(1)}, bf16[32,1024]{1,0:T(8,128)(2,1)S(1)}, u32[]{:S(2)}, u32[]{:S(2)}) collective-permute-start(bf16[32,1024]{1,0:T(8,128)(2,1)S(1)} %add_convert_fusion.2), channel_id=1, source_target_pairs={{0,8},{4,12},{8,0},{12,4},{1,9},{5,13},{9,1},{13,5},{2,10},{6,14},... | collective-permute-start | bytes 196616 | tf_op jit(solution)/shard_map/ppermute | solution.py:539
  40.2 0.0 collective-permute-done.13
  40.2 1.9 %collective-permute-start.14 = (bf16[32,1024]{1,0:T(8,128)(2,1)S(1)}, bf16[32,1024]{1,0:T(8,128)(2,1)S(1)}, u32[]{:S(2)}, u32[]{:S(2)}) collective-permute-start(bf16[32,1024]{1,0:T(8,128)(2,1)S(1)} %add_convert_fusion.1), channel_id=1, source_target_pairs={{0,12},{4,8},{8,4},{12,0},{1,13},{5,9},{9,5},{13,1},{2,14},{6,10},... | collective-permute-start | bytes 196616 | tf_op jit(solution)/shard_map/ppermute | solution.py:539
  42.2 0.0 collective-permute-done.16.back
  42.2 1.0 %collective-permute-start.17 = (bf16[32,1024]{1,0:T(8,128)(2,1)S(1)}, bf16[32,1024]{1,0:T(8,128)(2,1)S(1)}, u32[]{:S(2)}, u32[]{:S(2)}) collective-permute-start(bf16[32,1024]{1,0:T(8,128)(2,1)S(1)} %get-tuple-element.76), channel_id=1, source_target_pairs={{0,2},{2,0},{1,3},{3,1},{4,6},{6,4},{5,7},{7,5},{8,10},{10,8},{9,1... | collective-permute-start | bytes 196616 | tf_op jit(solution)/shard_map/ppermute | solution.py:539
  43.2 1.7 %collective-permute-done.12 = bf16[32,1024]{1,0:T(8,128)(2,1)S(1)} collective-permute-done((bf16[32,1024]{1,0:T(8,128)(2,1)S(1)}, bf16[32,1024]{1,0:T(8,128)(2,1)S(1)}, u32[]{:S(2)}, u32[]{:S(2)}) %collective-permute-start.12) | collective-permute-done | bytes 65568 | tf_op jit(solution)/shard_map/ppermute | solution.py:539
  45.0 1.5 %collective-permute-done.14 = bf16[32,1024]{1,0:T(8,128)(2,1)S(1)} collective-permute-done((bf16[32,1024]{1,0:T(8,128)(2,1)S(1)}, bf16[32,1024]{1,0:T(8,128)(2,1)S(1)}, u32[]{:S(2)}, u32[]{:S(2)}) %collective-permute-start.14) | collective-permute-done | bytes 65568 | tf_op jit(solution)/shard_map/ppermute | solution.py:539
  46.5 0.0 collective-permute-done.17
  46.6 0.6 %add_convert_fusion = bf16[32,1024]{1,0:T(8,128)(2,1)} fusion(bf16[32,1024]{1,0:T(8,128)(2,1)S(1)} %collective-permute-done.17, f32[32,1024]{1,0:T(8,128)S(1)} %convert_add_fusion, f32[32,1024]{1,0:T(8,128)S(1)} %get-tuple-element.75), kind=kLoop, calls=%fused_computation.1 | loop fusion | flops 131072 | bytes 393216 | tf_op jit(solution)/shard_map/convert_element_type | solution.py:627
  (16 shorter events, 0.3 us)
Async XLA Ops:
  4.9 1.6 %collective-permute-start = (bf16[32,3200]{1,0:T(8,128)(2,1)S(1)}, bf16[32,3200]{1,0:T(8,128)(2,1)S(1)}, u32[]{:S(2)}, u32[]{:S(2)}) collective-permute-start(bf16[32,3200]{1,0:T(8,128)(2,1)S(1)} %get-tuple-element.41.packed_ref), channel_id=1, source_target_pairs={{0,1},{1,0},{2,3},{3,2},{4,5},{5,4},{6,7},{7,6},{8,9},{9,8},{10,11... | collective-permute-start | bytes 614408 | tf_op jit(solution)/shard_map/ppermute | solution.py:539
  7.4 5.3 %collective-permute-start.1 = (bf16[32,1024]{1,0:T(8,128)(2,1)S(1)}, bf16[32,1024]{1,0:T(8,128)(2,1)S(1)}, u32[]{:S(2)}, u32[]{:S(2)}) collective-permute-start(bf16[32,1024]{1,0:T(8,128)(2,1)S(1)} %get-tuple-element.45), channel_id=1, source_target_pairs={{0,2},{2,0},{1,3},{3,1},{4,6},{6,4},{5,7},{7,5},{8,10},{10,8},{9,1... | collective-permute-start | bytes 196616 | tf_op jit(solution)/shard_map/ppermute | solution.py:539
  12.6 4.6 %collective-permute-start.2 = (bf16[32,1024]{1,0:T(8,128)(2,1)S(1)}, bf16[32,1024]{1,0:T(8,128)(2,1)S(1)}, u32[]{:S(2)}, u32[]{:S(2)}) collective-permute-start(bf16[32,1024]{1,0:T(8,128)(2,1)S(1)} %get-tuple-element.50), channel_id=1, source_target_pairs={{0,2},{2,0},{1,3},{3,1},{4,6},{6,4},{5,7},{7,5},{8,10},{10,8},{9,1... | collective-permute-start | bytes 196616 | tf_op jit(solution)/shard_map/ppermute | solution.py:539
  12.8 8.0 %collective-permute-start.4 = (bf16[32,1152]{1,0:T(8,128)(2,1)S(1)}, bf16[32,1152]{1,0:T(8,128)(2,1)S(1)}, u32[]{:S(2)}, u32[]{:S(2)}) collective-permute-start(bf16[32,1152]{1,0:T(8,128)(2,1)S(1)} %get-tuple-element.77), channel_id=1, source_target_pairs={{0,8},{4,12},{8,0},{12,4},{1,9},{5,13},{9,1},{13,5},{2,10},{6,14},... | collective-permute-start | bytes 221192 | tf_op jit(solution)/shard_map/ppermute | solution.py:539
  15.9 7.0 %collective-permute-start.5 = (bf16[32,1152]{1,0:T(8,128)(2,1)S(1)}, bf16[32,1152]{1,0:T(8,128)(2,1)S(1)}, u32[]{:S(2)}, u32[]{:S(2)}) collective-permute-start(bf16[32,1152]{1,0:T(8,128)(2,1)S(1)} %get-tuple-element.77), channel_id=1, source_target_pairs={{0,12},{4,8},{8,4},{12,0},{1,13},{5,9},{9,5},{13,1},{2,14},{6,10},... | collective-permute-start | bytes 221192 | tf_op jit(solution)/shard_map/ppermute | solution.py:539
  17.2 9.3 %collective-permute-start.3 = (bf16[64,1152]{1,0:T(8,128)(2,1)S(1)}, bf16[64,1152]{1,0:T(8,128)(2,1)S(1)}, u32[]{:S(2)}, u32[]{:S(2)}) collective-permute-start(bf16[64,1152]{1,0:T(8,128)(2,1)S(1)} %maximum_maximum_fusion), channel_id=1, source_target_pairs={{0,4},{4,0},{8,12},{12,8},{1,5},{5,1},{9,13},{13,9},{2,6},{6,2},{1... | collective-permute-start | bytes 442376 | tf_op jit(solution)/shard_map/ppermute | solution.py:539
  20.8 5.8 %collective-permute-start.6 = (bf16[32,1152]{1,0:T(8,128)(2,1)S(1)}, bf16[32,1152]{1,0:T(8,128)(2,1)S(1)}, u32[]{:S(2)}, u32[]{:S(2)}) collective-permute-start(bf16[32,1152]{1,0:T(8,128)(2,1)S(1)} %collective-permute-done.4), channel_id=1, source_target_pairs={{0,2},{2,0},{1,3},{3,1},{4,6},{6,4},{5,7},{7,5},{8,10},{10,8},{9,1... | collective-permute-start | bytes 221192 | tf_op jit(solution)/shard_map/ppermute | solution.py:539
  22.8 4.4 %collective-permute-start.7 = (bf16[32,1152]{1,0:T(8,128)(2,1)S(1)}, bf16[32,1152]{1,0:T(8,128)(2,1)S(1)}, u32[]{:S(2)}, u32[]{:S(2)}) collective-permute-start(bf16[32,1152]{1,0:T(8,128)(2,1)S(1)} %collective-permute-done.5), channel_id=1, source_target_pairs={{0,2},{2,0},{1,3},{3,1},{4,6},{6,4},{5,7},{7,5},{8,10},{10,8},{9,1... | collective-permute-start | bytes 221192 | tf_op jit(solution)/shard_map/ppermute | solution.py:539
  24.3 3.6 %copy-start = (f32[2048]{0:T(1024)S(1)}, f32[2048]{0:T(1024)}, u32[]{:S(2)}) copy-start(f32[2048]{0:T(1024)} %param.22) | copy-start | bytes 24580
  27.3 2.1 %collective-permute-start.8 = (bf16[192,1152]{1,0:T(8,128)(2,1)S(1)}, bf16[192,1152]{1,0:T(8,128)(2,1)S(1)}, u32[]{:S(2)}, u32[]{:S(2)}) collective-permute-start(bf16[192,1152]{1,0:T(8,128)(2,1)S(1)} %constant_dynamic-update-slice_fusion.refs_0_), channel_id=1, source_target_pairs={{0,1},{1,0},{2,3},{3,2},{4,5},{5,4},{6,7},{7,6},{8,9},{9,8},{10,11... | collective-permute-start | bytes 1327112 | tf_op jit(solution)/shard_map/ppermute | solution.py:539
  27.4 2.0 %collective-permute-start.9 = (bf16[64,1152]{1,0:T(8,128)(2,1)S(1)}, bf16[64,1152]{1,0:T(8,128)(2,1)S(1)}, u32[]{:S(2)}, u32[]{:S(2)}) collective-permute-start(bf16[64,1152]{1,0:T(8,128)(2,1)S(1)} %constant_dynamic-update-slice_fusion.4.refs_1_), channel_id=1, source_target_pairs={{0,1},{1,0},{2,3},{3,2},{4,5},{5,4},{6,7},{7,6},{8,9},{9,8},{10,11... | collective-permute-start | bytes 442376 | tf_op jit(solution)/shard_map/ppermute | solution.py:539
  30.8 2.1 %collective-permute-start.10 = (bf16[64,2048]{1,0:T(8,128)(2,1)S(1)}, bf16[64,2048]{1,0:T(8,128)(2,1)S(1)}, u32[]{:S(2)}, u32[]{:S(2)}) collective-permute-start(bf16[64,2048]{1,0:T(8,128)(2,1)S(1)} %get-tuple-element.66), channel_id=1, source_target_pairs={{0,1},{1,0},{2,3},{3,2},{4,5},{5,4},{6,7},{7,6},{8,9},{9,8},{10,11... | collective-permute-start | bytes 786440 | tf_op jit(solution)/shard_map/ppermute | solution.py:539
  32.5 2.6 %collective-permute-start.15 = (bf16[64,2048]{1,0:T(8,128)(2,1)S(1)}, bf16[64,2048]{1,0:T(8,128)(2,1)S(1)}, u32[]{:S(2)}, u32[]{:S(2)}) collective-permute-start(bf16[64,2048]{1,0:T(8,128)(2,1)S(1)} %get-tuple-element.72), channel_id=1, source_target_pairs={{0,1},{1,0},{2,3},{3,2},{4,5},{5,4},{6,7},{7,6},{8,9},{9,8},{10,11... | collective-permute-start | bytes 786440 | tf_op jit(solution)/shard_map/ppermute | solution.py:539
  32.9 4.7 %collective-permute-start.11 = (bf16[32,1024]{1,0:T(8,128)(2,1)S(1)}, bf16[32,1024]{1,0:T(8,128)(2,1)S(1)}, u32[]{:S(2)}, u32[]{:S(2)}) collective-permute-start(bf16[32,1024]{1,0:T(8,128)(2,1)S(1)} %get-tuple-element.68), channel_id=1, source_target_pairs={{0,2},{2,0},{1,3},{3,1},{4,6},{6,4},{5,7},{7,5},{8,10},{10,8},{9,1... | collective-permute-start | bytes 196616 | tf_op jit(solution)/shard_map/ppermute | solution.py:539
  34.5 5.7 %collective-permute-start.13 = (bf16[32,1024]{1,0:T(8,128)(2,1)S(1)}, bf16[32,1024]{1,0:T(8,128)(2,1)S(1)}, u32[]{:S(2)}, u32[]{:S(2)}) collective-permute-start(bf16[32,1024]{1,0:T(8,128)(2,1)S(1)} %get-tuple-element.70), channel_id=1, source_target_pairs={{0,2},{2,0},{1,3},{3,1},{4,6},{6,4},{5,7},{7,5},{8,10},{10,8},{9,1... | collective-permute-start | bytes 196616 | tf_op jit(solution)/shard_map/ppermute | solution.py:539
  35.1 7.1 %collective-permute-start.16 = (bf16[32,2048]{1,0:T(8,128)(2,1)S(1)}, bf16[32,2048]{1,0:T(8,128)(2,1)S(1)}, u32[]{:S(2)}, u32[]{:S(2)}) collective-permute-start(bf16[32,2048]{1,0:T(8,128)(2,1)S(1)} %get-tuple-element.74), channel_id=1, source_target_pairs={{0,4},{4,0},{8,12},{12,8},{1,5},{5,1},{9,13},{13,9},{2,6},{6,2},{1... | collective-permute-start | bytes 393224 | tf_op jit(solution)/shard_map/ppermute | solution.py:539
  37.7 7.2 %collective-permute-start.12 = (bf16[32,1024]{1,0:T(8,128)(2,1)S(1)}, bf16[32,1024]{1,0:T(8,128)(2,1)S(1)}, u32[]{:S(2)}, u32[]{:S(2)}) collective-permute-start(bf16[32,1024]{1,0:T(8,128)(2,1)S(1)} %add_convert_fusion.2), channel_id=1, source_target_pairs={{0,8},{4,12},{8,0},{12,4},{1,9},{5,13},{9,1},{13,5},{2,10},{6,14},... | collective-permute-start | bytes 196616 | tf_op jit(solution)/shard_map/ppermute | solution.py:539
  40.2 6.2 %collective-permute-start.14 = (bf16[32,1024]{1,0:T(8,128)(2,1)S(1)}, bf16[32,1024]{1,0:T(8,128)(2,1)S(1)}, u32[]{:S(2)}, u32[]{:S(2)}) collective-permute-start(bf16[32,1024]{1,0:T(8,128)(2,1)S(1)} %add_convert_fusion.1), channel_id=1, source_target_pairs={{0,12},{4,8},{8,4},{12,0},{1,13},{5,9},{9,5},{13,1},{2,14},{6,10},... | collective-permute-start | bytes 196616 | tf_op jit(solution)/shard_map/ppermute | solution.py:539
  42.2 4.3 %collective-permute-start.17 = (bf16[32,1024]{1,0:T(8,128)(2,1)S(1)}, bf16[32,1024]{1,0:T(8,128)(2,1)S(1)}, u32[]{:S(2)}, u32[]{:S(2)}) collective-permute-start(bf16[32,1024]{1,0:T(8,128)(2,1)S(1)} %get-tuple-element.76), channel_id=1, source_target_pairs={{0,2},{2,0},{1,3},{3,1},{4,6},{6,4},{5,7},{7,5},{8,10},{10,8},{9,1... | collective-permute-start | bytes 196616 | tf_op jit(solution)/shard_map/ppermute | solution.py:539

commit v6 on v5

--- a/solution.py
+++ b/solution.py
@@ -586,7 +586,7 @@
         next_chip = swap(chip, "ep", 1)
         w_up, _ = lax.optimization_barrier((w_up, chip))
         (w_up,) = load(w_up)
-        second, w_up = lax.optimization_barrier((second, w_up))
+        third, w_up = lax.optimization_barrier((third, w_up))
         second_far, third_far = swap(second, "tp"), swap(third, "tp")
         w_down, _, _ = lax.optimization_barrier((w_down, second, third))
         (w_down,) = load(w_down)

time: 47.4 us -> 46.8 us (0.987)
  starting transfers between devices: 21.7 us -> 20.7 us
    ppermute x18, starting transfers between devices: 21.7 us -> 20.7 us  [swap(): return lax.ppermute(array, axis, [(i, i ^ by) for i in range(size)])]
  transfers between devices with their start and end apart: 18 -> 18, of which waited for: 8 -> 9; matrix products, arithmetic and copies ran while one was open for 0% -> 0% of each run, Pallas kernels for 20% -> 20%
where the time goes in v6:
time: 46.8 us; the launch traced here: 46.6 us
  starting transfers between devices  20.7 us (44%)
  Pallas kernels  16.7 us (36%)
  waiting for transfers between devices  8.16 us (17%)
  other arithmetic  0.79 us (2%)
    ppermute x18, starting transfers between devices, swap(): return lax.ppermute(array, axis, [(i, i ^ by) for i in range(size)])  20.7 us
    ppermute x18, waiting for transfers between devices, swap(): return lax.ppermute(array, axis, [(i, i ^ by) for i in range(size)])  8.16 us
    pallas_call x3, Pallas kernels, load(): pl.pallas_call(load_kernel, in_specs=[ANYWHERE] * len(arrays), out_specs=...  6.59 us
    pallas_call x1, Pallas kernels, attend(): pl.pallas_call(functools.partial(attention_kernel, kv_count, per_group, c...  4.91 us
    pallas_call x2, Pallas kernels, finish_experts(): pl.pallas_call(functools.partial(finish_kernel, experts, lambda e, s: (e...  2.91 us
    pallas_call x1, Pallas kernels, start_experts(): pl.pallas_call(functools.partial(start_kernel, segments), in_specs=[WHOLE...  1.26 us
  transfers between devices with their start and end apart: 18, of which 9 were waited for; matrix products, arithmetic and copies ran while one was open for 0% of the time, Pallas kernels for 20%

profile of v6, /device:TPU:0, one launch (start us, length us, event | category | flops | bytes accessed | tf_op | source)
XLA Modules:
  0.0 46.6 jit_solution(8479551524866732787)
XLA Ops:
  0.0 4.9 %attention.1 = (bf16[32,3200]{1,0:T(8,128)(2,1)S(1)}, bf16[32,1024]{1,0:T(8,128)(2,1)S(1)}, bf16[2048,1024]{1,0:T(8,128)(2,1)S(1)}) custom-call(s32[32]{0:T(128)} %lengths_hbm.1, bf16[32,2048]{1,0:T(8,128)(2,1)} %query_hbm.1, bf16[32,256,512]{2,1,0:T(8,128)(2,1)} %key_hbm.1, bf16[32,256,512]{2,1,0:T(8,128)(2,1)} %value_hbm.1, bf16[32,512]{1,0:T(8,128)(2,1)} %new_key_hbm.1, ...), custom_call_target="tpu_custom_call" | custom-call | tf_op jit(solution)/shard_map/attention/pallas_call | solution.py:182
  4.9 0.5 %collective-permute-start = (bf16[32,3200]{1,0:T(8,128)(2,1)S(1)}, bf16[32,3200]{1,0:T(8,128)(2,1)S(1)}, u32[]{:S(2)}, u32[]{:S(2)}) collective-permute-start(bf16[32,3200]{1,0:T(8,128)(2,1)S(1)} %get-tuple-element.41.packed_ref), channel_id=1, source_target_pairs={{0,1},{1,0},{2,3},{3,2},{4,5},{5,4},{6,7},{7,6},{8,9},{9,8},{10,11... | collective-permute-start | bytes 614408 | tf_op jit(solution)/shard_map/ppermute | solution.py:539
  5.4 1.1 %collective-permute-done.other_ref = bf16[32,3200]{1,0:T(8,128)(2,1)S(1)} collective-permute-done((bf16[32,3200]{1,0:T(8,128)(2,1)S(1)}, bf16[32,3200]{1,0:T(8,128)(2,1)S(1)}, u32[]{:S(2)}, u32[]{:S(2)}) %collective-permute-start) | collective-permute-done | bytes 204832 | tf_op jit(solution)/shard_map/ppermute | solution.py:539
  6.5 0.9 %project.1 = (bf16[32,1024]{1,0:T(8,128)(2,1)S(1)}, bf16[32,1024]{1,0:T(8,128)(2,1)S(1)}, f32[32,1024]{1,0:T(8,128)S(1)}, f32[32,1024]{1,0:T(8,128)S(1)}, bf16[3...) custom-call(bf16[32,3200]{1,0:T(8,128)(2,1)S(1)} %get-tuple-element.41.packed_ref, ...), custom_call_target="tpu_custom_call" | custom-call | tf_op jit(solution)/shard_map/project/pallas_call | solution.py:239
  7.4 2.9 %collective-permute-start.1 = (bf16[32,1024]{1,0:T(8,128)(2,1)S(1)}, bf16[32,1024]{1,0:T(8,128)(2,1)S(1)}, u32[]{:S(2)}, u32[]{:S(2)}) collective-permute-start(bf16[32,1024]{1,0:T(8,128)(2,1)S(1)} %get-tuple-element.45), channel_id=1, source_target_pairs={{0,2},{2,0},{1,3},{3,1},{4,6},{6,4},{5,7},{7,5},{8,10},{10,8},{9,1... | collective-permute-start | bytes 196616 | tf_op jit(solution)/shard_map/ppermute | solution.py:539
  10.3 2.2 %load_weights.3.refs_3_.refs_6_ = bf16[2,2048,512]{2,1,0:T(8,128)(2,1)S(1)} custom-call(bf16[2,2048,512]{2,1,0:T(8,128)(2,1)} %refs_0_), custom_call_target="tpu_custom_call" | custom-call | tf_op jit(solution)/shard_map/load_weights/pallas_call | solution.py:268
  12.6 0.1 collective-permute-start.2
  12.6 0.1 collective-permute-done.1
  12.8 4.1 %collective-permute-start.5 = (bf16[32,1152]{1,0:T(8,128)(2,1)S(1)}, bf16[32,1152]{1,0:T(8,128)(2,1)S(1)}, u32[]{:S(2)}, u32[]{:S(2)}) collective-permute-start(bf16[32,1152]{1,0:T(8,128)(2,1)S(1)} %get-tuple-element.77), channel_id=1, source_target_pairs={{0,12},{4,8},{8,4},{12,0},{1,13},{5,9},{9,5},{13,1},{2,14},{6,10},... | collective-permute-start | bytes 221192 | tf_op jit(solution)/shard_map/ppermute | solution.py:539
  16.9 0.0 collective-permute-start.4
  16.9 0.0 collective-permute-done.2
  16.9 1.6 %collective-permute-start.3 = (bf16[64,1152]{1,0:T(8,128)(2,1)S(1)}, bf16[64,1152]{1,0:T(8,128)(2,1)S(1)}, u32[]{:S(2)}, u32[]{:S(2)}) collective-permute-start(bf16[64,1152]{1,0:T(8,128)(2,1)S(1)} %maximum_maximum_fusion), channel_id=1, source_target_pairs={{0,4},{4,0},{8,12},{12,8},{1,5},{5,1},{9,13},{13,9},{2,6},{6,2},{1... | collective-permute-start | bytes 442376 | tf_op jit(solution)/shard_map/ppermute | solution.py:539
  18.6 2.2 %load_weights.4.refs_4_.refs_7_ = bf16[2,2048,512]{2,1,0:T(8,128)(2,1)S(1)} custom-call(bf16[2,2048,512]{2,1,0:T(8,128)(2,1)} %refs_0_.1), custom_call_target="tpu_custom_call" | custom-call | tf_op jit(solution)/shard_map/load_weights/pallas_call | solution.py:268
  20.8 0.0 collective-permute-done.5
  20.8 1.0 %collective-permute-start.7 = (bf16[32,1152]{1,0:T(8,128)(2,1)S(1)}, bf16[32,1152]{1,0:T(8,128)(2,1)S(1)}, u32[]{:S(2)}, u32[]{:S(2)}) collective-permute-start(bf16[32,1152]{1,0:T(8,128)(2,1)S(1)} %collective-permute-done.5), channel_id=1, source_target_pairs={{0,2},{2,0},{1,3},{3,1},{4,6},{6,4},{5,7},{7,5},{8,10},{10,8},{9,1... | collective-permute-start | bytes 221192 | tf_op jit(solution)/shard_map/ppermute | solution.py:539
  21.8 1.1 %collective-permute-done.4 = bf16[32,1152]{1,0:T(8,128)(2,1)S(1)} collective-permute-done((bf16[32,1152]{1,0:T(8,128)(2,1)S(1)}, bf16[32,1152]{1,0:T(8,128)(2,1)S(1)}, u32[]{:S(2)}, u32[]{:S(2)}) %collective-permute-start.4) | collective-permute-done | bytes 73760 | tf_op jit(solution)/shard_map/ppermute | solution.py:539
  22.9 1.5 %collective-permute-start.6 = (bf16[32,1152]{1,0:T(8,128)(2,1)S(1)}, bf16[32,1152]{1,0:T(8,128)(2,1)S(1)}, u32[]{:S(2)}, u32[]{:S(2)}) collective-permute-start(bf16[32,1152]{1,0:T(8,128)(2,1)S(1)} %collective-permute-done.4), channel_id=1, source_target_pairs={{0,2},{2,0},{1,3},{3,1},{4,6},{6,4},{5,7},{7,5},{8,10},{10,8},{9,1... | collective-permute-start | bytes 221192 | tf_op jit(solution)/shard_map/ppermute | solution.py:539
  24.4 0.0 copy-start
  24.4 2.2 %load_weights.5.refs_8_ = bf16[2,512,2048]{2,1,0:T(8,128)(2,1)S(1)} custom-call(bf16[2,512,2048]{2,1,0:T(8,128)(2,1)} %refs_0_.2), custom_call_target="tpu_custom_call" | custom-call | tf_op jit(solution)/shard_map/load_weights/pallas_call | solution.py:268
  26.7 0.0 collective-permute-done.3
  26.7 0.0 collective-permute-done.7
  26.7 0.6 %collective-permute-done.6 = bf16[32,1152]{1,0:T(8,128)(2,1)S(1)} collective-permute-done((bf16[32,1152]{1,0:T(8,128)(2,1)S(1)}, bf16[32,1152]{1,0:T(8,128)(2,1)S(1)}, u32[]{:S(2)}, u32[]{:S(2)}) %collective-permute-start.6) | collective-permute-done | bytes 73760 | tf_op jit(solution)/shard_map/ppermute | solution.py:539
  27.3 0.1 collective-permute-start.8
  27.5 0.5 %collective-permute-start.9 = (bf16[64,1152]{1,0:T(8,128)(2,1)S(1)}, bf16[64,1152]{1,0:T(8,128)(2,1)S(1)}, u32[]{:S(2)}, u32[]{:S(2)}) collective-permute-start(bf16[64,1152]{1,0:T(8,128)(2,1)S(1)} %constant_dynamic-update-slice_fusion.4.refs_1_), channel_id=1, source_target_pairs={{0,1},{1,0},{2,3},{3,2},{4,5},{5,4},{6,7},{7,6},{8,9},{9,8},{10,11... | collective-permute-start | bytes 442376 | tf_op jit(solution)/shard_map/ppermute | solution.py:539
  28.0 0.0 copy-done
  28.0 1.3 %start_experts.1.refs_4_ = f32[256,2048]{1,0:T(8,128)S(1)} custom-call(bf16[192,1152]{1,0:T(8,128)(2,1)S(1)} %constant_dynamic-update-slice_fusion.refs_0_, bf16[64,1152]{1,0:T(8,128)(2,1)S(1)} %constant_dynamic-update-slice_fusion.4.refs_1_, f32[1,2048]{1,0:T(1,128)S(1)} %bitcast.3, bf16[2,2048,512]{2,1,0:T(8,128)(2,1)S(1)} %load_weights.3.refs_3_.refs_6_, ...), custom_call_target="tpu_custom_call" | custom-call | tf_op jit(solution)/shard_map/start_experts/pallas_call | solution.py:448
  29.3 0.1 collective-permute-done.9.refs_3_
  29.4 0.0 collective-permute-done.8.refs_2_
  29.4 1.5 %finish_experts.2 = (f32[64,2048]{1,0:T(8,128)S(1)}, bf16[64,2048]{1,0:T(8,128)(2,1)S(1)}) custom-call(bf16[192,1152]{1,0:T(8,128)(2,1)S(1)} %constant_dynamic-update-slice_fusion.refs_0_, bf16[64,1152]{1,0:T(8,128)(2,1)S(1)} %constant_dynamic-update-slice_fusion.4.refs_1_, bf16[192,1152]{1,0:T(8,128)(2,1)S(1)} %collective-permute-done.8.refs_2_, ...), custom_call_target="tpu_custom_call" | custom-call | tf_op jit(solution)/shard_map/finish_experts/pallas_call | solution.py:472
  30.9 0.2 collective-permute-start.10
  31.1 1.5 %finish_experts.3 = (f32[64,2048]{1,0:T(8,128)S(1)}, bf16[64,2048]{1,0:T(8,128)(2,1)S(1)}, bf16[32,1024]{1,0:T(8,128)(2,1)S(1)}) custom-call(bf16[192,1152]{1,0:T(8,128)(2,1)S(1)} %constant_dynamic-update-slice_fusion.refs_0_, bf16[64,1152]{1,0:T(8,128)(2,1)S(1)} %constant_dynamic-update-slice_fusion.4.refs_1_, ...), custom_call_target="tpu_custom_call" | custom-call | tf_op jit(solution)/shard_map/finish_experts/pallas_call | solution.py:472
  32.5 0.4 collective-permute-start.15
  33.0 0.0 collective-permute-done.10.back
  33.0 1.6 %collective-permute-start.11 = (bf16[32,1024]{1,0:T(8,128)(2,1)S(1)}, bf16[32,1024]{1,0:T(8,128)(2,1)S(1)}, u32[]{:S(2)}, u32[]{:S(2)}) collective-permute-start(bf16[32,1024]{1,0:T(8,128)(2,1)S(1)} %get-tuple-element.68), channel_id=1, source_target_pairs={{0,2},{2,0},{1,3},{3,1},{4,6},{6,4},{5,7},{7,5},{8,10},{10,8},{9,1... | collective-permute-start | bytes 196616 | tf_op jit(solution)/shard_map/ppermute | solution.py:539
  34.6 0.5 %collective-permute-start.13 = (bf16[32,1024]{1,0:T(8,128)(2,1)S(1)}, bf16[32,1024]{1,0:T(8,128)(2,1)S(1)}, u32[]{:S(2)}, u32[]{:S(2)}) collective-permute-start(bf16[32,1024]{1,0:T(8,128)(2,1)S(1)} %get-tuple-element.70), channel_id=1, source_target_pairs={{0,2},{2,0},{1,3},{3,1},{4,6},{6,4},{5,7},{7,5},{8,10},{10,8},{9,1... | collective-permute-start | bytes 196616 | tf_op jit(solution)/shard_map/ppermute | solution.py:539
  35.1 0.0 collective-permute-done.15.back
  35.2 0.5 %collective-permute-start.16 = (bf16[32,2048]{1,0:T(8,128)(2,1)S(1)}, bf16[32,2048]{1,0:T(8,128)(2,1)S(1)}, u32[]{:S(2)}, u32[]{:S(2)}) collective-permute-start(bf16[32,2048]{1,0:T(8,128)(2,1)S(1)} %get-tuple-element.74), channel_id=1, source_target_pairs={{0,4},{4,0},{8,12},{12,8},{1,5},{5,1},{9,13},{13,9},{2,6},{6,2},{1... | collective-permute-start | bytes 393224 | tf_op jit(solution)/shard_map/ppermute | solution.py:539
  35.7 2.1 %collective-permute-done.11 = bf16[32,1024]{1,0:T(8,128)(2,1)S(1)} collective-permute-done((bf16[32,1024]{1,0:T(8,128)(2,1)S(1)}, bf16[32,1024]{1,0:T(8,128)(2,1)S(1)}, u32[]{:S(2)}, u32[]{:S(2)}) %collective-permute-start.11) | collective-permute-done | bytes 65568 | tf_op jit(solution)/shard_map/ppermute | solution.py:539
  37.8 1.8 %collective-permute-start.12 = (bf16[32,1024]{1,0:T(8,128)(2,1)S(1)}, bf16[32,1024]{1,0:T(8,128)(2,1)S(1)}, u32[]{:S(2)}, u32[]{:S(2)}) collective-permute-start(bf16[32,1024]{1,0:T(8,128)(2,1)S(1)} %add_convert_fusion.2), channel_id=1, source_target_pairs={{0,8},{4,12},{8,0},{12,4},{1,9},{5,13},{9,1},{13,5},{2,10},{6,14},... | collective-permute-start | bytes 196616 | tf_op jit(solution)/shard_map/ppermute | solution.py:539
  39.6 0.0 collective-permute-done.13
  39.6 2.0 %collective-permute-start.14 = (bf16[32,1024]{1,0:T(8,128)(2,1)S(1)}, bf16[32,1024]{1,0:T(8,128)(2,1)S(1)}, u32[]{:S(2)}, u32[]{:S(2)}) collective-permute-start(bf16[32,1024]{1,0:T(8,128)(2,1)S(1)} %add_convert_fusion.1), channel_id=1, source_target_pairs={{0,12},{4,8},{8,4},{12,0},{1,13},{5,9},{9,5},{13,1},{2,14},{6,10},... | collective-permute-start | bytes 196616 | tf_op jit(solution)/shard_map/ppermute | solution.py:539
  41.6 0.0 collective-permute-done.16.back
  41.6 1.3 %collective-permute-start.17 = (bf16[32,1024]{1,0:T(8,128)(2,1)S(1)}, bf16[32,1024]{1,0:T(8,128)(2,1)S(1)}, u32[]{:S(2)}, u32[]{:S(2)}) collective-permute-start(bf16[32,1024]{1,0:T(8,128)(2,1)S(1)} %get-tuple-element.76), channel_id=1, source_target_pairs={{0,2},{2,0},{1,3},{3,1},{4,6},{6,4},{5,7},{7,5},{8,10},{10,8},{9,1... | collective-permute-start | bytes 196616 | tf_op jit(solution)/shard_map/ppermute | solution.py:539
  43.0 1.5 %collective-permute-done.12 = bf16[32,1024]{1,0:T(8,128)(2,1)S(1)} collective-permute-done((bf16[32,1024]{1,0:T(8,128)(2,1)S(1)}, bf16[32,1024]{1,0:T(8,128)(2,1)S(1)}, u32[]{:S(2)}, u32[]{:S(2)}) %collective-permute-start.12) | collective-permute-done | bytes 65568 | tf_op jit(solution)/shard_map/ppermute | solution.py:539
  44.4 1.4 %collective-permute-done.14 = bf16[32,1024]{1,0:T(8,128)(2,1)S(1)} collective-permute-done((bf16[32,1024]{1,0:T(8,128)(2,1)S(1)}, bf16[32,1024]{1,0:T(8,128)(2,1)S(1)}, u32[]{:S(2)}, u32[]{:S(2)}) %collective-permute-start.14) | collective-permute-done | bytes 65568 | tf_op jit(solution)/shard_map/ppermute | solution.py:539
  45.9 0.1 collective-permute-done.17
  46.0 0.6 %add_convert_fusion = bf16[32,1024]{1,0:T(8,128)(2,1)} fusion(bf16[32,1024]{1,0:T(8,128)(2,1)S(1)} %collective-permute-done.17, f32[32,1024]{1,0:T(8,128)S(1)} %convert_add_fusion, f32[32,1024]{1,0:T(8,128)S(1)} %get-tuple-element.75), kind=kLoop, calls=%fused_computation.1 | loop fusion | flops 131072 | bytes 393216 | tf_op jit(solution)/shard_map/convert_element_type | solution.py:627
  (16 shorter events, 0.3 us)
Async XLA Ops:
  4.9 1.6 %collective-permute-start = (bf16[32,3200]{1,0:T(8,128)(2,1)S(1)}, bf16[32,3200]{1,0:T(8,128)(2,1)S(1)}, u32[]{:S(2)}, u32[]{:S(2)}) collective-permute-start(bf16[32,3200]{1,0:T(8,128)(2,1)S(1)} %get-tuple-element.41.packed_ref), channel_id=1, source_target_pairs={{0,1},{1,0},{2,3},{3,2},{4,5},{5,4},{6,7},{7,6},{8,9},{9,8},{10,11... | collective-permute-start | bytes 614408 | tf_op jit(solution)/shard_map/ppermute | solution.py:539
  7.4 5.3 %collective-permute-start.1 = (bf16[32,1024]{1,0:T(8,128)(2,1)S(1)}, bf16[32,1024]{1,0:T(8,128)(2,1)S(1)}, u32[]{:S(2)}, u32[]{:S(2)}) collective-permute-start(bf16[32,1024]{1,0:T(8,128)(2,1)S(1)} %get-tuple-element.45), channel_id=1, source_target_pairs={{0,2},{2,0},{1,3},{3,1},{4,6},{6,4},{5,7},{7,5},{8,10},{10,8},{9,1... | collective-permute-start | bytes 196616 | tf_op jit(solution)/shard_map/ppermute | solution.py:539
  12.6 4.3 %collective-permute-start.2 = (bf16[32,1024]{1,0:T(8,128)(2,1)S(1)}, bf16[32,1024]{1,0:T(8,128)(2,1)S(1)}, u32[]{:S(2)}, u32[]{:S(2)}) collective-permute-start(bf16[32,1024]{1,0:T(8,128)(2,1)S(1)} %get-tuple-element.50), channel_id=1, source_target_pairs={{0,2},{2,0},{1,3},{3,1},{4,6},{6,4},{5,7},{7,5},{8,10},{10,8},{9,1... | collective-permute-start | bytes 196616 | tf_op jit(solution)/shard_map/ppermute | solution.py:539
  12.8 8.0 %collective-permute-start.5 = (bf16[32,1152]{1,0:T(8,128)(2,1)S(1)}, bf16[32,1152]{1,0:T(8,128)(2,1)S(1)}, u32[]{:S(2)}, u32[]{:S(2)}) collective-permute-start(bf16[32,1152]{1,0:T(8,128)(2,1)S(1)} %get-tuple-element.77), channel_id=1, source_target_pairs={{0,12},{4,8},{8,4},{12,0},{1,13},{5,9},{9,5},{13,1},{2,14},{6,10},... | collective-permute-start | bytes 221192 | tf_op jit(solution)/shard_map/ppermute | solution.py:539
  16.9 6.1 %collective-permute-start.4 = (bf16[32,1152]{1,0:T(8,128)(2,1)S(1)}, bf16[32,1152]{1,0:T(8,128)(2,1)S(1)}, u32[]{:S(2)}, u32[]{:S(2)}) collective-permute-start(bf16[32,1152]{1,0:T(8,128)(2,1)S(1)} %get-tuple-element.77), channel_id=1, source_target_pairs={{0,8},{4,12},{8,0},{12,4},{1,9},{5,13},{9,1},{13,5},{2,10},{6,14},... | collective-permute-start | bytes 221192 | tf_op jit(solution)/shard_map/ppermute | solution.py:539
  16.9 9.7 %collective-permute-start.3 = (bf16[64,1152]{1,0:T(8,128)(2,1)S(1)}, bf16[64,1152]{1,0:T(8,128)(2,1)S(1)}, u32[]{:S(2)}, u32[]{:S(2)}) collective-permute-start(bf16[64,1152]{1,0:T(8,128)(2,1)S(1)} %maximum_maximum_fusion), channel_id=1, source_target_pairs={{0,4},{4,0},{8,12},{12,8},{1,5},{5,1},{9,13},{13,9},{2,6},{6,2},{1... | collective-permute-start | bytes 442376 | tf_op jit(solution)/shard_map/ppermute | solution.py:539
  20.8 5.9 %collective-permute-start.7 = (bf16[32,1152]{1,0:T(8,128)(2,1)S(1)}, bf16[32,1152]{1,0:T(8,128)(2,1)S(1)}, u32[]{:S(2)}, u32[]{:S(2)}) collective-permute-start(bf16[32,1152]{1,0:T(8,128)(2,1)S(1)} %collective-permute-done.5), channel_id=1, source_target_pairs={{0,2},{2,0},{1,3},{3,1},{4,6},{6,4},{5,7},{7,5},{8,10},{10,8},{9,1... | collective-permute-start | bytes 221192 | tf_op jit(solution)/shard_map/ppermute | solution.py:539
  22.9 4.4 %collective-permute-start.6 = (bf16[32,1152]{1,0:T(8,128)(2,1)S(1)}, bf16[32,1152]{1,0:T(8,128)(2,1)S(1)}, u32[]{:S(2)}, u32[]{:S(2)}) collective-permute-start(bf16[32,1152]{1,0:T(8,128)(2,1)S(1)} %collective-permute-done.4), channel_id=1, source_target_pairs={{0,2},{2,0},{1,3},{3,1},{4,6},{6,4},{5,7},{7,5},{8,10},{10,8},{9,1... | collective-permute-start | bytes 221192 | tf_op jit(solution)/shard_map/ppermute | solution.py:539
  24.4 3.6 %copy-start = (f32[2048]{0:T(1024)S(1)}, f32[2048]{0:T(1024)}, u32[]{:S(2)}) copy-start(f32[2048]{0:T(1024)} %param.22) | copy-start | bytes 24580
  27.3 2.1 %collective-permute-start.8 = (bf16[192,1152]{1,0:T(8,128)(2,1)S(1)}, bf16[192,1152]{1,0:T(8,128)(2,1)S(1)}, u32[]{:S(2)}, u32[]{:S(2)}) collective-permute-start(bf16[192,1152]{1,0:T(8,128)(2,1)S(1)} %constant_dynamic-update-slice_fusion.refs_0_), channel_id=1, source_target_pairs={{0,1},{1,0},{2,3},{3,2},{4,5},{5,4},{6,7},{7,6},{8,9},{9,8},{10,11... | collective-permute-start | bytes 1327112 | tf_op jit(solution)/shard_map/ppermute | solution.py:539
  27.5 2.0 %collective-permute-start.9 = (bf16[64,1152]{1,0:T(8,128)(2,1)S(1)}, bf16[64,1152]{1,0:T(8,128)(2,1)S(1)}, u32[]{:S(2)}, u32[]{:S(2)}) collective-permute-start(bf16[64,1152]{1,0:T(8,128)(2,1)S(1)} %constant_dynamic-update-slice_fusion.4.refs_1_), channel_id=1, source_target_pairs={{0,1},{1,0},{2,3},{3,2},{4,5},{5,4},{6,7},{7,6},{8,9},{9,8},{10,11... | collective-permute-start | bytes 442376 | tf_op jit(solution)/shard_map/ppermute | solution.py:539
  30.9 2.1 %collective-permute-start.10 = (bf16[64,2048]{1,0:T(8,128)(2,1)S(1)}, bf16[64,2048]{1,0:T(8,128)(2,1)S(1)}, u32[]{:S(2)}, u32[]{:S(2)}) collective-permute-start(bf16[64,2048]{1,0:T(8,128)(2,1)S(1)} %get-tuple-element.66), channel_id=1, source_target_pairs={{0,1},{1,0},{2,3},{3,2},{4,5},{5,4},{6,7},{7,6},{8,9},{9,8},{10,11... | collective-permute-start | bytes 786440 | tf_op jit(solution)/shard_map/ppermute | solution.py:539
  32.5 2.6 %collective-permute-start.15 = (bf16[64,2048]{1,0:T(8,128)(2,1)S(1)}, bf16[64,2048]{1,0:T(8,128)(2,1)S(1)}, u32[]{:S(2)}, u32[]{:S(2)}) collective-permute-start(bf16[64,2048]{1,0:T(8,128)(2,1)S(1)} %get-tuple-element.72), channel_id=1, source_target_pairs={{0,1},{1,0},{2,3},{3,2},{4,5},{5,4},{6,7},{7,6},{8,9},{9,8},{10,11... | collective-permute-start | bytes 786440 | tf_op jit(solution)/shard_map/ppermute | solution.py:539
  33.0 4.7 %collective-permute-start.11 = (bf16[32,1024]{1,0:T(8,128)(2,1)S(1)}, bf16[32,1024]{1,0:T(8,128)(2,1)S(1)}, u32[]{:S(2)}, u32[]{:S(2)}) collective-permute-start(bf16[32,1024]{1,0:T(8,128)(2,1)S(1)} %get-tuple-element.68), channel_id=1, source_target_pairs={{0,2},{2,0},{1,3},{3,1},{4,6},{6,4},{5,7},{7,5},{8,10},{10,8},{9,1... | collective-permute-start | bytes 196616 | tf_op jit(solution)/shard_map/ppermute | solution.py:539
  34.6 5.0 %collective-permute-start.13 = (bf16[32,1024]{1,0:T(8,128)(2,1)S(1)}, bf16[32,1024]{1,0:T(8,128)(2,1)S(1)}, u32[]{:S(2)}, u32[]{:S(2)}) collective-permute-start(bf16[32,1024]{1,0:T(8,128)(2,1)S(1)} %get-tuple-element.70), channel_id=1, source_target_pairs={{0,2},{2,0},{1,3},{3,1},{4,6},{6,4},{5,7},{7,5},{8,10},{10,8},{9,1... | collective-permute-start | bytes 196616 | tf_op jit(solution)/shard_map/ppermute | solution.py:539
  35.2 6.4 %collective-permute-start.16 = (bf16[32,2048]{1,0:T(8,128)(2,1)S(1)}, bf16[32,2048]{1,0:T(8,128)(2,1)S(1)}, u32[]{:S(2)}, u32[]{:S(2)}) collective-permute-start(bf16[32,2048]{1,0:T(8,128)(2,1)S(1)} %get-tuple-element.74), channel_id=1, source_target_pairs={{0,4},{4,0},{8,12},{12,8},{1,5},{5,1},{9,13},{13,9},{2,6},{6,2},{1... | collective-permute-start | bytes 393224 | tf_op jit(solution)/shard_map/ppermute | solution.py:539
  37.8 6.6 %collective-permute-start.12 = (bf16[32,1024]{1,0:T(8,128)(2,1)S(1)}, bf16[32,1024]{1,0:T(8,128)(2,1)S(1)}, u32[]{:S(2)}, u32[]{:S(2)}) collective-permute-start(bf16[32,1024]{1,0:T(8,128)(2,1)S(1)} %add_convert_fusion.2), channel_id=1, source_target_pairs={{0,8},{4,12},{8,0},{12,4},{1,9},{5,13},{9,1},{13,5},{2,10},{6,14},... | collective-permute-start | bytes 196616 | tf_op jit(solution)/shard_map/ppermute | solution.py:539
  39.6 6.2 %collective-permute-start.14 = (bf16[32,1024]{1,0:T(8,128)(2,1)S(1)}, bf16[32,1024]{1,0:T(8,128)(2,1)S(1)}, u32[]{:S(2)}, u32[]{:S(2)}) collective-permute-start(bf16[32,1024]{1,0:T(8,128)(2,1)S(1)} %add_convert_fusion.1), channel_id=1, source_target_pairs={{0,12},{4,8},{8,4},{12,0},{1,13},{5,9},{9,5},{13,1},{2,14},{6,10},... | collective-permute-start | bytes 196616 | tf_op jit(solution)/shard_map/ppermute | solution.py:539
  41.6 4.3 %collective-permute-start.17 = (bf16[32,1024]{1,0:T(8,128)(2,1)S(1)}, bf16[32,1024]{1,0:T(8,128)(2,1)S(1)}, u32[]{:S(2)}, u32[]{:S(2)}) collective-permute-start(bf16[32,1024]{1,0:T(8,128)(2,1)S(1)} %get-tuple-element.76), channel_id=1, source_target_pairs={{0,2},{2,0},{1,3},{3,1},{4,6},{6,4},{5,7},{7,5},{8,10},{10,8},{9,1... | collective-permute-start | bytes 196616 | tf_op jit(solution)/shard_map/ppermute | solution.py:539
